TPU v7x, 32 devices: a whole 2x2x4 slice. The times are simulated.
32 devices in a mesh: rep: 4 (over y, x), exp: 8 (over z, core).
Axes of the slice: x: 2, y: 2, z: 4, core: 2. Of those that a mesh axis runs over, the one named last changes fastest.
Arguments:
- tokens: bfloat16 [2048, 1024], P('exp', 'rep'), may hold values from -6 to 6
- routes: int32 [2048, 2], P('exp'), may hold values from 0 to 7, all different within a row; in each aligned block of 256 rows (0 to 255, 256 to 511, ...) at most 128 rows name the same one
- probs: float32 [2048, 2], P('exp'), may hold values from 0.2 to 1
- capacity: int32 [8], replicated, may hold values from 256 to 767
- plan: int32 [8], replicated, may hold values from 0 to 7, each once
- grad_out: bfloat16 [2048, 1024], P('exp', 'rep'), may hold values from -6 to 6
- w_gate: bfloat16 [8, 1024, 4096], P('exp', None, 'rep'), may hold values from -0.1875 to 0.1875
- w_up: bfloat16 [8, 1024, 4096], P('exp', None, 'rep'), may hold values from -0.1875 to 0.1875
- w_down: bfloat16 [8, 4096, 1024], P('exp', 'rep'), may hold values from -0.09375 to 0.09375
Outputs:
- mixed: bfloat16 [2048, 1024], P('exp', 'rep')
- grad_tokens: bfloat16 [2048, 1024], P('exp', 'rep')
- grad_probs: float32 [2048, 2], P('exp')
- grad_gate: float32 [8, 1024, 4096], P('exp', None, 'rep')
- grad_up: float32 [8, 1024, 4096], P('exp', None, 'rep')
- grad_down: float32 [8, 4096, 1024], P('exp', 'rep')
Inputs may be any that keep to these rules, and one draw needn't show every extreme that they name: `routes`: each row names two different experts; among the rows of one block of 256 tokens no expert is named more than 128 times, a bound that some block reaches. `plan`: a permutation of the experts; its first 4 entries are the hot experts.
All inputs are finite; a program needn't handle non-finite values.
Results may differ from a plain program's by a relative error of at most 0.01.
Values may be sent and summed in bfloat16 or wider, within the bound.
No kernel may reach another device: no remote copies, remote signals or barrier semaphores. Data moves between devices by JAX's collectives and lax.ppermute only.
A program may use at most 128 MiB of HBM per device.

v0:
```python
import jax
import jax.numpy as jnp
from jax import lax
from jax.sharding import PartitionSpec as P

HOT = 4


def carried_in(value, axis, combine, identity):
    peers, mine = (lax.axis_size(axis), lax.axis_index(axis))
    everything = lax.all_gather(value, axis)
    start = jnp.broadcast_to(jnp.asarray(identity, value.dtype), value.shape)

    def step(k, before):
        reached = k < mine
        new = combine(before, everything[k])
        return jnp.where(reached, new, before)

    return lax.fori_loop(0, peers, step, start)


def fill_rows(shard, flat, rank, token_of, scale, experts, per_slot):
    picked = shard[token_of]
    if scale is not None:
        picked = (picked.astype(jnp.float32) * scale[:, None]).astype(jnp.bfloat16)
    empty = jnp.zeros((experts, per_slot, shard.shape[1]), jnp.bfloat16)
    return empty.at[flat, rank].set(picked)


def dispatch(shard, flat, rank, token_of, scale, experts, per_slot):
    buffer = fill_rows(shard, flat, rank, token_of, scale, experts, per_slot)
    received = lax.all_to_all(buffer, "exp", split_axis=0, concat_axis=0, tiled=True)
    narrow = received.reshape(-1, received.shape[2])
    return lax.all_gather(narrow, "rep", axis=1, tiled=True)


def return_rows(rows, flat, rank, experts, per_slot):
    back = lax.all_to_all(
        rows.reshape(experts, per_slot, rows.shape[1]),
        "exp",
        split_axis=0,
        concat_axis=0,
        tiled=True,
    )
    return back[flat, rank].astype(jnp.float32)


def on_device(tokens, routes, probs, capacity, plan, grad_out, w_gate, w_up, w_down):
    tok_rows = tokens.shape[0]
    experts = capacity.shape[0]
    per_slot = 4 * tok_rows // experts
    feat_cols = tokens.shape[1]
    flat = routes.reshape(-1)
    expert_ids = jnp.arange(experts, dtype=jnp.int32)
    onehot = (flat[:, None] == expert_ids[None, :]).astype(jnp.int32)
    rank = jnp.sum((jnp.cumsum(onehot, axis=0) - onehot) * onehot, axis=1)
    counts = jnp.sum(onehot, axis=0)
    earlier = carried_in(
        counts, "exp", lambda first, second: first + second, jnp.zeros_like(counts)
    )
    position = rank + jnp.sum(onehot * earlier[None, :], axis=1)
    hot_flag = jnp.any(plan[:HOT][:, None] == expert_ids[None, :], axis=0).astype(jnp.int32)
    limit = capacity + 2 * tok_rows * hot_flag
    keep = (position < jnp.sum(onehot * limit[None, :], axis=1)).astype(jnp.float32)
    weight = probs.reshape(-1) * keep
    token_of = jnp.arange(2 * tok_rows, dtype=jnp.int32) // 2
    wg = w_gate[0]
    wu = w_up[0]
    wd = w_down[0]
    xs = dispatch(tokens, flat, rank, token_of, None, experts, per_slot)
    gate = jnp.dot(xs, wg, preferred_element_type=jnp.float32)
    up = jnp.dot(xs, wu, preferred_element_type=jnp.float32)
    sig = jax.nn.sigmoid(gate)
    silu = gate * sig
    hidden = (silu * up).astype(jnp.bfloat16)
    partial_value = jnp.dot(hidden, wd, preferred_element_type=jnp.float32)
    out_rows = lax.psum_scatter(
        partial_value.astype(jnp.bfloat16), "rep", scatter_dimension=1, tiled=True
    )
    picked = return_rows(out_rows, flat, rank, experts, per_slot)
    mixed = jnp.sum((weight[:, None] * picked).reshape(tok_rows, 2, feat_cols), axis=1).astype(
        jnp.bfloat16
    )
    dots = jnp.sum(grad_out[token_of].astype(jnp.float32) * picked, axis=1)
    dots = lax.psum(dots, "rep")
    grad_probs = (keep * dots).reshape(tok_rows, 2)
    dout = dispatch(grad_out, flat, rank, token_of, weight, experts, per_slot)
    dh = lax.dot_general(dout, wd, (((1,), (1,)), ((), ())), preferred_element_type=jnp.float32)
    dgate = (dh * up * sig * (1.0 + gate * (1.0 - sig))).astype(jnp.bfloat16)
    dup = (dh * silu).astype(jnp.bfloat16)
    grad_down = lax.dot_general(
        hidden, dout, (((0,), (0,)), ((), ())), preferred_element_type=jnp.float32
    )
    grad_gate = lax.dot_general(
        xs, dgate, (((0,), (0,)), ((), ())), preferred_element_type=jnp.float32
    )
    grad_up = lax.dot_general(xs, dup, (((0,), (0,)), ((), ())), preferred_element_type=jnp.float32)
    dpartial = lax.dot_general(
        dgate, wg, (((1,), (1,)), ((), ())), preferred_element_type=jnp.float32
    )
    dpartial = dpartial + lax.dot_general(
        dup, wu, (((1,), (1,)), ((), ())), preferred_element_type=jnp.float32
    )
    dx_rows = lax.psum_scatter(
        dpartial.astype(jnp.bfloat16), "rep", scatter_dimension=1, tiled=True
    )
    back = return_rows(dx_rows, flat, rank, experts, per_slot)
    grad_tokens = jnp.sum((weight[:, None] * back).reshape(tok_rows, 2, feat_cols), axis=1).astype(
        jnp.bfloat16
    )
    return (mixed, grad_tokens, grad_probs, grad_gate[None], grad_up[None], grad_down[None])


def solution(mesh):
    return jax.shard_map(
        on_device,
        mesh=mesh,
        in_specs=(
            P("exp", "rep"),
            P("exp", None),
            P("exp", None),
            P(),
            P(),
            P("exp", "rep"),
            P("exp", None, "rep"),
            P("exp", None, "rep"),
            P("exp", "rep", None),
        ),
        out_specs=(
            P("exp", "rep"),
            P("exp", "rep"),
            P("exp", None),
            P("exp", None, "rep"),
            P("exp", None, "rep"),
            P("exp", "rep", None),
        ),
        check_vma=False,
    )
```

profile of v0, /device:TPU:0, one launch (start us, length us, event | category | flops | bytes accessed | tf_op | source)
XLA Modules:
  0.0 347.6 jit_solution(13623334577716664741)
XLA Ops:
  7.3 1.0 copy.22
  8.8 1.2 dynamic-slice
  10.9 10.6 %all-reduce = s32[64]{0:T(128)S(1)} all-reduce(s32[64]{0:T(128)S(1)} %dynamic-update-slice), channel_id=2, replica_groups=mesh['rep'=4,'exp'=8] {'exp'}, use_global_device_ids=true, to_apply=%add | all-reduce | flops 64 | bytes 512
  22.7 1.1 reduce-window.6
  24.9 2.0 gather_fusion
  26.9 26.3 %scatter_fusion = bf16[8,128,256]{2,1,0:T(8,128)(2,1)S(1)} fusion(bf16[8,128,256]{2,1,0:T(8,128)(2,1)S(1)} %broadcast.150.clone, s32[512]{0:T(512)S(1)} %bitcast.61, bf16[512,256]{1,0:T(8,128)(2,1)S(1)} %gather_fusion), kind=kCustom, calls=%fused_computation.4 | custom fusion | bytes 790528 | tf_op jit(solution)/shard_map/scatter | solution.py:27
  53.2 18.4 %all_to_all.20 = bf16[8,128,256]{2,1,0:T(8,128)(2,1)} all-to-all(bf16[8,128,256]{2,1,0:T(8,128)(2,1)S(1)} %scatter_fusion), channel_id=1, replica_groups=mesh['rep'=4,'exp'=8] {'exp'}, dimensions={0} | all-to-all | bytes 1048576 | tf_op jit(solution)/shard_map/all_to_all | solution.py:32
  71.7 34.2 %all-gather.4.cloned.1.call-done = bf16[1024,1024]{1,0:T(8,128)(2,1)} async-done(((bf16[1024,256]{1,0:T(8,128)(2,1)}), bf16[1024,1024]{1,0:T(8,128)(2,1)}) %all-gather.4.cloned.1.call-update) | async-done | bytes 2097168 | tf_op jit(solution)/shard_map/all_gather | solution.py:34
  105.9 4.7 %fusion.11 = f32[1024,1024]{1,0:T(8,128)S(1)} fusion(bf16[1024,1024]{1,0:T(8,128)(2,1)} %all-gather.4.cloned.1.call-done, bf16[1,1024,1024]{2,1,0:T(8,128)(2,1)} %param.17), kind=kOutput, calls=%fused_computation.27 | convolution fusion | flops 2147483648 | bytes 8388608 | tf_op jit(solution)/shard_map/dot_general | solution.py:71
  110.6 4.7 %multiply_convert_fusion.2 = (bf16[1024,1024]{1,0:T(8,128)(2,1)S(1)}, f32[1024,1024]{1,0:T(8,128)}) fusion(f32[1024,1024]{1,0:T(8,128)S(1)} %fusion.11, bf16[1024,1024]{1,0:T(8,128)(2,1)S(1)} %copy-done.9, bf16[1,1024,1024]{2,1,0:T(8,128)(2,1)S(1)} %copy-done.6), kind=kOutput, calls=%fused_computation.11 | convolution fusion | flops 2153775104 | bytes 14680064 | tf_op jit(solution)/shard_map/dot_general | solution.py:72
  115.3 1.3 copy-done.12
  116.6 3.7 %fusion.13 = bf16[1024,1024]{1,0:T(8,128)(2,1)} fusion(bf16[1024,1024]{1,0:T(8,128)(2,1)S(1)} %get-tuple-element.132, bf16[1,1024,1024]{2,1,0:T(8,128)(2,1)S(1)} %copy-done), kind=kOutput, calls=%fused_computation.29 | convolution fusion | flops 2148532224 | bytes 6291456 | tf_op jit(solution)/shard_map/dot_general | solution.py:76
  120.3 35.3 %reduce-scatter.3.cloned.1.call-done = bf16[1024,256]{1,0:T(8,128)(2,1)} async-done(((bf16[1024,1024]{1,0:T(8,128)(2,1)}), bf16[1024,256]{1,0:T(8,128)(2,1)}) %reduce-scatter.3.cloned.1.call-update) | async-done | bytes 524304 | tf_op jit(solution)/shard_map/reduce_scatter | solution.py:77
  155.7 4.6 %all-to-all-start.1 = ((bf16[8,128,256]{2,1,0:T(8,128)(2,1)}), bf16[8,128,256]{2,1,0:T(8,128)(2,1)S(1)}, u32[]{:S(2)}, u32[]{:S(2)}) async-start(bf16[8,128,256]{2,1,0:T(8,128)(2,1)} %bitcast.66), calls=%async_computation.2 | async-start | bytes 1048576 | tf_op jit(solution)/shard_map/all_to_all | solution.py:38
  160.4 2.0 gather_fusion.2
  162.6 13.0 %all-to-all-done.1 = bf16[8,128,256]{2,1,0:T(8,128)(2,1)S(1)} async-done(((bf16[8,128,256]{2,1,0:T(8,128)(2,1)}), bf16[8,128,256]{2,1,0:T(8,128)(2,1)S(1)}, u32[]{:S(2)}, u32[]{:S(2)}) %all-to-all-start.1) | async-done | bytes 524320 | tf_op jit(solution)/shard_map/all_to_all | solution.py:38
  175.7 3.2 gather_fusion.1
  179.0 8.9 %psum.7 = f32[512]{0:T(512)S(1)} all-reduce(f32[512]{0:T(512)S(1)} %fusion.19), channel_id=1, replica_groups=mesh['rep'=4,'exp'=8] {'rep'}, use_global_device_ids=true, to_apply=%region_16.17 | all-reduce | flops 512 | bytes 4096 | tf_op jit(solution)/shard_map/psum | solution.py:85
  188.1 26.3 %scatter_fusion.1 = bf16[8,128,256]{2,1,0:T(8,128)(2,1)S(1)} fusion(bf16[8,128,256]{2,1,0:T(8,128)(2,1)S(1)} %broadcast.150, s32[512]{0:T(512)S(1)} %bitcast.62, bf16[512,256]{1,0:T(8,128)(2,1)S(1)} %fusion.18), kind=kCustom, calls=%fused_computation.5 | custom fusion | bytes 790528 | tf_op jit(solution)/shard_map/scatter | solution.py:27
  214.4 18.6 %all_to_all.21 = bf16[8,128,256]{2,1,0:T(8,128)(2,1)} all-to-all(bf16[8,128,256]{2,1,0:T(8,128)(2,1)S(1)} %scatter_fusion.1), channel_id=1, replica_groups=mesh['rep'=4,'exp'=8] {'exp'}, dimensions={0} | all-to-all | bytes 1048576 | tf_op jit(solution)/shard_map/all_to_all | solution.py:32
  233.1 33.1 %all-gather.6.cloned.1.call-done = bf16[1024,1024]{1,0:T(8,128)(2,1)} async-done(((bf16[1024,256]{1,0:T(8,128)(2,1)}), bf16[1024,1024]{1,0:T(8,128)(2,1)}) %all-gather.6.cloned.1.call-update) | async-done | bytes 2097168 | tf_op jit(solution)/shard_map/all_gather | solution.py:34
  266.3 7.1 %multiply_convert_fusion.1 = (bf16[1024,1024]{1,0:T(8,128)(2,1)S(1)}, bf16[1024,1024]{1,0:T(8,128)(2,1)S(1)}) fusion(f32[1024,1024]{1,0:T(8,128)} %copy-done.11, f32[1024,1024]{1,0:T(8,128)} %get-tuple-element.133, bf16[1024,1024]{1,0:T(8,128)(2,1)} %all-gather.6.cloned.1.call-done, bf16[1,1024,1024]{2,1,0:T(8,128)(2,1)S(1)} %copy-done), kind=kOutput, calls=%fused_computation.10 | convolution fusion | flops 2161115136 | bytes 16777216 | tf_op jit(solution)/shard_map/dot_general | solution.py:88
  273.4 2.4 fusion.5
  276.5 3.7 %add_convert_fusion = bf16[1024,1024]{1,0:T(8,128)(2,1)} fusion(f32[1024,1024]{1,0:T(8,128)S(1)} %fusion.5, bf16[1024,1024]{1,0:T(8,128)(2,1)S(1)} %get-tuple-element.130, bf16[1,1024,1024]{2,1,0:T(8,128)(2,1)S(1)} %copy-done.8), kind=kOutput, calls=%fused_computation.8 | convolution fusion | flops 2149580800 | bytes 10485760 | tf_op jit(solution)/shard_map/dot_general | solution.py:98
  281.5 6.6 %convolution_bitcast_fusion.2 = f32[1,1024,1024]{2,1,0:T(8,128)} fusion(bf16[1024,1024]{1,0:T(8,128)(2,1)} %all-gather.4.cloned.1.call-done, bf16[1024,1024]{1,0:T(8,128)(2,1)} %copy-done.15), kind=kOutput, calls=%fused_computation.16 | convolution fusion | flops 2147483648 | bytes 8388608 | tf_op jit(solution)/shard_map/dot_general | solution.py:94
  288.1 27.5 %reduce-scatter.5.cloned.1.call-done = bf16[1024,256]{1,0:T(8,128)(2,1)} async-done(((bf16[1024,1024]{1,0:T(8,128)(2,1)}), bf16[1024,256]{1,0:T(8,128)(2,1)}) %reduce-scatter.5.cloned.1.call-update) | async-done | bytes 524304 | tf_op jit(solution)/shard_map/reduce_scatter | solution.py:104
  315.6 4.6 %all-to-all-start.3 = ((bf16[8,128,256]{2,1,0:T(8,128)(2,1)}), bf16[8,128,256]{2,1,0:T(8,128)(2,1)S(1)}, u32[]{:S(2)}, u32[]{:S(2)}) async-start(bf16[8,128,256]{2,1,0:T(8,128)(2,1)} %bitcast.65), calls=%async_computation.5 | async-start | bytes 1048576 | tf_op jit(solution)/shard_map/all_to_all | solution.py:38
  320.2 6.8 %convolution_bitcast_fusion.1 = f32[1,1024,1024]{2,1,0:T(8,128)} fusion(bf16[1024,1024]{1,0:T(8,128)(2,1)} %all-gather.4.cloned.1.call-done, bf16[1024,1024]{1,0:T(8,128)(2,1)} %copy-done.14), kind=kOutput, calls=%fused_computation.15 | convolution fusion | flops 2147483648 | bytes 8388608 | tf_op jit(solution)/shard_map/dot_general | solution.py:97
  327.0 4.4 %convolution_bitcast_fusion = f32[1,1024,1024]{2,1,0:T(8,128)} fusion(bf16[1024,1024]{1,0:T(8,128)(2,1)S(1)} %copy-done.13, bf16[1024,1024]{1,0:T(8,128)(2,1)S(1)} %copy-done.10), kind=kOutput, calls=%fused_computation.14 | convolution fusion | flops 2147483648 | bytes 8388608 | tf_op jit(solution)/shard_map/dot_general | solution.py:91
  331.4 4.2 %all-to-all-done.3 = bf16[8,128,256]{2,1,0:T(8,128)(2,1)S(1)} async-done(((bf16[8,128,256]{2,1,0:T(8,128)(2,1)}), bf16[8,128,256]{2,1,0:T(8,128)(2,1)S(1)}, u32[]{:S(2)}, u32[]{:S(2)}) %all-to-all-start.3) | async-done | bytes 524320 | tf_op jit(solution)/shard_map/all_to_all | solution.py:38
  335.5 3.2 gather_fusion.3
  339.0 2.1 multiply_reduce_fusion
  (80 shorter events, 6.2 us)
Async XLA Ops:
  7.2 109.5 %copy-start = (bf16[1,1024,1024]{2,1,0:T(8,128)(2,1)S(1)}, bf16[1,1024,1024]{2,1,0:T(8,128)(2,1)}, u32[]{:S(2)}) copy-start(bf16[1,1024,1024]{2,1,0:T(8,128)(2,1)} %param.19) | copy-start | bytes 6291460
  7.2 17.7 %copy-start.1 = (bf16[256,256]{1,0:T(8,128)(2,1)S(1)}, bf16[256,256]{1,0:T(8,128)(2,1)}, u32[]{:S(2)}) copy-start(bf16[256,256]{1,0:T(8,128)(2,1)} %param.11) | copy-start | bytes 393220
  7.2 98.7 %all-gather.4.cloned.1.call-start = ((), (), s32[]{:S(2)}) async-start(), calls=%async_computation.6 | async-start | bytes 2621440 | tf_op jit(solution)/shard_map/all_gather | solution.py:34
  71.7 84.0 %reduce-scatter.3.cloned.1.call-start = ((), (), s32[]{:S(2)}) async-start(), calls=%async_computation.7 | async-start | bytes 2621440 | tf_op jit(solution)/shard_map/reduce_scatter | solution.py:77
  105.9 4.7 %copy-start.6 = (bf16[1,1024,1024]{2,1,0:T(8,128)(2,1)S(1)}, bf16[1,1024,1024]{2,1,0:T(8,128)(2,1)}, u32[]{:S(2)}) copy-start(bf16[1,1024,1024]{2,1,0:T(8,128)(2,1)} %param.18) | copy-start | bytes 6291460
  105.9 4.7 %copy-start.9 = (bf16[1024,1024]{1,0:T(8,128)(2,1)S(1)}, bf16[1024,1024]{1,0:T(8,128)(2,1)}, u32[]{:S(2)}) copy-start(bf16[1024,1024]{1,0:T(8,128)(2,1)} %all-gather.4.cloned.1.call-done) | copy-start | bytes 6291460
  110.6 4.7 %copy-start.11 = (f32[1024,1024]{1,0:T(8,128)}, f32[1024,1024]{1,0:T(8,128)S(1)}, u32[]{:S(2)}) copy-start(f32[1024,1024]{1,0:T(8,128)S(1)} %fusion.11) | copy-start | bytes 12582916
  115.3 1.4 copy-start.12
  120.3 40.0 %copy-start.2 = (bf16[256,256]{1,0:T(8,128)(2,1)S(1)}, bf16[256,256]{1,0:T(8,128)(2,1)}, u32[]{:S(2)}) copy-start(bf16[256,256]{1,0:T(8,128)(2,1)} %param.16) | copy-start | bytes 393220
  120.3 42.0 %copy-start.5 = (f32[256,2]{0,1:T(2,128)S(1)}, f32[256,2]{0,1:T(2,128)}, u32[]{:S(2)}) copy-start(f32[256,2]{0,1:T(2,128)} %param.13) | copy-start | bytes 6148
  155.7 20.0 %all-to-all-start.1 = ((bf16[8,128,256]{2,1,0:T(8,128)(2,1)}), bf16[8,128,256]{2,1,0:T(8,128)(2,1)S(1)}, u32[]{:S(2)}, u32[]{:S(2)}) async-start(bf16[8,128,256]{2,1,0:T(8,128)(2,1)} %bitcast.66), calls=%async_computation.2 | async-start | bytes 1048576 | tf_op jit(solution)/shard_map/all_to_all | solution.py:38
  160.3 106.0 %all-gather.6.cloned.1.call-start = ((), (), s32[]{:S(2)}) async-start(), calls=%async_computation.8 | async-start | bytes 2621440 | tf_op jit(solution)/shard_map/all_gather | solution.py:34
  162.5 25.5 %copy-start.3 = (f32[256,2]{1,0:T(8,128)}, f32[256,2]{1,0:T(8,128)S(1)}, u32[]{:S(2)}) copy-start(f32[256,2]{1,0:T(8,128)S(1)} %copy.24) | copy-start | bytes 6148
  233.1 82.5 %reduce-scatter.5.cloned.1.call-start = ((), (), s32[]{:S(2)}) async-start(), calls=%async_computation.9 | async-start | bytes 2621440 | tf_op jit(solution)/shard_map/reduce_scatter | solution.py:104
  266.3 7.1 %copy-start.7 = (bf16[1,1024,1024]{2,1,0:T(8,128)(2,1)S(1)}, bf16[1,1024,1024]{2,1,0:T(8,128)(2,1)}, u32[]{:S(2)}) copy-start(bf16[1,1024,1024]{2,1,0:T(8,128)(2,1)} %param.18) | copy-start | bytes 6291460
  273.3 2.4 copy-start.14
  273.3 2.4 copy-start.15
  273.4 3.1 copy-start.8
  280.2 1.3 copy-start.4
  315.6 20.0 %all-to-all-start.3 = ((bf16[8,128,256]{2,1,0:T(8,128)(2,1)}), bf16[8,128,256]{2,1,0:T(8,128)(2,1)S(1)}, u32[]{:S(2)}, u32[]{:S(2)}) async-start(bf16[8,128,256]{2,1,0:T(8,128)(2,1)} %bitcast.65), calls=%async_computation.5 | async-start | bytes 1048576 | tf_op jit(solution)/shard_map/all_to_all | solution.py:38
  320.2 6.8 %copy-start.10 = (bf16[1024,1024]{1,0:T(8,128)(2,1)S(1)}, bf16[1024,1024]{1,0:T(8,128)(2,1)}, u32[]{:S(2)}) copy-start(bf16[1024,1024]{1,0:T(8,128)(2,1)} %all-gather.6.cloned.1.call-done) | copy-start | bytes 6291460
  320.2 6.8 %copy-start.13 = (bf16[1024,1024]{1,0:T(8,128)(2,1)S(1)}, bf16[1024,1024]{1,0:T(8,128)(2,1)}, u32[]{:S(2)}) copy-start(bf16[1024,1024]{1,0:T(8,128)(2,1)} %copy-done.12) | copy-start | bytes 6291460
Sparse Core Ops, SparseCore 0:
  71.8 34.0 all-gather.3
  120.5 35.1 reduce-scatter.2
  233.2 33.0 all-gather.5
  280.3 35.1 reduce-scatter.4
where the time goes:
time: 348 us
  waiting for transfers between devices  147 us (42%)
  local copies, waits for them, and re-layouts  69.9 us (20%)
  blocking collectives  56.6 us (16%)
  matrix products  44 us (13%)
  between operations  14.8 us (4%)
  starting transfers between devices  9.38 us (3%)
  other arithmetic  5.34 us (2%)
    all_gather x2, waiting for transfers between devices, dispatch(): return lax.all_gather(narrow, 'rep', axis=1, tiled=True)  67.3 us
    scatter x2, local copies, waits for them, and re-layouts, fill_rows(): return empty.at[flat, rank].set(picked)  52.6 us
    all_to_all x2, blocking collectives, dispatch(): lax.all_to_all(buffer, 'exp', split_axis=0, concat_axis=0, tiled=True)  37.1 us
    reduce_scatter x1, waiting for transfers between devices, on_device(): lax.psum_scatter(partial_value.astype(jnp.bfloat16), 'rep', scatter_dimen...  35.3 us
    reduce_scatter x1, waiting for transfers between devices, on_device(): lax.psum_scatter(dpartial.astype(jnp.bfloat16), 'rep', scatter_dimension=...  27.5 us
    all_to_all x2, waiting for transfers between devices, return_rows(): lax.all_to_all(rows.reshape(experts, per_slot, rows.shape[1]), 'exp', spl...  17.2 us
    unnamed x1, blocking collectives  10.6 us
    all_to_all x2, starting transfers between devices, return_rows(): lax.all_to_all(rows.reshape(experts, per_slot, rows.shape[1]), 'exp', spl...  9.22 us
  transfers between devices with their start and end apart: 6, of which 6 were waited for; matrix products, arithmetic and copies ran while one was open for 6% of the time, Pallas kernels for 0%

commit v1 on v0

--- a/solution.py
+++ b/solution.py
@@ -1,6 +1,10 @@
+import functools
+
 import jax
 import jax.numpy as jnp
 from jax import lax
+from jax.experimental import pallas as pl
+from jax.experimental.pallas import tpu as pltpu
 from jax.sharding import PartitionSpec as P
 
 HOT = 4
@@ -111,9 +115,473 @@
     return (mixed, grad_tokens, grad_probs, grad_gate[None], grad_up[None], grad_down[None])
 
 
+F32 = jnp.float32
+BF16 = jnp.bfloat16
+I32 = jnp.int32
+CHIPS = 4
+VMEM_BYTES = 56 * 1024 * 1024
+
+
+def dot(a, b, dims=((1,), (0,))):
+    return lax.dot_general(a, b, (dims, ((), ())), preferred_element_type=F32)
+
+
+def params(**kw):
+    return pltpu.CompilerParams(vmem_limit_bytes=VMEM_BYTES, **kw)
+
+
+def vmem():
+    return pl.BlockSpec(memory_space=pltpu.VMEM)
+
+
+def smem():
+    return pl.BlockSpec(memory_space=pltpu.SMEM)
+
+
+def place_rows(ids, own, par, per):
+    z, c = ids[0], ids[1]
+    toks = own.shape[1]
+    row = lax.broadcasted_iota(I32, (2 * CHIPS, toks), 0)
+    expert = 2 * (z ^ (row % CHIPS)) + c
+    first = row < CHIPS
+    named = [
+        jnp.where(first, own[k : k + 1, :], par[k : k + 1, :]).astype(I32) == expert
+        for k in range(2)
+    ]
+    either = jnp.logical_or(named[0], named[1])
+    before = lax.broadcasted_iota(I32, (toks, toks), 0) < lax.broadcasted_iota(
+        I32, (toks, toks), 1
+    )
+    rank = dot(either.astype(F32).astype(BF16), before.astype(F32).astype(BF16)).astype(I32)
+    return row, expert, named, either, rank
+
+
+def pick(rank, either, i, per):
+    at = jnp.where(either[i : i + 1, :], rank[i : i + 1, :], -1)
+    slots = lax.broadcasted_iota(I32, (per, at.shape[1]), 0)
+    return (slots == at).astype(F32)
+
+
+def x_kernel(per, ids, own_m, par_m, own_x, par_x, x0, x1, x2, x3):
+    own, par = own_m[...], par_m[...]
+    toks = own.shape[1]
+    row, _, _, either, rank = place_rows(ids, own, par, per)
+    place = either.astype(I32)
+    tail = lax.broadcasted_iota(I32, (16, toks), 0)
+    extra = jnp.zeros((16, toks), F32)
+    for i, line in enumerate((own[0:1, :], own[1:2, :], par[0:1, :], par[1:2, :])):
+        extra = jnp.where(tail == i, line, extra)
+    for q, out in enumerate((x0, x1, x2, x3)):
+        for src, ref in enumerate((own_x, par_x)):
+            hot = pick(rank, place > 0, CHIPS * src + q, per).astype(BF16)
+            out[src * per : (src + 1) * per, :] = dot(hot, ref[...]).astype(BF16)
+        if q:
+            out[2 * per : 2 * per + 16, :] = extra.astype(BF16)
+
+
+def g_kernel(
+    per, extra_slots, ids, cap, plan, own_m, par_m, e1, e2, e3, own_g, par_g, g0, g1, g2, g3, info
+):
+    own, par = own_m[...], par_m[...]
+    toks = own.shape[1]
+    z, c = ids[0], ids[1]
+    row, expert, named, either, rank = place_rows(ids, own, par, per)
+    expert_col = expert[:, 0:1]
+    q_col = row[:, 0:1] % CHIPS
+    first_col = row[:, 0:1] < CHIPS
+    limit = jnp.zeros((2 * CHIPS, 1), I32)
+    for q in range(CHIPS):
+        e = 2 * (z ^ q) + c
+        room = cap[e]
+        for h in range(HOT):
+            room = room + jnp.where(plan[h] == e, extra_slots, 0)
+        limit = jnp.where(q_col == q, room, limit)
+    earlier = jnp.zeros((2 * CHIPS, 1), F32)
+    remote = (None, e1, e2, e3)
+    for p in range(CHIPS):
+        table = None if p == 0 else remote[p][...].astype(F32)
+        for s in range(2):
+            if p == 0:
+                lines = [(own, par)[s][k : k + 1, :] for k in range(2)]
+            else:
+                lines = [table[2 * s + k : 2 * s + k + 1, :] for k in range(2)]
+            hits = jnp.logical_or(
+                lines[0].astype(I32) == expert, lines[1].astype(I32) == expert
+            ).astype(F32)
+            count = jnp.sum(hits, axis=1, keepdims=True)
+            block = 2 * (z ^ p) + (c ^ s)
+            ahead = jnp.where(
+                first_col,
+                (block < 2 * z + c).astype(F32),
+                (block < 2 * z + (c ^ 1)).astype(F32),
+            )
+            earlier = earlier + count * ahead
+    position = rank + earlier.astype(I32)
+    keep = jnp.where(position < limit, 1.0, 0.0)
+    first = row < CHIPS
+    weight = jnp.zeros((2 * CHIPS, toks), F32)
+    lines = []
+    for k in range(2):
+        prob = jnp.where(first, own[2 + k : 3 + k, :], par[2 + k : 3 + k, :])
+        mine = named[k].astype(F32)
+        weight = weight + mine * keep * prob
+        lines.append((mine * (row % CHIPS * per + rank + 1).astype(F32), mine * keep * prob, mine * keep))
+    at = lax.broadcasted_iota(I32, (128, toks), 0)
+    table = jnp.zeros((128, toks), F32)
+    for kind in range(3):
+        for src in range(2):
+            for k in range(2):
+                line = jnp.sum(
+                    jnp.where(first if src == 0 else jnp.logical_not(first), lines[k][kind], 0.0),
+                    axis=0,
+                    keepdims=True,
+                )
+                table = jnp.where(at == 4 * kind + 2 * src + k, line, table)
+    info[...] = jnp.transpose(table)
+    for q, out in enumerate((g0, g1, g2, g3)):
+        for src, ref in enumerate((own_g, par_g)):
+            i = CHIPS * src + q
+            hot = pick(rank, either, i, per)
+            scale = jnp.sum(hot * weight[i : i + 1, :], axis=1, keepdims=True)
+            rows = dot(hot.astype(BF16), ref[...])
+            out[src * per : (src + 1) * per, :] = (rows * scale).astype(BF16)
+
+
+def combine(per, src, k, rows, info):
+    slot = info[:, 2 * src + k : 2 * src + k + 1].astype(I32) - 1
+    slots = lax.broadcasted_iota(I32, (info.shape[0], CHIPS * per), 1)
+    return dot((slots == slot).astype(F32).astype(BF16), rows)
+
+
+def back_kernel(per, with_dots, y0, y1, y2, y3, info_ref, *refs):
+    if with_dots:
+        own_g, par_g, kept, sent = refs
+    else:
+        kept, sent = refs
+    info = info_ref[...]
+    feats = y0.shape[1]
+    toks = info.shape[0]
+    lane = lax.broadcasted_iota(I32, (toks, 128), 1)
+    for src, out in enumerate((kept, sent)):
+        rows = jnp.concatenate([y[src * per : (src + 1) * per, :] for y in (y0, y1, y2, y3)], axis=0)
+        total = jnp.zeros((toks, feats), F32)
+        dots = jnp.zeros((toks, 128), F32)
+        for k in range(2):
+            picked = combine(per, src, k, rows, info)
+            at = 2 * src + k
+            total = total + info[:, 4 + at : 5 + at] * picked
+            if with_dots:
+                grad = (own_g, par_g)[src][...].astype(F32)
+                inner = jnp.sum(grad * picked, axis=1, keepdims=True) * info[:, 8 + at : 9 + at]
+                dots = jnp.where(lane == k, inner, dots)
+        out[:, 0:feats] = total
+        if with_dots:
+            out[:, feats : feats + 128] = dots
+
+
+def assemble(r, shards, cat):
+    own, a, b, c, d = shards
+    feats = own.shape[1]
+    half = c.shape[0]
+
+    def cols(k):
+        return pl.ds(pl.multiple_of((r ^ k) * feats, feats), feats)
+
+    cat[:, cols(0)] = own[...]
+    cat[:, cols(1)] = a[...]
+    cat[:, cols(2)] = b[...]
+    cat[0:half, cols(3)] = c[...]
+    cat[half : 2 * half, cols(3)] = d[...]
+
+
+def split_out(r, total, feats, outs):
+    send_a, keep_a, send_b, keep_b = outs
+    half = send_a.shape[0]
+    for rows, out, pair in (
+        (0, send_a, (1, 3)),
+        (0, keep_a, (0, 2)),
+        (half, send_b, (2, 3)),
+        (half, keep_b, (0, 1)),
+    ):
+        for n, k in enumerate(pair):
+            cols = pl.ds(pl.multiple_of((r ^ k) * feats, feats), feats)
+            out[:, n * feats : (n + 1) * feats] = total[rows : rows + half, cols].astype(BF16)
+
+
+def forward_kernel(ids, own, a, b, c, d, wg, wu, wd, cat, hid, act, slope, sa, ka, sb, kb, total, gs, us):
+    j = pl.program_id(0)
+    r = ids[2]
+
+    @pl.when(j == 0)
+    def _():
+        assemble(r, (own, a, b, c, d), cat)
+
+    gs[...] = dot(cat[...], wg[...])
+    us[...] = dot(cat[...], wu[...])
+    step = 256
+    for at in range(0, gs.shape[0], step):
+        gate, up = gs[at : at + step, :], us[at : at + step, :]
+        sig = jax.nn.sigmoid(gate)
+        silu = gate * sig
+        hid[at : at + step, :] = (silu * up).astype(BF16)
+        act[at : at + step, :] = silu.astype(act.dtype)
+        slope[at : at + step, :] = (up * sig * (1.0 + gate * (1.0 - sig))).astype(slope.dtype)
+    part = dot(hid[...], wd[...])
+
+    @pl.when(j == 0)
+    def _():
+        total[...] = part
+
+    @pl.when(j > 0)
+    def _():
+        total[...] += part
+
+    @pl.when(j == pl.num_programs(0) - 1)
+    def _():
+        split_out(r, total, own.shape[1], (sa, ka, sb, kb))
+
+
+def backward_kernel(ids, own, a, b, c, d, wg, wu, wd, act, slope, cat, dgate, dup, sa, ka, sb, kb, total, dh):
+    j = pl.program_id(0)
+    r = ids[2]
+
+    @pl.when(j == 0)
+    def _():
+        assemble(r, (own, a, b, c, d), cat)
+
+    dh[...] = dot(cat[...], wd[...], ((1,), (1,)))
+    step = 256
+    for at in range(0, dh.shape[0], step):
+        piece = dh[at : at + step, :]
+        dgate[at : at + step, :] = (piece * slope[at : at + step, :].astype(F32)).astype(BF16)
+        dup[at : at + step, :] = (piece * act[at : at + step, :].astype(F32)).astype(BF16)
+    part = dot(dgate[...], wg[...], ((1,), (1,))) + dot(dup[...], wu[...], ((1,), (1,)))
+
+    @pl.when(j == 0)
+    def _():
+        total[...] = part
+
+    @pl.when(j > 0)
+    def _():
+        total[...] += part
+
+    @pl.when(j == pl.num_programs(0) - 1)
+    def _():
+        split_out(r, total, own.shape[1], (sa, ka, sb, kb))
+
+
+def weights_kernel(xcat, gcat, dgate, dup, hid, ggate, gup, gdown, turned):
+    @pl.when(pl.program_id(0) == 0)
+    def _():
+        turned[...] = jnp.transpose(xcat[...])
+
+    ggate[...] = dot(turned[...], dgate[...])
+    gup[...] = dot(turned[...], dup[...])
+    gdown[...] = dot(hid[...], gcat[...], ((0,), (0,)))
+
+
+def middle_kernel(ka, ra, kb, rb, sa, sb, kept):
+    half, feats = sa.shape
+    kept[0:half, :] = ka[:, 0:feats].astype(F32) + ra[:, 0:feats].astype(F32)
+    kept[half : 2 * half, :] = kb[:, 0:feats].astype(F32) + rb[:, 0:feats].astype(F32)
+    sa[...] = (ka[:, feats:].astype(F32) + ra[:, feats:].astype(F32)).astype(BF16)
+    sb[...] = (kb[:, feats:].astype(F32) + rb[:, feats:].astype(F32)).astype(BF16)
+
+
+def last_kernel(kept, ra, rb, y0, y1, y2, y3):
+    half = ra.shape[0]
+    size = y0.shape[0]
+    for q, out in enumerate((y0, y1, y2, y3)):
+        at = q * size
+        other = ra[at : at + size, :] if at < half else rb[at - half : at - half + size, :]
+        out[...] = (kept[at : at + size, :] + other.astype(F32)).astype(BF16)
+
+
+def shift(x, axis, bit):
+    n = lax.axis_size(axis)
+    return lax.ppermute(x, axis, [(i, i ^ bit) for i in range(n)])
+
+
+def sds(shape, dtype):
+    return jax.ShapeDtypeStruct(shape, dtype)
+
+
+def gather_quad(x):
+    half = x.shape[0] // 2
+    a = shift(x, "rep", 1)
+    b = shift(x, "rep", 2)
+    c = shift(a[:half], "rep", 2)
+    d = shift(b[half:], "rep", 1)
+    return x, a, b, c, d
+
+
+def reduce_quad(sa, ka, sb, kb):
+    ra = shift(sa, "rep", 1)
+    rb = shift(sb, "rep", 2)
+    half, feats = sa.shape[0], sa.shape[1] // 2
+    piece = sds((half, feats), BF16)
+    ma, mb, kept = pl.pallas_call(
+        middle_kernel,
+        out_shape=(piece, piece, sds((2 * half, feats), F32)),
+        compiler_params=params(),
+        name="reduce_middle",
+    )(ka, ra, kb, rb)
+    fa = shift(ma, "rep", 2)
+    fb = shift(mb, "rep", 1)
+    quarter = sds((half // 2, feats), BF16)
+    return pl.pallas_call(
+        last_kernel,
+        out_shape=(quarter,) * 4,
+        compiler_params=params(),
+        name="reduce_last",
+    )(kept, fa, fb)
+
+
+def over_chips(chunks):
+    return [chunks[q] if q == 0 else shift(chunks[q], "exp", 2 * q) for q in range(CHIPS)]
+
+
+def on_quad(tokens, routes, probs, capacity, plan, grad_out, w_gate, w_up, w_down):
+    toks, feats = tokens.shape
+    per = 4 * toks // capacity.shape[0]
+    wg, wu, wd = w_gate[0], w_up[0], w_down[0]
+    width, ff = wg.shape
+    rows = 2 * per * CHIPS
+    me = lax.axis_index("exp").astype(I32)
+    ids = jnp.stack([me // 2, me % 2, lax.axis_index("rep").astype(I32)])
+    own_m = jnp.concatenate(
+        [routes.T.astype(F32), probs.T, jnp.zeros((4, toks), F32)], axis=0
+    )
+    par_m = shift(own_m, "exp", 1)
+    par_x = shift(tokens, "exp", 1)
+    par_g = shift(grad_out, "exp", 1)
+
+    near = sds((2 * per, feats), BF16)
+    far = sds((2 * per + 16, feats), BF16)
+    xc = pl.pallas_call(
+        functools.partial(x_kernel, per),
+        in_specs=[smem()] + [vmem()] * 4,
+        out_shape=(near, far, far, far),
+        compiler_params=params(),
+        name="send_tokens",
+    )(ids, own_m, par_m, tokens, par_x)
+    xr = over_chips(xc)
+    whole = pl.BlockSpec((8, toks), lambda i: (0, 0))
+    block = pl.BlockSpec((toks, feats), lambda i: (0, 0))
+    tail = pl.BlockSpec((16, feats), lambda i: (2 * per // 16, 0))
+    gc = pl.pallas_call(
+        functools.partial(g_kernel, per, 2 * toks),
+        grid=(1,),
+        in_specs=[smem()] * 3 + [whole] * 2 + [tail] * 3 + [block] * 2,
+        out_specs=[pl.BlockSpec((2 * per, feats), lambda i: (0, 0))] * 4
+        + [pl.BlockSpec((toks, 128), lambda i: (0, 0))],
+        out_shape=(near,) * 4 + (sds((toks, 128), F32),),
+        compiler_params=params(),
+        name="send_grads",
+    )(ids, capacity, plan, own_m, par_m, xr[1], xr[2], xr[3], grad_out, par_g)
+    info = gc[4]
+    gr = over_chips(gc[:4])
+
+    xs = gather_quad(jnp.concatenate([xr[0]] + [x[: 2 * per] for x in xr[1:]], axis=0))
+    gs = gather_quad(jnp.concatenate(gr, axis=0))
+
+    jb = 256
+    steps = ff // jb
+    shards = [
+        pl.BlockSpec((rows, feats), lambda j: (0, 0)),
+        pl.BlockSpec((rows, feats), lambda j: (0, 0)),
+        pl.BlockSpec((rows, feats), lambda j: (0, 0)),
+        pl.BlockSpec((rows // 2, feats), lambda j: (0, 0)),
+        pl.BlockSpec((rows // 2, feats), lambda j: (0, 0)),
+    ]
+    w_col = pl.BlockSpec((width, jb), lambda j: (0, j))
+    w_row = pl.BlockSpec((jb, width), lambda j: (j, 0))
+    full = pl.BlockSpec((rows, width), lambda j: (0, 0))
+    col = pl.BlockSpec((rows, jb), lambda j: (0, j))
+    pair = pl.BlockSpec((rows // 2, 2 * feats), lambda j: (0, 0))
+    pair_t = sds((rows // 2, 2 * feats), BF16)
+    inner = sds((rows, ff), BF16)
+    xcat, hid, act, slope, *out_parts = pl.pallas_call(
+        forward_kernel,
+        grid=(steps,),
+        in_specs=[smem()] + shards + [w_col, w_col, w_row],
+        out_specs=[full, col, col, col] + [pair] * 4,
+        out_shape=(sds((rows, width), BF16), inner, inner, inner) + (pair_t,) * 4,
+        scratch_shapes=[
+            pltpu.VMEM((rows, width), F32),
+            pltpu.VMEM((rows, jb), F32),
+            pltpu.VMEM((rows, jb), F32),
+        ],
+        compiler_params=params(),
+        cost_estimate=pl.CostEstimate(
+            flops=6 * rows * width * ff, bytes_accessed=24 * rows * width, transcendentals=rows * ff
+        ),
+        name="forward",
+    )(ids, *xs, wg, wu, wd)
+    y = reduce_quad(*out_parts)
+
+    gcat, dgate, dup, *dx_parts = pl.pallas_call(
+        backward_kernel,
+        grid=(steps,),
+        in_specs=[smem()] + shards + [w_col, w_col, w_row, col, col],
+        out_specs=[full, col, col] + [pair] * 4,
+        out_shape=(sds((rows, width), BF16), inner, inner) + (pair_t,) * 4,
+        scratch_shapes=[pltpu.VMEM((rows, width), F32), pltpu.VMEM((rows, jb), F32)],
+        compiler_params=params(),
+        cost_estimate=pl.CostEstimate(
+            flops=6 * rows * width * ff, bytes_accessed=24 * rows * width, transcendentals=0
+        ),
+        name="backward",
+    )(ids, *gs, wg, wu, wd, act, slope)
+    dx = reduce_quad(*dx_parts)
+
+    grad_gate, grad_up, grad_down = pl.pallas_call(
+        weights_kernel,
+        grid=(steps,),
+        in_specs=[full, full, col, col, col],
+        out_specs=[w_col, w_col, w_row],
+        out_shape=(sds((width, ff), F32), sds((width, ff), F32), sds((ff, width), F32)),
+        scratch_shapes=[pltpu.VMEM((width, rows), BF16)],
+        compiler_params=params(),
+        cost_estimate=pl.CostEstimate(
+            flops=6 * rows * width * ff, bytes_accessed=24 * rows * width, transcendentals=0
+        ),
+        name="weight_grads",
+    )(xcat, gcat, dgate, dup, hid)
+
+    yr = over_chips(y)
+    wide = sds((toks, feats + 128), F32)
+    kept, sent = pl.pallas_call(
+        functools.partial(back_kernel, per, True),
+        out_shape=(wide, wide),
+        compiler_params=params(),
+        name="combine_out",
+    )(*yr, info, grad_out, par_g)
+    got = shift(sent, "exp", 1)
+    both = kept + got
+    mixed = both[:, :feats].astype(BF16)
+    dots = both[:, feats : feats + 2].T
+    dots = dots + shift(dots, "rep", 1)
+    dots = dots + shift(dots, "rep", 2)
+    grad_probs = dots.T
+
+    dr = over_chips(dx)
+    flat = sds((toks, feats), F32)
+    kept, sent = pl.pallas_call(
+        functools.partial(back_kernel, per, False),
+        out_shape=(flat, flat),
+        compiler_params=params(),
+        name="combine_grad",
+    )(*dr, info)
+    grad_tokens = (kept + shift(sent, "exp", 1)).astype(BF16)
+    return (mixed, grad_tokens, grad_probs, grad_gate[None], grad_up[None], grad_down[None])
+
+
 def solution(mesh):
+    sizes = dict(mesh.shape)
+    fast = sizes["rep"] == 4 and sizes["exp"] == 8
     return jax.shard_map(
-        on_device,
+        on_quad if fast else on_device,
         mesh=mesh,
         in_specs=(
             P("exp", "rep"),

time: 348 us -> 182 us (0.52)
  waiting for transfers between devices: 147 us -> 56.9 us
  Pallas kernels: 0 us -> 64.7 us
  blocking collectives: 56.6 us -> 0 us
  local copies, waits for them, and re-layouts: 69.9 us -> 14.1 us
  matrix products: 44 us -> 0 us
  starting transfers between devices: 9.38 us -> 40.9 us
  between operations: 14.8 us -> 0.93 us
    all_gather x2 -> x0, waiting for transfers between devices: 67.3 us -> none  [dispatch(): return lax.all_gather(narrow, 'rep', axis=1, tiled=True)]
    pallas_call x0 -> x11, Pallas kernels: none -> 64.7 us  [the longest x1 18.4 us: on_quad(): pl.pallas_call(backward_kernel, grid=(steps,), in_specs=[smem()] + shards...]
    reduce_scatter x2 -> x0, waiting for transfers between devices: 62.8 us -> none  [the longest x1 35.3 us: on_device(): lax.psum_scatter(partial_value.astype(jnp.bfloat16), 'rep', scatter_dimen...]
    ppermute x0 -> x35, waiting for transfers between devices: none -> 56.9 us  [shift(): return lax.ppermute(x, axis, [(i, i ^ bit) for i in range(n)])]
    scatter x2 -> x0, local copies, waits for them, and re-layouts: 52.6 us -> none  [fill_rows(): return empty.at[flat, rank].set(picked)]
    dot_general x9 -> x0, matrix products: 44 us -> none  [the longest x1 7.07 us: on_device(): lax.dot_general(dout, wd, (((1,), (1,)), ((), ())), preferred_element_typ...]
    ppermute x0 -> x35, starting transfers between devices: none -> 40.9 us  [shift(): return lax.ppermute(x, axis, [(i, i ^ bit) for i in range(n)])]
    all_to_all x2 -> x0, blocking collectives: 37.1 us -> none  [dispatch(): lax.all_to_all(buffer, 'exp', split_axis=0, concat_axis=0, tiled=True)]
  transfers between devices with their start and end apart: 6 -> 35, of which waited for: 6 -> 14; matrix products, arithmetic and copies ran while one was open for 6% -> 5% of each run, Pallas kernels for 0% -> 33%
where the time goes in v1:
time: 182 us; the launch traced here: 181 us
  Pallas kernels  64.7 us (36%)
  waiting for transfers between devices  56.9 us (31%)
  starting transfers between devices  40.9 us (22%)
  local copies, waits for them, and re-layouts  14.1 us (8%)
  other arithmetic  3.71 us (2%)
    ppermute x35, waiting for transfers between devices, shift(): return lax.ppermute(x, axis, [(i, i ^ bit) for i in range(n)])  56.9 us
    ppermute x35, starting transfers between devices, shift(): return lax.ppermute(x, axis, [(i, i ^ bit) for i in range(n)])  40.9 us
    pallas_call x1, Pallas kernels, on_quad(): pl.pallas_call(backward_kernel, grid=(steps,), in_specs=[smem()] + shards...  18.4 us
    pallas_call x1, Pallas kernels, on_quad(): pl.pallas_call(forward_kernel, grid=(steps,), in_specs=[smem()] + shards...  14.5 us
    pallas_call x1, Pallas kernels, on_quad(): pl.pallas_call(weights_kernel, grid=(steps,), in_specs=[full, full, col,...  12.1 us
    unnamed x70, local copies, waits for them, and re-layouts  10.5 us
    pallas_call x2, Pallas kernels, reduce_quad(): pl.pallas_call(middle_kernel, out_shape=(piece, piece, sds((2 * half, fea...  5.45 us
    pallas_call x2, Pallas kernels, reduce_quad(): pl.pallas_call(last_kernel, out_shape=(quarter,) * 4, compiler_params=par...  4.32 us
  transfers between devices with their start and end apart: 35, of which 14 were waited for; matrix products, arithmetic and copies ran while one was open for 5% of the time, Pallas kernels for 33%

profile of v1, /device:TPU:0, one launch (start us, length us, event | category | flops | bytes accessed | tf_op | source)
XLA Modules:
  0.0 181.3 jit_solution(7173922937559236379)
XLA Ops:
  5.1 2.1 %send_tokens.1 = (bf16[256,256]{1,0:T(8,128)(2,1)}, bf16[272,256]{1,0:T(8,128)(2,1)}, bf16[272,256]{1,0:T(8,128)(2,1)}, bf16[272,256]{1,0:T(8,128)(2,1)}) custom-call(s32[3]{0:T(128)} %pad_add_fusion.ids, f32[8,256]{1,0:T(8,128)} %copy-done.26, f32[8,256]{1,0:T(8,128)} %copy-done.27, bf16[256,256]{1,0:T(8,128)(2,1)} %own_x.1, bf16[256,256]{1,0:T(8,128)(2,1)} %copy-done.25), custom_call_target="tpu_custom_call" | custom-call | tf_op jit(solution)/shard_map/send_tokens/pallas_call | solution.py:461
  7.2 2.7 %collective-permute-start.2 = (bf16[272,256]{1,0:T(8,128)(2,1)}, bf16[272,256]{1,0:T(8,128)(2,1)S(1)}, u32[]{:S(2)}, u32[]{:S(2)}) collective-permute-start(bf16[272,256]{1,0:T(8,128)(2,1)} %get-tuple-element.52), channel_id=1, source_target_pairs={{0,2},{1,3},{2,0},{3,1},{4,6},{5,7},{6,4},{7,5},{8,10},{9,11},{10,... | collective-permute-start | bytes 417800 | tf_op jit(solution)/shard_map/ppermute | solution.py:402
  10.0 2.6 %collective-permute-start.3 = (bf16[272,256]{1,0:T(8,128)(2,1)}, bf16[272,256]{1,0:T(8,128)(2,1)S(1)}, u32[]{:S(2)}, u32[]{:S(2)}) collective-permute-start(bf16[272,256]{1,0:T(8,128)(2,1)} %get-tuple-element.53), channel_id=1, source_target_pairs={{0,4},{1,5},{2,6},{3,7},{4,0},{5,1},{6,2},{7,3},{8,12},{9,13},{10,... | collective-permute-start | bytes 417800 | tf_op jit(solution)/shard_map/ppermute | solution.py:402
  12.6 1.6 collective-permute-done.16.par_g.refs_1_
  14.1 2.6 %collective-permute-done.2.e1 = bf16[272,256]{1,0:T(8,128)(2,1)S(1)} collective-permute-done((bf16[272,256]{1,0:T(8,128)(2,1)}, bf16[272,256]{1,0:T(8,128)(2,1)S(1)}, u32[]{:S(2)}, u32[]{:S(2)}) %collective-permute-start.2) | collective-permute-done | bytes 139296 | tf_op jit(solution)/shard_map/ppermute | solution.py:402
  16.7 6.9 %collective-permute-done.3.e2 = bf16[272,256]{1,0:T(8,128)(2,1)S(1)} collective-permute-done((bf16[272,256]{1,0:T(8,128)(2,1)}, bf16[272,256]{1,0:T(8,128)(2,1)S(1)}, u32[]{:S(2)}, u32[]{:S(2)}) %collective-permute-start.3) | collective-permute-done | bytes 139296 | tf_op jit(solution)/shard_map/ppermute | solution.py:402
  24.9 2.4 %send_grads.1 = (bf16[256,256]{1,0:T(8,128)(2,1)}, bf16[256,256]{1,0:T(8,128)(2,1)}, bf16[256,256]{1,0:T(8,128)(2,1)}, bf16[256,256]{1,0:T(8,128)(2,1)}, f32[256,128]{1,0:T(8,128)}) custom-call(s32[3]{0:T(128)} %pad_add_fusion.ids, s32[8]{0:T(128)} %cap.1, s32[8]{0:T(128)} %plan.1, f32[8,256]{1,0:T(8,128)} %copy-done.26, f32[8,256]{1,0:T(8,128)} %copy-done.27, ...), custom_call_target="tpu_custom_call" | custom-call | tf_op jit(solution)/shard_map/send_grads/pallas_call | solution.py:472
  27.3 2.0 %collective-permute-start.18 = (bf16[256,256]{1,0:T(8,128)(2,1)}, bf16[256,256]{1,0:T(8,128)(2,1)S(1)}, u32[]{:S(2)}, u32[]{:S(2)}) collective-permute-start(bf16[256,256]{1,0:T(8,128)(2,1)} %get-tuple-element.70), channel_id=1, source_target_pairs={{0,2},{1,3},{2,0},{3,1},{4,6},{5,7},{6,4},{7,5},{8,10},{9,11},{10,... | collective-permute-start | bytes 393224 | tf_op jit(solution)/shard_map/ppermute | solution.py:402
  33.0 1.6 collective-permute-start.6
  39.5 7.8 %collective-permute-done.19 = bf16[256,256]{1,0:T(8,128)(2,1)S(1)} collective-permute-done((bf16[256,256]{1,0:T(8,128)(2,1)}, bf16[256,256]{1,0:T(8,128)(2,1)S(1)}, u32[]{:S(2)}, u32[]{:S(2)}) %collective-permute-start.19) | collective-permute-done | bytes 131104 | tf_op jit(solution)/shard_map/ppermute | solution.py:402
  48.5 1.5 collective-permute-start.8
  50.1 1.6 collective-permute-start.7
  51.7 10.6 %collective-permute-done.22.b = bf16[1024,256]{1,0:T(8,128)(2,1)S(1)} collective-permute-done((bf16[1024,256]{1,0:T(8,128)(2,1)S(1)}, bf16[1024,256]{1,0:T(8,128)(2,1)S(1)}, u32[]{:S(2)}, u32[]{:S(2)}) %collective-permute-start.22) | collective-permute-done | bytes 524320 | tf_op jit(solution)/shard_map/ppermute | solution.py:402
  64.4 3.9 %collective-permute-done.8.d = bf16[512,256]{1,0:T(8,128)(2,1)S(1)} collective-permute-done((bf16[512,256]{1,0:T(8,128)(2,1)S(1)}, bf16[512,256]{1,0:T(8,128)(2,1)S(1)}, u32[]{:S(2)}, u32[]{:S(2)}) %collective-permute-start.8) | collective-permute-done | bytes 262176 | tf_op jit(solution)/shard_map/ppermute | solution.py:402
  69.2 14.5 %forward.1 = (bf16[1024,1024]{1,0:T(8,128)(2,1)}, bf16[1024,1024]{1,0:T(8,128)(2,1)}, bf16[1024,1024]{1,0:T(8,128)(2,1)}, bf16[1024,1024]{1,0:T(8,128)(2,1)}, bf...) custom-call(s32[3]{0:T(128)} %pad_add_fusion.ids, ...), custom_call_target="tpu_custom_call" | custom-call | flops 6442450944 | bytes 25165824 | tf_op jit(solution)/shard_map/forward/pallas_call | solution.py:504
  86.6 18.4 %backward.1 = (bf16[1024,1024]{1,0:T(8,128)(2,1)}, bf16[1024,1024]{1,0:T(8,128)(2,1)}, bf16[1024,1024]{1,0:T(8,128)(2,1)}, bf16[512,512]{1,0:T(8,128)(2,1)}, bf1...) custom-call(s32[3]{0:T(128)} %pad_add_fusion.ids, bf16[1024,256]{1,0:T(8,128)(2,1)} %copy-done.28, ...), custom_call_target="tpu_custom_call" | custom-call | flops 6442450944 | bytes 25165824 | tf_op jit(solution)/shard_map/backward/pallas_call | solution.py:523
  105.0 1.6 collective-permute-start.25
  108.1 2.7 %reduce_middle.2 = (bf16[512,256]{1,0:T(8,128)(2,1)}, bf16[512,256]{1,0:T(8,128)(2,1)}, f32[1024,256]{1,0:T(8,128)}) custom-call(bf16[512,512]{1,0:T(8,128)(2,1)} %get-tuple-element.55.ka, bf16[512,512]{1,0:T(8,128)(2,1)} %copy-done.7, bf16[512,512]{1,0:T(8,128)(2,1)} %get-tuple-element.57.kb, bf16[512,512]{1,0:T(8,128)(2,1)} %copy-done.8), custom_call_target="tpu_custom_call" | custom-call | tf_op jit(solution)/shard_map/reduce_middle/pallas_call | solution.py:423
  110.8 1.5 collective-permute-start.11
  112.9 7.0 %collective-permute-done.11.ra = bf16[512,256]{1,0:T(8,128)(2,1)S(1)} collective-permute-done((bf16[512,256]{1,0:T(8,128)(2,1)}, bf16[512,256]{1,0:T(8,128)(2,1)S(1)}, u32[]{:S(2)}, u32[]{:S(2)}) %collective-permute-start.11) | collective-permute-done | bytes 262176 | tf_op jit(solution)/shard_map/ppermute | solution.py:402
  120.6 2.2 %reduce_last.2 = (bf16[256,256]{1,0:T(8,128)(2,1)}, bf16[256,256]{1,0:T(8,128)(2,1)}, bf16[256,256]{1,0:T(8,128)(2,1)}, bf16[256,256]{1,0:T(8,128)(2,1)}) custom-call(f32[1024,256]{1,0:T(8,128)} %get-tuple-element.59.kept, bf16[512,256]{1,0:T(8,128)(2,1)} %copy-done.13, bf16[512,256]{1,0:T(8,128)(2,1)} %copy-done.14), custom_call_target="tpu_custom_call" | custom-call | tf_op jit(solution)/shard_map/reduce_last/pallas_call | solution.py:432
  122.8 4.2 %collective-permute-start.13 = (bf16[256,256]{1,0:T(8,128)(2,1)}, bf16[256,256]{1,0:T(8,128)(2,1)S(1)}, u32[]{:S(2)}, u32[]{:S(2)}) collective-permute-start(bf16[256,256]{1,0:T(8,128)(2,1)} %get-tuple-element.63), channel_id=1, source_target_pairs={{0,2},{1,3},{2,0},{3,1},{4,6},{5,7},{6,4},{7,5},{8,10},{9,11},{10,... | collective-permute-start | bytes 393224 | tf_op jit(solution)/shard_map/ppermute | solution.py:402
  127.0 2.4 %collective-permute-start.14 = (bf16[256,256]{1,0:T(8,128)(2,1)}, bf16[256,256]{1,0:T(8,128)(2,1)S(1)}, u32[]{:S(2)}, u32[]{:S(2)}) collective-permute-start(bf16[256,256]{1,0:T(8,128)(2,1)} %get-tuple-element.64), channel_id=1, source_target_pairs={{0,4},{1,5},{2,6},{3,7},{4,0},{5,1},{6,2},{7,3},{8,12},{9,13},{10,... | collective-permute-start | bytes 393224 | tf_op jit(solution)/shard_map/ppermute | solution.py:402
  131.8 2.7 %reduce_middle.3 = (bf16[512,256]{1,0:T(8,128)(2,1)}, bf16[512,256]{1,0:T(8,128)(2,1)}, f32[1024,256]{1,0:T(8,128)}) custom-call(bf16[512,512]{1,0:T(8,128)(2,1)} %get-tuple-element.75.ka, bf16[512,512]{1,0:T(8,128)(2,1)} %copy-done.5, bf16[512,512]{1,0:T(8,128)(2,1)} %get-tuple-element.77.kb, bf16[512,512]{1,0:T(8,128)(2,1)} %copy-done.6), custom_call_target="tpu_custom_call" | custom-call | tf_op jit(solution)/shard_map/reduce_middle/pallas_call | solution.py:423
  135.6 1.7 collective-permute-done.14.y2
  138.0 3.1 %combine_out.1 = (f32[256,384]{1,0:T(8,128)}, f32[256,384]{1,0:T(8,128)}) custom-call(bf16[256,256]{1,0:T(8,128)(2,1)} %get-tuple-element.62.y0, bf16[256,256]{1,0:T(8,128)(2,1)} %copy-done.15, bf16[256,256]{1,0:T(8,128)(2,1)} %copy-done.16, bf16[256,256]{1,0:T(8,128)(2,1)} %copy-done.17, f32[256,128]{1,0:T(8,128)} %get-tuple-element.66.info_ref, ...), custom_call_target="tpu_custom_call" | custom-call | tf_op jit(solution)/shard_map/combine_out/pallas_call | solution.py:554
  142.4 2.2 %reduce_last.3 = (bf16[256,256]{1,0:T(8,128)(2,1)}, bf16[256,256]{1,0:T(8,128)(2,1)}, bf16[256,256]{1,0:T(8,128)(2,1)}, bf16[256,256]{1,0:T(8,128)(2,1)}) custom-call(f32[1024,256]{1,0:T(8,128)} %get-tuple-element.79.kept, bf16[512,256]{1,0:T(8,128)(2,1)} %copy-done.11, bf16[512,256]{1,0:T(8,128)(2,1)} %copy-done.12), custom_call_target="tpu_custom_call" | custom-call | tf_op jit(solution)/shard_map/reduce_last/pallas_call | solution.py:432
  148.9 3.6 %collective-permute-done.29.y1 = bf16[256,256]{1,0:T(8,128)(2,1)S(1)} collective-permute-done((bf16[256,256]{1,0:T(8,128)(2,1)}, bf16[256,256]{1,0:T(8,128)(2,1)S(1)}, u32[]{:S(2)}, u32[]{:S(2)}) %collective-permute-start.29) | collective-permute-done | bytes 131104 | tf_op jit(solution)/shard_map/ppermute | solution.py:402
  152.6 6.5 %collective-permute-done.30.y2 = bf16[256,256]{1,0:T(8,128)(2,1)S(1)} collective-permute-done((bf16[256,256]{1,0:T(8,128)(2,1)}, bf16[256,256]{1,0:T(8,128)(2,1)S(1)}, u32[]{:S(2)}, u32[]{:S(2)}) %collective-permute-start.30) | collective-permute-done | bytes 131104 | tf_op jit(solution)/shard_map/ppermute | solution.py:402
  159.8 2.4 %combine_grad.1 = (f32[256,256]{1,0:T(8,128)}, f32[256,256]{1,0:T(8,128)}) custom-call(bf16[256,256]{1,0:T(8,128)(2,1)} %get-tuple-element.82.y0, bf16[256,256]{1,0:T(8,128)(2,1)} %copy-done.18, bf16[256,256]{1,0:T(8,128)(2,1)} %copy-done.19, bf16[256,256]{1,0:T(8,128)(2,1)} %copy-done.20, f32[256,128]{1,0:T(8,128)} %get-tuple-element.66.info_ref), custom_call_target="tpu_custom_call" | custom-call | tf_op jit(solution)/shard_map/combine_grad/pallas_call | solution.py:570
  162.8 12.1 %weight_grads.1 = (f32[1024,1024]{1,0:T(8,128)}, f32[1024,1024]{1,0:T(8,128)}, f32[1024,1024]{1,0:T(8,128)}) custom-call(bf16[1024,1024]{1,0:T(8,128)(2,1)} %get-tuple-element.88.xcat, bf16[1024,1024]{1,0:T(8,128)(2,1)} %get-tuple-element.89.gcat, bf16[1024,1024]{1,0:T(8,128)(2,1)} %get-tuple-element.90.dgate, bf16[1024,1024]{1,0:T(8,128)(2,1)} %get-tuple-element.91.dup, ...), custom_call_target="tpu_custom_call" | custom-call | flops 6442450944 | bytes 25165824 | tf_op jit(solution)/shard_map/weight_grads/pallas_call | solution.py:538
  177.1 3.6 %collective-permute-done.34 = f32[2,256]{0,1:T(8,128)S(1)} collective-permute-done((f32[2,256]{0,1:T(8,128)S(1)}, f32[2,256]{0,1:T(8,128)S(1)}, u32[]{:S(2)}, u32[]{:S(2)}) %collective-permute-start.34) | collective-permute-done | bytes 2080 | tf_op jit(solution)/shard_map/ppermute | solution.py:402
  (139 shorter events, 38.1 us)
Async XLA Ops:
  7.2 9.4 %collective-permute-start.2 = (bf16[272,256]{1,0:T(8,128)(2,1)}, bf16[272,256]{1,0:T(8,128)(2,1)S(1)}, u32[]{:S(2)}, u32[]{:S(2)}) collective-permute-start(bf16[272,256]{1,0:T(8,128)(2,1)} %get-tuple-element.52), channel_id=1, source_target_pairs={{0,2},{1,3},{2,0},{3,1},{4,6},{5,7},{6,4},{7,5},{8,10},{9,11},{10,... | collective-permute-start | bytes 417800 | tf_op jit(solution)/shard_map/ppermute | solution.py:402
  10.0 13.7 %collective-permute-start.3 = (bf16[272,256]{1,0:T(8,128)(2,1)}, bf16[272,256]{1,0:T(8,128)(2,1)S(1)}, u32[]{:S(2)}, u32[]{:S(2)}) collective-permute-start(bf16[272,256]{1,0:T(8,128)(2,1)} %get-tuple-element.53), channel_id=1, source_target_pairs={{0,4},{1,5},{2,6},{3,7},{4,0},{5,1},{6,2},{7,3},{8,12},{9,13},{10,... | collective-permute-start | bytes 417800 | tf_op jit(solution)/shard_map/ppermute | solution.py:402
  12.6 11.1 %collective-permute-start.4 = (bf16[272,256]{1,0:T(8,128)(2,1)}, bf16[272,256]{1,0:T(8,128)(2,1)S(1)}, u32[]{:S(2)}, u32[]{:S(2)}) collective-permute-start(bf16[272,256]{1,0:T(8,128)(2,1)} %get-tuple-element.54), channel_id=1, source_target_pairs={{0,6},{1,7},{2,4},{3,5},{4,2},{5,3},{6,0},{7,1},{8,14},{9,15},{10,... | collective-permute-start | bytes 417800 | tf_op jit(solution)/shard_map/ppermute | solution.py:402
  27.3 12.2 %collective-permute-start.18 = (bf16[256,256]{1,0:T(8,128)(2,1)}, bf16[256,256]{1,0:T(8,128)(2,1)S(1)}, u32[]{:S(2)}, u32[]{:S(2)}) collective-permute-start(bf16[256,256]{1,0:T(8,128)(2,1)} %get-tuple-element.70), channel_id=1, source_target_pairs={{0,2},{1,3},{2,0},{3,1},{4,6},{5,7},{6,4},{7,5},{8,10},{9,11},{10,... | collective-permute-start | bytes 393224 | tf_op jit(solution)/shard_map/ppermute | solution.py:402
  33.0 15.4 %collective-permute-start.6 = (bf16[1024,256]{1,0:T(8,128)(2,1)S(1)}, bf16[1024,256]{1,0:T(8,128)(2,1)S(1)}, u32[]{:S(2)}, u32[]{:S(2)}) collective-permute-start(bf16[1024,256]{1,0:T(8,128)(2,1)S(1)} %pad_maximum_fusion.own), channel_id=1, source_target_pairs={{0,16},{8,24},{16,0},{24,8},{1,17},{9,25},{17,1},{25,9},{2,18},{10... | collective-permute-start | bytes 1572872 | tf_op jit(solution)/shard_map/ppermute | solution.py:402
  34.6 15.4 %collective-permute-start.5 = (bf16[1024,256]{1,0:T(8,128)(2,1)S(1)}, bf16[1024,256]{1,0:T(8,128)(2,1)S(1)}, u32[]{:S(2)}, u32[]{:S(2)}) collective-permute-start(bf16[1024,256]{1,0:T(8,128)(2,1)S(1)} %pad_maximum_fusion.own), channel_id=1, source_target_pairs={{0,8},{8,0},{16,24},{24,16},{1,9},{9,1},{17,25},{25,17},{2,10},{10... | collective-permute-start | bytes 1572872 | tf_op jit(solution)/shard_map/ppermute | solution.py:402
  36.1 11.2 %collective-permute-start.19 = (bf16[256,256]{1,0:T(8,128)(2,1)}, bf16[256,256]{1,0:T(8,128)(2,1)S(1)}, u32[]{:S(2)}, u32[]{:S(2)}) collective-permute-start(bf16[256,256]{1,0:T(8,128)(2,1)} %get-tuple-element.71), channel_id=1, source_target_pairs={{0,4},{1,5},{2,6},{3,7},{4,0},{5,1},{6,2},{7,3},{8,12},{9,13},{10,... | collective-permute-start | bytes 393224 | tf_op jit(solution)/shard_map/ppermute | solution.py:402
  37.1 10.2 %collective-permute-start.20 = (bf16[256,256]{1,0:T(8,128)(2,1)}, bf16[256,256]{1,0:T(8,128)(2,1)S(1)}, u32[]{:S(2)}, u32[]{:S(2)}) collective-permute-start(bf16[256,256]{1,0:T(8,128)(2,1)} %get-tuple-element.72), channel_id=1, source_target_pairs={{0,6},{1,7},{2,4},{3,5},{4,2},{5,3},{6,0},{7,1},{8,14},{9,15},{10,... | collective-permute-start | bytes 393224 | tf_op jit(solution)/shard_map/ppermute | solution.py:402
  47.4 14.9 %collective-permute-start.22 = (bf16[1024,256]{1,0:T(8,128)(2,1)S(1)}, bf16[1024,256]{1,0:T(8,128)(2,1)S(1)}, u32[]{:S(2)}, u32[]{:S(2)}) collective-permute-start(bf16[1024,256]{1,0:T(8,128)(2,1)S(1)} %constant_dynamic-update-slice_fusion.own), channel_id=1, source_target_pairs={{0,16},{8,24},{16,0},{24,8},{1,17},{9,25},{17,1},{25,9},{2,18},{10... | collective-permute-start | bytes 1572872 | tf_op jit(solution)/shard_map/ppermute | solution.py:402
  47.9 15.0 %collective-permute-start.21 = (bf16[1024,256]{1,0:T(8,128)(2,1)S(1)}, bf16[1024,256]{1,0:T(8,128)(2,1)S(1)}, u32[]{:S(2)}, u32[]{:S(2)}) collective-permute-start(bf16[1024,256]{1,0:T(8,128)(2,1)S(1)} %constant_dynamic-update-slice_fusion.own), channel_id=1, source_target_pairs={{0,8},{8,0},{16,24},{24,16},{1,9},{9,1},{17,25},{25,17},{2,10},{10... | collective-permute-start | bytes 1572872 | tf_op jit(solution)/shard_map/ppermute | solution.py:402
  48.5 19.8 %collective-permute-start.8 = (bf16[512,256]{1,0:T(8,128)(2,1)S(1)}, bf16[512,256]{1,0:T(8,128)(2,1)S(1)}, u32[]{:S(2)}, u32[]{:S(2)}) collective-permute-start(bf16[512,256]{1,0:T(8,128)(2,1)S(1)} %slice.41), channel_id=1, source_target_pairs={{0,8},{8,0},{16,24},{24,16},{1,9},{9,1},{17,25},{25,17},{2,10},{10... | collective-permute-start | bytes 786440 | tf_op jit(solution)/shard_map/ppermute | solution.py:402
  50.1 18.3 %collective-permute-start.7 = (bf16[512,256]{1,0:T(8,128)(2,1)S(1)}, bf16[512,256]{1,0:T(8,128)(2,1)S(1)}, u32[]{:S(2)}, u32[]{:S(2)}) collective-permute-start(bf16[512,256]{1,0:T(8,128)(2,1)S(1)} %slice.40), channel_id=1, source_target_pairs={{0,16},{8,24},{16,0},{24,8},{1,17},{9,25},{17,1},{25,9},{2,18},{10... | collective-permute-start | bytes 786440 | tf_op jit(solution)/shard_map/ppermute | solution.py:402
  62.3 23.6 %collective-permute-start.24 = (bf16[512,256]{1,0:T(8,128)(2,1)S(1)}, bf16[512,256]{1,0:T(8,128)(2,1)S(1)}, u32[]{:S(2)}, u32[]{:S(2)}) collective-permute-start(bf16[512,256]{1,0:T(8,128)(2,1)S(1)} %slice.44), channel_id=1, source_target_pairs={{0,8},{8,0},{16,24},{24,16},{1,9},{9,1},{17,25},{25,17},{2,10},{10... | collective-permute-start | bytes 786440 | tf_op jit(solution)/shard_map/ppermute | solution.py:402
  62.9 22.9 %collective-permute-start.23 = (bf16[512,256]{1,0:T(8,128)(2,1)S(1)}, bf16[512,256]{1,0:T(8,128)(2,1)S(1)}, u32[]{:S(2)}, u32[]{:S(2)}) collective-permute-start(bf16[512,256]{1,0:T(8,128)(2,1)S(1)} %slice.43), channel_id=1, source_target_pairs={{0,16},{8,24},{16,0},{24,8},{1,17},{9,25},{17,1},{25,9},{2,18},{10... | collective-permute-start | bytes 786440 | tf_op jit(solution)/shard_map/ppermute | solution.py:402
  83.7 23.4 %collective-permute-start.9 = (bf16[512,512]{1,0:T(8,128)(2,1)}, bf16[512,512]{1,0:T(8,128)(2,1)S(1)}, u32[]{:S(2)}, u32[]{:S(2)}) collective-permute-start(bf16[512,512]{1,0:T(8,128)(2,1)} %get-tuple-element.56), channel_id=1, source_target_pairs={{0,8},{8,0},{16,24},{24,16},{1,9},{9,1},{17,25},{25,17},{2,10},{10... | collective-permute-start | bytes 1572872 | tf_op jit(solution)/shard_map/ppermute | solution.py:402
  84.3 22.8 %collective-permute-start.10 = (bf16[512,512]{1,0:T(8,128)(2,1)}, bf16[512,512]{1,0:T(8,128)(2,1)S(1)}, u32[]{:S(2)}, u32[]{:S(2)}) collective-permute-start(bf16[512,512]{1,0:T(8,128)(2,1)} %get-tuple-element.58), channel_id=1, source_target_pairs={{0,16},{8,24},{16,0},{24,8},{1,17},{9,25},{17,1},{25,9},{2,18},{10... | collective-permute-start | bytes 1572872 | tf_op jit(solution)/shard_map/ppermute | solution.py:402
  105.0 25.8 %collective-permute-start.25 = (bf16[512,512]{1,0:T(8,128)(2,1)}, bf16[512,512]{1,0:T(8,128)(2,1)S(1)}, u32[]{:S(2)}, u32[]{:S(2)}) collective-permute-start(bf16[512,512]{1,0:T(8,128)(2,1)} %get-tuple-element.76), channel_id=1, source_target_pairs={{0,8},{8,0},{16,24},{24,16},{1,9},{9,1},{17,25},{25,17},{2,10},{10... | collective-permute-start | bytes 1572872 | tf_op jit(solution)/shard_map/ppermute | solution.py:402
  106.6 24.3 %collective-permute-start.26 = (bf16[512,512]{1,0:T(8,128)(2,1)}, bf16[512,512]{1,0:T(8,128)(2,1)S(1)}, u32[]{:S(2)}, u32[]{:S(2)}) collective-permute-start(bf16[512,512]{1,0:T(8,128)(2,1)} %get-tuple-element.78), channel_id=1, source_target_pairs={{0,16},{8,24},{16,0},{24,8},{1,17},{9,25},{17,1},{25,9},{2,18},{10... | collective-permute-start | bytes 1572872 | tf_op jit(solution)/shard_map/ppermute | solution.py:402
  110.8 9.0 %collective-permute-start.11 = (bf16[512,256]{1,0:T(8,128)(2,1)}, bf16[512,256]{1,0:T(8,128)(2,1)S(1)}, u32[]{:S(2)}, u32[]{:S(2)}) collective-permute-start(bf16[512,256]{1,0:T(8,128)(2,1)} %get-tuple-element.60), channel_id=1, source_target_pairs={{0,16},{8,24},{16,0},{24,8},{1,17},{9,25},{17,1},{25,9},{2,18},{10... | collective-permute-start | bytes 786440 | tf_op jit(solution)/shard_map/ppermute | solution.py:402
  112.3 7.5 %collective-permute-start.12 = (bf16[512,256]{1,0:T(8,128)(2,1)}, bf16[512,256]{1,0:T(8,128)(2,1)S(1)}, u32[]{:S(2)}, u32[]{:S(2)}) collective-permute-start(bf16[512,256]{1,0:T(8,128)(2,1)} %get-tuple-element.61), channel_id=1, source_target_pairs={{0,8},{8,0},{16,24},{24,16},{1,9},{9,1},{17,25},{25,17},{2,10},{10... | collective-permute-start | bytes 786440 | tf_op jit(solution)/shard_map/ppermute | solution.py:402
  122.8 12.8 %collective-permute-start.13 = (bf16[256,256]{1,0:T(8,128)(2,1)}, bf16[256,256]{1,0:T(8,128)(2,1)S(1)}, u32[]{:S(2)}, u32[]{:S(2)}) collective-permute-start(bf16[256,256]{1,0:T(8,128)(2,1)} %get-tuple-element.63), channel_id=1, source_target_pairs={{0,2},{1,3},{2,0},{3,1},{4,6},{5,7},{6,4},{7,5},{8,10},{9,11},{10,... | collective-permute-start | bytes 393224 | tf_op jit(solution)/shard_map/ppermute | solution.py:402
  127.0 10.3 %collective-permute-start.14 = (bf16[256,256]{1,0:T(8,128)(2,1)}, bf16[256,256]{1,0:T(8,128)(2,1)S(1)}, u32[]{:S(2)}, u32[]{:S(2)}) collective-permute-start(bf16[256,256]{1,0:T(8,128)(2,1)} %get-tuple-element.64), channel_id=1, source_target_pairs={{0,4},{1,5},{2,6},{3,7},{4,0},{5,1},{6,2},{7,3},{8,12},{9,13},{10,... | collective-permute-start | bytes 393224 | tf_op jit(solution)/shard_map/ppermute | solution.py:402
  129.4 7.9 %collective-permute-start.15 = (bf16[256,256]{1,0:T(8,128)(2,1)}, bf16[256,256]{1,0:T(8,128)(2,1)S(1)}, u32[]{:S(2)}, u32[]{:S(2)}) collective-permute-start(bf16[256,256]{1,0:T(8,128)(2,1)} %get-tuple-element.65), channel_id=1, source_target_pairs={{0,6},{1,7},{2,4},{3,5},{4,2},{5,3},{6,0},{7,1},{8,14},{9,15},{10,... | collective-permute-start | bytes 393224 | tf_op jit(solution)/shard_map/ppermute | solution.py:402
  134.6 6.6 %collective-permute-start.27 = (bf16[512,256]{1,0:T(8,128)(2,1)}, bf16[512,256]{1,0:T(8,128)(2,1)S(1)}, u32[]{:S(2)}, u32[]{:S(2)}) collective-permute-start(bf16[512,256]{1,0:T(8,128)(2,1)} %get-tuple-element.80), channel_id=1, source_target_pairs={{0,16},{8,24},{16,0},{24,8},{1,17},{9,25},{17,1},{25,9},{2,18},{10... | collective-permute-start | bytes 786440 | tf_op jit(solution)/shard_map/ppermute | solution.py:402
  135.1 6.6 %collective-permute-start.28 = (bf16[512,256]{1,0:T(8,128)(2,1)}, bf16[512,256]{1,0:T(8,128)(2,1)S(1)}, u32[]{:S(2)}, u32[]{:S(2)}) collective-permute-start(bf16[512,256]{1,0:T(8,128)(2,1)} %get-tuple-element.81), channel_id=1, source_target_pairs={{0,8},{8,0},{16,24},{24,16},{1,9},{9,1},{17,25},{25,17},{2,10},{10... | collective-permute-start | bytes 786440 | tf_op jit(solution)/shard_map/ppermute | solution.py:402
  141.1 21.1 %collective-permute-start.17 = (f32[256,384]{1,0:T(8,128)}, f32[256,384]{1,0:T(8,128)S(1)}, u32[]{:S(2)}, u32[]{:S(2)}) collective-permute-start(f32[256,384]{1,0:T(8,128)} %get-tuple-element.68), channel_id=1, source_target_pairs={{0,1},{1,0},{2,3},{3,2},{4,5},{5,4},{6,7},{7,6},{8,9},{9,8},{10,11... | collective-permute-start | bytes 1179656 | tf_op jit(solution)/shard_map/ppermute | solution.py:402
  144.5 8.0 %collective-permute-start.29 = (bf16[256,256]{1,0:T(8,128)(2,1)}, bf16[256,256]{1,0:T(8,128)(2,1)S(1)}, u32[]{:S(2)}, u32[]{:S(2)}) collective-permute-start(bf16[256,256]{1,0:T(8,128)(2,1)} %get-tuple-element.83), channel_id=1, source_target_pairs={{0,2},{1,3},{2,0},{3,1},{4,6},{5,7},{6,4},{7,5},{8,10},{9,11},{10,... | collective-permute-start | bytes 393224 | tf_op jit(solution)/shard_map/ppermute | solution.py:402
  146.0 13.1 %collective-permute-start.30 = (bf16[256,256]{1,0:T(8,128)(2,1)}, bf16[256,256]{1,0:T(8,128)(2,1)S(1)}, u32[]{:S(2)}, u32[]{:S(2)}) collective-permute-start(bf16[256,256]{1,0:T(8,128)(2,1)} %get-tuple-element.84), channel_id=1, source_target_pairs={{0,4},{1,5},{2,6},{3,7},{4,0},{5,1},{6,2},{7,3},{8,12},{9,13},{10,... | collective-permute-start | bytes 393224 | tf_op jit(solution)/shard_map/ppermute | solution.py:402
  147.5 11.6 %collective-permute-start.31 = (bf16[256,256]{1,0:T(8,128)(2,1)}, bf16[256,256]{1,0:T(8,128)(2,1)S(1)}, u32[]{:S(2)}, u32[]{:S(2)}) collective-permute-start(bf16[256,256]{1,0:T(8,128)(2,1)} %get-tuple-element.85), channel_id=1, source_target_pairs={{0,6},{1,7},{2,4},{3,5},{4,2},{5,3},{6,0},{7,1},{8,14},{9,15},{10,... | collective-permute-start | bytes 393224 | tf_op jit(solution)/shard_map/ppermute | solution.py:402
  162.2 13.6 %collective-permute-start.32 = (f32[256,256]{1,0:T(8,128)}, f32[256,256]{1,0:T(8,128)S(1)}, u32[]{:S(2)}, u32[]{:S(2)}) collective-permute-start(f32[256,256]{1,0:T(8,128)} %get-tuple-element.87), channel_id=1, source_target_pairs={{0,1},{1,0},{2,3},{3,2},{4,5},{5,4},{6,7},{7,6},{8,9},{9,8},{10,11... | collective-permute-start | bytes 786440 | tf_op jit(solution)/shard_map/ppermute | solution.py:402
  162.2 12.7 %collective-permute-start.33 = (f32[2,256]{0,1:T(8,128)S(1)}, f32[2,256]{0,1:T(8,128)S(1)}, u32[]{:S(2)}, u32[]{:S(2)}) collective-permute-start(f32[2,256]{0,1:T(8,128)S(1)} %slice_bitcast_fusion), channel_id=1, source_target_pairs={{0,8},{8,0},{16,24},{24,16},{1,9},{9,1},{17,25},{25,17},{2,10},{10... | collective-permute-start | bytes 6152 | tf_op jit(solution)/shard_map/ppermute | solution.py:402
  174.9 5.7 %collective-permute-start.34 = (f32[2,256]{0,1:T(8,128)S(1)}, f32[2,256]{0,1:T(8,128)S(1)}, u32[]{:S(2)}, u32[]{:S(2)}) collective-permute-start(f32[2,256]{0,1:T(8,128)S(1)} %fusion), channel_id=1, source_target_pairs={{0,16},{8,24},{16,0},{24,8},{1,17},{9,25},{17,1},{25,9},{2,18},{10... | collective-permute-start | bytes 6152 | tf_op jit(solution)/shard_map/ppermute | solution.py:402
  (36 other events, 232.6 us)

commit v2 on v0

--- a/solution.py
+++ b/solution.py
@@ -1,6 +1,10 @@
+import functools
+
 import jax
 import jax.numpy as jnp
 from jax import lax
+from jax.experimental import pallas as pl
+from jax.experimental.pallas import tpu as pltpu
 from jax.sharding import PartitionSpec as P
 
 HOT = 4
@@ -111,9 +115,533 @@
     return (mixed, grad_tokens, grad_probs, grad_gate[None], grad_up[None], grad_down[None])
 
 
+F32 = jnp.float32
+BF16 = jnp.bfloat16
+I32 = jnp.int32
+CHIPS = 4
+VMEM_BYTES = 24 * 1024 * 1024
+
+
+def dot(a, b, dims=((1,), (0,))):
+    return lax.dot_general(a, b, (dims, ((), ())), preferred_element_type=F32)
+
+
+def params(**kw):
+    return pltpu.CompilerParams(vmem_limit_bytes=VMEM_BYTES, **kw)
+
+
+def vmem():
+    return pl.BlockSpec(memory_space=pltpu.VMEM)
+
+
+def smem():
+    return pl.BlockSpec(memory_space=pltpu.SMEM)
+
+
+def place_rows(ids, own, par, per):
+    z, c = ids[0], ids[1]
+    toks = own.shape[1]
+    row = lax.broadcasted_iota(I32, (2 * CHIPS, toks), 0)
+    expert = 2 * (z ^ (row % CHIPS)) + c
+    first = row < CHIPS
+    named = [
+        jnp.where(first, own[k : k + 1, :], par[k : k + 1, :]).astype(I32) == expert
+        for k in range(2)
+    ]
+    either = jnp.logical_or(named[0], named[1])
+    before = lax.broadcasted_iota(I32, (toks, toks), 0) < lax.broadcasted_iota(
+        I32, (toks, toks), 1
+    )
+    rank = dot(either.astype(F32).astype(BF16), before.astype(F32).astype(BF16)).astype(I32)
+    return row, expert, named, either, rank
+
+
+def pick(rank, either, i, per):
+    at = jnp.where(either[i : i + 1, :], rank[i : i + 1, :], -1)
+    slots = lax.broadcasted_iota(I32, (per, at.shape[1]), 0)
+    return (slots == at).astype(F32)
+
+
+def thirds(line):
+    high = line.astype(BF16).astype(F32)
+    middle = (line - high).astype(BF16).astype(F32)
+    return high, middle, line - high - middle
+
+
+def send_kernel(per, ids, own_x, own_g, own_m, par_m, par_x, par_g, x0, x1, x2, x3, g0, g1, g2, g3):
+    own, par = own_m[...], par_m[...]
+    toks = own.shape[1]
+    _, _, _, either, rank = place_rows(ids, own, par, per)
+    tail = lax.broadcasted_iota(I32, (16, toks), 0)
+    lines = [own[0:1, :], own[1:2, :], par[0:1, :], par[1:2, :]]
+    for table in (own, par):
+        for k in range(2):
+            lines += thirds(table[2 + k : 3 + k, :])
+    extra = jnp.zeros((16, toks), F32)
+    for i, line in enumerate(lines):
+        extra = jnp.where(tail == i, line, extra)
+    for q in range(CHIPS):
+        for src in range(2):
+            hot = pick(rank, either, CHIPS * src + q, per).astype(BF16)
+            place = slice(src * per, (src + 1) * per)
+            (x0, x1, x2, x3)[q][place, :] = dot(hot, (own_x, par_x)[src][...]).astype(BF16)
+            (g0, g1, g2, g3)[q][place, :] = dot(hot, (own_g, par_g)[src][...]).astype(BF16)
+        if q:
+            (x0, x1, x2, x3)[q][2 * per : 2 * per + 16, :] = extra.astype(BF16)
+
+
+def room_of(e, cap, plan, extra_slots):
+    room = cap[e]
+    for h in range(HOT):
+        room = room + jnp.where(plan[h] == e, extra_slots, 0)
+    return room
+
+
+def place_kernel(per, extra_slots, ids, cap, plan, own_m, par_m, e1, e2, e3, info, scale):
+    own, par = own_m[...], par_m[...]
+    toks = own.shape[1]
+    z, c = ids[0], ids[1]
+    row, expert, named, either, rank = place_rows(ids, own, par, per)
+    q_col = row[:, 0:1] % CHIPS
+    first = row < CHIPS
+    first_col = first[:, 0:1]
+
+    sources = []
+    for s, table in enumerate((own, par)):
+        sources.append((0, s, [table[k : k + 1, :] for k in range(4)]))
+    for p, ref in ((1, e1), (2, e2), (3, e3)):
+        table = ref[2 * per : 2 * per + 16, :].astype(F32)
+        for s in range(2):
+            lines = [table[2 * s + k : 2 * s + k + 1, :] for k in range(2)]
+            for k in range(2):
+                at = 4 + 3 * (2 * s + k)
+                lines.append(
+                    table[at : at + 1, :] + table[at + 1 : at + 2, :] + table[at + 2 : at + 3, :]
+                )
+            sources.append((p, s, lines))
+
+    limit = jnp.zeros((2 * CHIPS, 1), I32)
+    for q in range(CHIPS):
+        limit = jnp.where(q_col == q, room_of(2 * (z ^ q) + c, cap, plan, extra_slots), limit)
+    earlier = jnp.zeros((2 * CHIPS, 1), F32)
+    for p, s, lines in sources:
+        hits = jnp.logical_or(lines[0].astype(I32) == expert, lines[1].astype(I32) == expert)
+        count = jnp.sum(hits.astype(F32), axis=1, keepdims=True)
+        block = 2 * (z ^ p) + (c ^ s)
+        ahead = jnp.where(
+            first_col,
+            (block < 2 * z + c).astype(F32),
+            (block < 2 * z + (c ^ 1)).astype(F32),
+        )
+        earlier = earlier + count * ahead
+    keep = jnp.where(rank + earlier.astype(I32) < limit, 1.0, 0.0)
+    kinds = []
+    for k in range(2):
+        prob = jnp.where(first, own[2 + k : 3 + k, :], par[2 + k : 3 + k, :])
+        mine = named[k].astype(F32)
+        slot = (row % CHIPS * per + rank + 1).astype(F32)
+        kinds.append((mine * slot, mine * keep * prob, mine * keep))
+    at = lax.broadcasted_iota(I32, (128, toks), 0)
+    table = jnp.zeros((128, toks), F32)
+    for kind in range(3):
+        for src in range(2):
+            half = first if src == 0 else jnp.logical_not(first)
+            for k in range(2):
+                line = jnp.sum(jnp.where(half, kinds[k][kind], 0.0), axis=0, keepdims=True)
+                table = jnp.where(at == 4 * kind + 2 * src + k, line, table)
+    info[...] = jnp.transpose(table)
+
+    stacked = [jnp.zeros((2 * CHIPS, toks), F32) for _ in range(4)]
+    blocks = jnp.zeros((2 * CHIPS, 1), I32)
+    for p, s, lines in sources:
+        i = 2 * p + s
+        stacked = [jnp.where(row == i, line, old) for line, old in zip(lines, stacked)]
+        blocks = jnp.where(row[:, 0:1] == i, 2 * (z ^ p) + (c ^ s), blocks)
+    mine = 2 * z + c
+    named = [stacked[k].astype(I32) == mine for k in range(2)]
+    either = jnp.logical_or(named[0], named[1])
+    before = lax.broadcasted_iota(I32, (toks, toks), 0) < lax.broadcasted_iota(
+        I32, (toks, toks), 1
+    )
+    hits = either.astype(F32)
+    rank = dot(hits.astype(BF16), before.astype(F32).astype(BF16)).astype(I32)
+    count = jnp.sum(hits, axis=1, keepdims=True)
+    earlier = jnp.zeros((2 * CHIPS, 1), F32)
+    for p, s, _ in sources:
+        i = 2 * p + s
+        ahead = (2 * (z ^ p) + (c ^ s) < blocks).astype(F32)
+        earlier = earlier + ahead * count[i : i + 1, :]
+    keep = rank + earlier.astype(I32) < room_of(mine, cap, plan, extra_slots)
+    weight = jnp.where(keep, 1.0, 0.0) * (
+        named[0].astype(F32) * stacked[2] + named[1].astype(F32) * stacked[3]
+    )
+    for i in range(2 * CHIPS):
+        hot = pick(rank, either, i, per)
+        value = jnp.sum(hot * weight[i : i + 1, :], axis=1, keepdims=True)
+        scale[i * per : (i + 1) * per, :] = jnp.broadcast_to(value, (per, 128))
+
+
+def load_kernel(a, b, c, x, y, z, sems):
+    copies = [
+        pltpu.make_async_copy(src, dst, sems.at[i])
+        for i, (src, dst) in enumerate(((a, x), (b, y), (c, z)))
+    ]
+    for copy in copies:
+        copy.start()
+    for copy in copies:
+        copy.wait()
+
+
+def combine(per, src, k, rows, info):
+    slot = info[:, 2 * src + k : 2 * src + k + 1].astype(I32) - 1
+    slots = lax.broadcasted_iota(I32, (info.shape[0], CHIPS * per), 1)
+    return dot((slots == slot).astype(F32).astype(BF16), rows)
+
+
+def back_kernel(per, with_dots, y0, y1, y2, y3, info_ref, *refs):
+    if with_dots:
+        own_g, par_g, kept, sent = refs
+    else:
+        kept, sent = refs
+    info = info_ref[...]
+    feats = y0.shape[1]
+    toks = info.shape[0]
+    lane = lax.broadcasted_iota(I32, (toks, 128), 1)
+    for src, out in enumerate((kept, sent)):
+        rows = jnp.concatenate([y[src * per : (src + 1) * per, :] for y in (y0, y1, y2, y3)], axis=0)
+        total = jnp.zeros((toks, feats), F32)
+        dots = jnp.zeros((toks, 128), F32)
+        for k in range(2):
+            picked = combine(per, src, k, rows, info)
+            at = 2 * src + k
+            total = total + info[:, 4 + at : 5 + at] * picked
+            if with_dots:
+                grad = (own_g, par_g)[src][...].astype(F32)
+                inner = jnp.sum(grad * picked, axis=1, keepdims=True) * info[:, 8 + at : 9 + at]
+                dots = jnp.where(lane == k, inner, dots)
+        out[:, 0:feats] = total
+        if with_dots:
+            out[:, feats : feats + 128] = dots
+
+
+def assemble(r, at, shards, cat):
+    own, a, b, c, d = shards
+    rows, feats = own.shape
+    half = rows // 2
+
+    def cols(k):
+        return pl.ds(pl.multiple_of((r ^ k) * feats, feats), feats)
+
+    cat[at : at + rows, cols(0)] = own[...]
+    cat[at : at + rows, cols(1)] = a[...]
+    cat[at : at + rows, cols(2)] = b[...]
+    cat[at : at + half, cols(3)] = c[...]
+    cat[at + half : at + rows, cols(3)] = d[...]
+
+
+def split_out(part, groups):
+    _, (send, *_) = groups[0]
+    feats = send.shape[1] // 2
+    low, high = slice(0, feats), slice(feats, 2 * feats)
+    for k in (3, 1, 2, 0):
+        piece = part(k).astype(BF16)
+        for at, (send_a, keep_a, send_b, keep_b) in groups:
+            half = send_a.shape[0]
+            top = ((keep_a, low), (send_a, low), (keep_a, high), (send_a, high))[k]
+            bottom = ((keep_b, low), (keep_b, high), (send_b, low), (send_b, high))[k]
+            top[0][:, top[1]] = piece[at : at + half, :]
+            bottom[0][:, bottom[1]] = piece[at + half : at + 2 * half, :]
+
+
+def forward_kernel(ids, *refs):
+    near, far, (wg, wu, cat, hid, act, slope) = refs[:5], refs[5:10], refs[10:]
+    r = ids[2]
+    assemble(r, 0, near, cat)
+    assemble(r, near[0].shape[0], far, cat)
+    step = 256
+    for j in range(0, hid.shape[1], step):
+        cols = slice(j, j + step)
+        gate = dot(cat[...], wg[:, cols])
+        up = dot(cat[...], wu[:, cols])
+        sig = jax.nn.sigmoid(gate)
+        silu = gate * sig
+        hid[:, cols] = (silu * up).astype(BF16)
+        act[:, cols] = silu.astype(BF16)
+        slope[:, cols] = (up * (sig + silu * (1.0 - sig))).astype(BF16)
+
+
+def out_kernel(ids, hid, wd, sa, ka, sb, kb):
+    r = ids[2]
+    feats = sa.shape[1] // 2
+
+    def part(k):
+        return dot(hid[...], wd[:, pl.ds(pl.multiple_of((r ^ k) * feats, feats), feats)])
+
+    split_out(part, [(0, (sa, ka, sb, kb))])
+
+
+def backward_kernel(ids, own, a, b, c, d, wg, wu, wd, act, slope, cat, dgate, dup, *outs):
+    r = ids[2]
+    assemble(r, 0, (own, a, b, c, d), cat)
+    step = 256
+    for j in range(0, dgate.shape[1], step):
+        cols = slice(j, j + step)
+        dh = dot(cat[...], wd[cols, :], ((1,), (1,)))
+        dgate[:, cols] = (dh * slope[:, cols].astype(F32)).astype(BF16)
+        dup[:, cols] = (dh * act[:, cols].astype(F32)).astype(BF16)
+
+    def part(k):
+        feats = own.shape[1]
+        line = pl.ds(pl.multiple_of((r ^ k) * feats, feats), feats)
+        return dot(dgate[...], wg[line, :], ((1,), (1,))) + dot(dup[...], wu[line, :], ((1,), (1,)))
+
+    split_out(part, [(cat.shape[0] // 2, outs[:4]), (0, outs[4:])])
+
+
+def weights_kernel(xcat, gcat, dgate, dup, hid, ggate, gup, gdown, done):
+    done[...] = jnp.zeros_like(done)
+    size = ggate.shape[0]
+    cols = pl.ds(pl.multiple_of(pl.program_id(0) * size, size), size)
+    x = xcat[:, cols]
+    ggate[...] = dot(x, dgate[...], ((0,), (0,)))
+    gup[...] = dot(x, dup[...], ((0,), (0,)))
+    gdown[...] = dot(hid[:, cols], gcat[...], ((0,), (0,)))
+
+
+def join_kernel(a, b, out):
+    size = out.shape[0] // 2
+    out[0:size, :] = a[0:size, :]
+    out[size : 2 * size, :] = b[0:size, :]
+
+
+def join_scaled_kernel(a, b, c, d, scale, out):
+    size = out.shape[0] // CHIPS
+    for q, ref in enumerate((a, b, c, d)):
+        at = slice(q * size, (q + 1) * size)
+        out[at, :] = (ref[...].astype(F32) * scale[at, 0:1]).astype(BF16)
+
+
+def middle_kernel(ka, ra, kb, rb, sa, sb, kept):
+    half, feats = sa.shape
+    kept[0:half, :] = ka[:, 0:feats].astype(F32) + ra[:, 0:feats].astype(F32)
+    kept[half : 2 * half, :] = kb[:, 0:feats].astype(F32) + rb[:, 0:feats].astype(F32)
+    sa[...] = (ka[:, feats:].astype(F32) + ra[:, feats:].astype(F32)).astype(BF16)
+    sb[...] = (kb[:, feats:].astype(F32) + rb[:, feats:].astype(F32)).astype(BF16)
+
+
+def last_kernel(kept, ra, rb, *outs):
+    half = ra.shape[0]
+    size = outs[0].shape[0]
+    for q, out in enumerate(outs):
+        at = q * size
+        other = ra[at : at + size, :] if at < half else rb[at - half : at - half + size, :]
+        out[...] = (kept[at : at + size, :] + other.astype(F32)).astype(BF16)
+
+
+def shift(x, axis, bit):
+    n = lax.axis_size(axis)
+    return lax.ppermute(x, axis, [(i, i ^ bit) for i in range(n)])
+
+
+def sds(shape, dtype):
+    return jax.ShapeDtypeStruct(shape, dtype)
+
+
+def vm(shape, dtype):
+    return pltpu.VMEM(shape, dtype)
+
+
+def pin(*arrays):
+    return [pltpu.with_memory_space_constraint(x, pltpu.VMEM) for x in arrays]
+
+
+def kernel_call(body, name, outs, *args, plan_args=0, loose=0, flops=0, after=()):
+    count = len(args)
+    pinned = list(args[: plan_args + loose]) + pin(*args[plan_args + loose :], *after)
+
+    def run(*refs):
+        body(*refs[:count], *refs[count + len(after) :])
+
+    return pl.pallas_call(
+        run,
+        in_specs=[smem()] * plan_args + [vmem()] * (count - plan_args + len(after)),
+        out_shape=outs,
+        compiler_params=params(),
+        cost_estimate=pl.CostEstimate(flops=flops, bytes_accessed=1 << 20, transcendentals=0),
+        name=name,
+    )(*pinned)
+
+
+def relay_kernel(a, b, top, bottom):
+    half = top.shape[0]
+    top[...] = a[0:half, :]
+    bottom[...] = b[half : 2 * half, :]
+
+
+def gather_first(x):
+    return x, shift(x, "rep", 1), shift(x, "rep", 2)
+
+
+def gather_second(parts, after):
+    x, a, b = parts
+    half = vm((x.shape[0] // 2, x.shape[1]), BF16)
+    top, bottom = kernel_call(relay_kernel, "relay", (half, half), a, b, after=after)
+    return x, a, b, shift(top, "rep", 2), shift(bottom, "rep", 1)
+
+
+def reduce_first(sa, ka, sb, kb):
+    return ka, shift(sa, "rep", 1), kb, shift(sb, "rep", 2)
+
+
+def reduce_second(parts, after=()):
+    half, feats = parts[0].shape[0], parts[0].shape[1] // 2
+    piece = vm((half, feats), BF16)
+    ma, mb, kept = kernel_call(
+        middle_kernel, "reduce_middle", (piece, piece, vm((2 * half, feats), F32)), *parts, after=after
+    )
+    return kept, shift(ma, "rep", 2), shift(mb, "rep", 1)
+
+
+def reduce_last(parts, size, after=()):
+    rows, feats = parts[0].shape
+    outs = (vm((size, feats), BF16),) * (rows // size)
+    return kernel_call(last_kernel, "reduce_last", outs, *parts, after=after)
+
+
+def over_chips(chunks):
+    return [chunks[q] if q == 0 else shift(chunks[q], "exp", 2 * q) for q in range(CHIPS)]
+
+
+def on_quad(tokens, routes, probs, capacity, plan, grad_out, w_gate, w_up, w_down):
+    toks, feats = tokens.shape
+    per = 4 * toks // capacity.shape[0]
+    wg, wu, wd = w_gate[0], w_up[0], w_down[0]
+    width, ff = wg.shape
+    rows = 2 * per * CHIPS
+    me = lax.axis_index("exp").astype(I32)
+    ids = jnp.stack([me // 2, me % 2, lax.axis_index("rep").astype(I32)])
+    own_m = jnp.concatenate(
+        [routes.T.astype(F32), probs.T, jnp.zeros((4, toks), F32)], axis=0
+    )
+    par_m = shift(own_m, "exp", 1)
+    par_x = shift(tokens, "exp", 1)
+    par_g = shift(grad_out, "exp", 1)
+
+    size = 2 * per
+    near = vm((size, feats), BF16)
+    far = vm((size + 16, feats), BF16)
+    sent = kernel_call(
+        functools.partial(send_kernel, per),
+        "send",
+        (near, far, far, far) + (near,) * 4,
+        ids, tokens, grad_out, own_m, par_m, par_x, par_g,
+        plan_args=1,
+        loose=2,
+    )
+    xr = over_chips(sent[:CHIPS])
+    gr = over_chips(sent[CHIPS:])
+    loaded = vm((width, ff), BF16)
+    wg, wu, wd = pl.pallas_call(
+        load_kernel,
+        in_specs=[pl.BlockSpec(memory_space=pltpu.HBM)] * 3,
+        out_shape=(loaded, loaded, vm((ff, width), BF16)),
+        scratch_shapes=[pltpu.SemaphoreType.DMA((3,))],
+        compiler_params=params(),
+        name="load_weights",
+    )(*[pltpu.with_memory_space_constraint(w, pltpu.HBM) for w in (wg, wu, wd)])
+    pair_rows = vm((2 * size, feats), BF16)
+    xa = gather_first(kernel_call(join_kernel, "join_near", pair_rows, xr[0], xr[1]))
+    xb = gather_first(kernel_call(join_kernel, "join_far", pair_rows, xr[2], xr[3], after=(wg,)))
+    info, scale = kernel_call(
+        functools.partial(place_kernel, per, 2 * toks),
+        "place",
+        (vm((toks, 128), F32), vm((rows, 128), F32)),
+        ids, capacity, plan, own_m, par_m, *xr[1:],
+        plan_args=3,
+    )
+    xa = gather_second(xa, (info, xb[0]))
+    xb = gather_second(xb, gr[1:])
+    gs = gather_first(
+        kernel_call(join_scaled_kernel, "join_grads", vm((rows, feats), BF16), *gr, scale)
+    )
+
+    pair_t = vm((rows // 2, 2 * feats), BF16)
+    inner = vm((rows, ff), BF16)
+    wide = vm((rows, width), BF16)
+    work = 2 * rows * width * ff
+    xcat, hid, act, slope = kernel_call(
+        forward_kernel,
+        "forward",
+        (wide, inner, inner, inner),
+        ids, *xa, *xb, wg, wu,
+        plan_args=1,
+        flops=2 * work,
+        after=gs[:1],
+    )
+    gs = gather_second(gs, (hid,))
+    out_parts = kernel_call(
+        out_kernel, "out_parts", (pair_t,) * 4, ids, hid, wd, plan_args=1, flops=work, after=gs[3:]
+    )
+    out_sums = reduce_second(reduce_first(*out_parts))
+
+    gcat, dgate, dup, *dx_parts = kernel_call(
+        backward_kernel,
+        "backward",
+        (wide, inner, inner) + (vm((size, 2 * feats), BF16),) * 8,
+        ids, *gs, wg, wu, wd, act, slope,
+        plan_args=1,
+        flops=3 * work,
+        after=out_parts[:1],
+    )
+    far_first = reduce_first(*dx_parts[:4])
+    near_first = reduce_first(*dx_parts[4:])
+
+    steps = 4
+    grad_gate, grad_up, grad_down, done = pl.pallas_call(
+        weights_kernel,
+        grid=(steps,),
+        in_specs=[vmem()] * 5,
+        out_specs=[pl.BlockSpec((n // steps, m), lambda i: (i, 0)) for n, m in ((width, ff), (width, ff), (ff, width))] + [vmem()],
+        out_shape=(sds((width, ff), F32), sds((width, ff), F32), sds((ff, width), F32), vm((8, 128), F32)),
+        compiler_params=params(),
+        cost_estimate=pl.CostEstimate(flops=3 * work, bytes_accessed=12 << 20, transcendentals=0),
+        name="weight_grads",
+    )(*pin(xcat, gcat, dgate, dup, hid))
+
+    far_sums = reduce_second(far_first, (done, out_sums[0]))
+    near_sums = reduce_second(near_first, (far_sums[0],))
+    yr = over_chips(reduce_last(out_sums, size, (near_sums[0],)))
+    dx_far = reduce_last(far_sums, size, yr[:1])
+    dx_near = reduce_last(near_sums, size, dx_far[:1])
+    dr = over_chips([*dx_near, *dx_far])
+    broad = vm((toks, feats + 128), F32)
+    kept, sent = kernel_call(
+        functools.partial(back_kernel, per, True),
+        "combine_out",
+        (broad, broad),
+        *yr, info, grad_out, par_g,
+        after=dx_near[:1],
+    )
+    both = kept + shift(sent, "exp", 1)
+    mixed = both[:, :feats].astype(BF16)
+    dots = both[:, feats : feats + 2].T
+    dots = dots + shift(dots, "rep", 1)
+    dots = dots + shift(dots, "rep", 2)
+    grad_probs = dots.T
+
+    flat = vm((toks, feats), F32)
+    kept, sent = kernel_call(
+        functools.partial(back_kernel, per, False), "combine_grad", (flat, flat), *dr, info, after=(dots,)
+    )
+    grad_tokens = (kept + shift(sent, "exp", 1)).astype(BF16)
+    return (mixed, grad_tokens, grad_probs, grad_gate[None], grad_up[None], grad_down[None])
+
+
 def solution(mesh):
+    sizes = dict(mesh.shape)
+    fast = sizes["rep"] == 4 and sizes["exp"] == 8
     return jax.shard_map(
-        on_device,
+        on_quad if fast else on_device,
         mesh=mesh,
         in_specs=(
             P("exp", "rep"),

time: 348 us -> 133 us (0.38)
  waiting for transfers between devices: 147 us -> 45.6 us
  local copies, waits for them, and re-layouts: 69.9 us -> 3.02 us
  blocking collectives: 56.6 us -> 0 us
  matrix products: 44 us -> 0 us
  starting transfers between devices: 9.38 us -> 48 us
  Pallas kernels: 0 us -> 33 us
  between operations: 14.8 us -> 0.96 us
    all_gather x2 -> x0, waiting for transfers between devices: 67.3 us -> none  [dispatch(): return lax.all_gather(narrow, 'rep', axis=1, tiled=True)]
    reduce_scatter x2 -> x0, waiting for transfers between devices: 62.8 us -> none  [the longest x1 35.3 us: on_device(): lax.psum_scatter(partial_value.astype(jnp.bfloat16), 'rep', scatter_dimen...]
    scatter x2 -> x0, local copies, waits for them, and re-layouts: 52.6 us -> none  [fill_rows(): return empty.at[flat, rank].set(picked)]
    ppermute x0 -> x43, starting transfers between devices: none -> 48 us  [shift(): return lax.ppermute(x, axis, [(i, i ^ bit) for i in range(n)])]
    ppermute x0 -> x43, waiting for transfers between devices: none -> 45.6 us  [shift(): return lax.ppermute(x, axis, [(i, i ^ bit) for i in range(n)])]
    dot_general x9 -> x0, matrix products: 44 us -> none  [the longest x1 7.07 us: on_device(): lax.dot_general(dout, wd, (((1,), (1,)), ((), ())), preferred_element_typ...]
    all_to_all x2 -> x0, blocking collectives: 37.1 us -> none  [dispatch(): lax.all_to_all(buffer, 'exp', split_axis=0, concat_axis=0, tiled=True)]
    pallas_call x0 -> x21, Pallas kernels: none -> 33 us  [the longest x19 21.6 us: kernel_call(): pl.pallas_call(run, in_specs=[smem()] * plan_args + [vmem()] * (count - p...]
  transfers between devices with their start and end apart: 6 -> 43, of which waited for: 6 -> 21; matrix products, arithmetic and copies ran while one was open for 6% -> 2% of each run, Pallas kernels for 0% -> 21%
where the time goes in v2:
time: 133 us
  starting transfers between devices  48 us (36%)
  waiting for transfers between devices  45.6 us (34%)
  Pallas kernels  33 us (25%)
  local copies, waits for them, and re-layouts  3.02 us (2%)
  other arithmetic  2.25 us (2%)
    ppermute x43, starting transfers between devices, shift(): return lax.ppermute(x, axis, [(i, i ^ bit) for i in range(n)])  48 us
    ppermute x43, waiting for transfers between devices, shift(): return lax.ppermute(x, axis, [(i, i ^ bit) for i in range(n)])  45.6 us
    pallas_call x19, Pallas kernels, kernel_call(): pl.pallas_call(run, in_specs=[smem()] * plan_args + [vmem()] * (count - p...  21.6 us
    pallas_call x1, Pallas kernels, on_quad(): pl.pallas_call(weights_kernel, grid=(steps,), in_specs=[vmem()] * 5, out_...  8.47 us
    pallas_call x1, Pallas kernels, on_quad(): pl.pallas_call(load_kernel, in_specs=[pl.BlockSpec(memory_space=pltpu.HBM...  2.88 us
  transfers between devices with their start and end apart: 43, of which 21 were waited for; matrix products, arithmetic and copies ran while one was open for 2% of the time, Pallas kernels for 21%

profile of v2, /device:TPU:0, one launch (start us, length us, event | category | flops | bytes accessed | tf_op | source)
XLA Modules:
  0.0 132.8 jit_solution(9310641098112465715)
XLA Ops:
  7.0 3.0 %collective-permute-start.3 = (bf16[272,256]{1,0:T(8,128)(2,1)S(1)}, bf16[272,256]{1,0:T(8,128)(2,1)S(1)}, u32[]{:S(2)}, u32[]{:S(2)}) collective-permute-start(bf16[272,256]{1,0:T(8,128)(2,1)S(1)} %get-tuple-element.70), channel_id=1, source_target_pairs={{0,2},{1,3},{2,0},{3,1},{4,6},{5,7},{6,4},{7,5},{8,10},{9,11},{10,... | collective-permute-start | bytes 417800 | tf_op jit(solution)/shard_map/ppermute | solution.py:443
  9.9 2.6 %collective-permute-start.6 = (bf16[272,256]{1,0:T(8,128)(2,1)S(1)}, bf16[272,256]{1,0:T(8,128)(2,1)S(1)}, u32[]{:S(2)}, u32[]{:S(2)}) collective-permute-start(bf16[272,256]{1,0:T(8,128)(2,1)S(1)} %get-tuple-element.71), channel_id=1, source_target_pairs={{0,4},{1,5},{2,6},{3,7},{4,0},{5,1},{6,2},{7,3},{8,12},{9,13},{10,... | collective-permute-start | bytes 417800 | tf_op jit(solution)/shard_map/ppermute | solution.py:443
  12.5 3.6 %collective-permute-done.3.refs_1_.refs_5_ = bf16[272,256]{1,0:T(8,128)(2,1)S(1)} collective-permute-done((bf16[272,256]{1,0:T(8,128)(2,1)S(1)}, bf16[272,256]{1,0:T(8,128)(2,1)S(1)}, u32[]{:S(2)}, u32[]{:S(2)}) %collective-permute-start.3) | collective-permute-done | bytes 139296 | tf_op jit(solution)/shard_map/ppermute | solution.py:443
  16.1 1.8 %collective-permute-start.5 = (bf16[512,256]{1,0:T(8,128)(2,1)S(1)}, bf16[512,256]{1,0:T(8,128)(2,1)S(1)}, u32[]{:S(2)}, u32[]{:S(2)}) collective-permute-start(bf16[512,256]{1,0:T(8,128)(2,1)S(1)} %join_near.1.refs_1_), channel_id=1, source_target_pairs={{0,16},{8,24},{16,0},{24,8},{1,17},{9,25},{17,1},{25,9},{2,18},{10... | collective-permute-start | bytes 786440 | tf_op jit(solution)/shard_map/ppermute | solution.py:443
  19.4 2.9 %load_weights.1 = (bf16[1024,1024]{1,0:T(8,128)(2,1)S(1)}, bf16[1024,1024]{1,0:T(8,128)(2,1)S(1)}, bf16[1024,1024]{1,0:T(8,128)(2,1)S(1)}) custom-call(bf16[1024,1024]{1,0:T(8,128)(2,1)} %bitcast.18, bf16[1024,1024]{1,0:T(8,128)(2,1)} %bitcast.19, bf16[1024,1024]{1,0:T(8,128)(2,1)} %bitcast.20), custom_call_target="tpu_custom_call" | custom-call | tf_op jit(solution)/shard_map/load_weights/pallas_call | solution.py:544
  23.4 1.6 %collective-permute-start.11 = (bf16[512,256]{1,0:T(8,128)(2,1)S(1)}, bf16[512,256]{1,0:T(8,128)(2,1)S(1)}, u32[]{:S(2)}, u32[]{:S(2)}) collective-permute-start(bf16[512,256]{1,0:T(8,128)(2,1)S(1)} %join_far.1.refs_3_.refs_6_), channel_id=1, source_target_pairs={{0,16},{8,24},{16,0},{24,8},{1,17},{9,25},{17,1},{25,9},{2,18},{10... | collective-permute-start | bytes 786440 | tf_op jit(solution)/shard_map/ppermute | solution.py:443
  25.0 1.5 %collective-permute-start.10 = (bf16[512,256]{1,0:T(8,128)(2,1)S(1)}, bf16[512,256]{1,0:T(8,128)(2,1)S(1)}, u32[]{:S(2)}, u32[]{:S(2)}) collective-permute-start(bf16[512,256]{1,0:T(8,128)(2,1)S(1)} %join_far.1.refs_3_.refs_6_), channel_id=1, source_target_pairs={{0,8},{8,0},{16,24},{24,16},{1,9},{9,1},{17,25},{25,17},{2,10},{10... | collective-permute-start | bytes 786440 | tf_op jit(solution)/shard_map/ppermute | solution.py:443
  26.5 2.5 %collective-permute-start.12 = (bf16[256,256]{1,0:T(8,128)(2,1)S(1)}, bf16[256,256]{1,0:T(8,128)(2,1)S(1)}, u32[]{:S(2)}, u32[]{:S(2)}) collective-permute-start(bf16[256,256]{1,0:T(8,128)(2,1)S(1)} %get-tuple-element.77), channel_id=1, source_target_pairs={{0,2},{1,3},{2,0},{3,1},{4,6},{5,7},{6,4},{7,5},{8,10},{9,11},{10,... | collective-permute-start | bytes 393224 | tf_op jit(solution)/shard_map/ppermute | solution.py:443
  30.0 1.5 %collective-permute-start.14 = (bf16[256,256]{1,0:T(8,128)(2,1)S(1)}, bf16[256,256]{1,0:T(8,128)(2,1)S(1)}, u32[]{:S(2)}, u32[]{:S(2)}) collective-permute-start(bf16[256,256]{1,0:T(8,128)(2,1)S(1)} %get-tuple-element.79), channel_id=1, source_target_pairs={{0,6},{1,7},{2,4},{3,5},{4,2},{5,3},{6,0},{7,1},{8,14},{9,15},{10,... | collective-permute-start | bytes 393224 | tf_op jit(solution)/shard_map/ppermute | solution.py:443
  33.7 6.8 %collective-permute-done.13.refs_3_.refs_2_ = bf16[256,256]{1,0:T(8,128)(2,1)S(1)} collective-permute-done((bf16[256,256]{1,0:T(8,128)(2,1)S(1)}, bf16[256,256]{1,0:T(8,128)(2,1)S(1)}, u32[]{:S(2)}, u32[]{:S(2)}) %collective-permute-start.13) | collective-permute-done | bytes 131104 | tf_op jit(solution)/shard_map/ppermute | solution.py:443
  43.4 1.6 %collective-permute-start.18 = (bf16[1024,256]{1,0:T(8,128)(2,1)S(1)}, bf16[1024,256]{1,0:T(8,128)(2,1)S(1)}, u32[]{:S(2)}, u32[]{:S(2)}) collective-permute-start(bf16[1024,256]{1,0:T(8,128)(2,1)S(1)} %join_grads.1.refs_13_.refs_1_), channel_id=1, source_target_pairs={{0,16},{8,24},{16,0},{24,8},{1,17},{9,25},{17,1},{25,9},{2,18},{10... | collective-permute-start | bytes 1572872 | tf_op jit(solution)/shard_map/ppermute | solution.py:443
  47.4 2.0 %collective-permute-done.16.refs_10_ = bf16[256,256]{1,0:T(8,128)(2,1)S(1)} collective-permute-done((bf16[256,256]{1,0:T(8,128)(2,1)S(1)}, bf16[256,256]{1,0:T(8,128)(2,1)S(1)}, u32[]{:S(2)}, u32[]{:S(2)}) %collective-permute-start.16) | collective-permute-done | bytes 131104 | tf_op jit(solution)/shard_map/ppermute | solution.py:443
  49.4 5.7 %forward.1 = (bf16[1024,1024]{1,0:T(8,128)(2,1)S(1)}, bf16[1024,1024]{1,0:T(8,128)(2,1)S(1)}, bf16[1024,1024]{1,0:T(8,128)(2,1)S(1)}, bf16[1024,1024]{1,0:T(8,128)(2,1)S(1)}) custom-call(s32[3]{0:T(128)S(1)} %pad_add_fusion.refs_0_, bf16[512,256]{1,0:T(8,128)(2,1)S(1)} %join_near.1.refs_1_, bf16[512,256]{1,0:T(8,128)(2,1)S(1)} %collective-permute-done.4.refs_0_.refs_2_, ...), custom_call_target="tpu_custom_call" | custom-call | flops 4294967296 | bytes 1048576 | tf_op jit(solution)/shard_map/forward/pallas_call | solution.py:465
  58.8 4.4 %collective-permute-done.19.refs_3_.refs_4_ = bf16[512,256]{1,0:T(8,128)(2,1)S(1)} collective-permute-done((bf16[512,256]{1,0:T(8,128)(2,1)S(1)}, bf16[512,256]{1,0:T(8,128)(2,1)S(1)}, u32[]{:S(2)}, u32[]{:S(2)}) %collective-permute-start.19) | collective-permute-done | bytes 262176 | tf_op jit(solution)/shard_map/ppermute | solution.py:443
  63.1 1.6 %collective-permute-done.20.refs_4_.refs_5_ = bf16[512,256]{1,0:T(8,128)(2,1)S(1)} collective-permute-done((bf16[512,256]{1,0:T(8,128)(2,1)S(1)}, bf16[512,256]{1,0:T(8,128)(2,1)S(1)}, u32[]{:S(2)}, u32[]{:S(2)}) %collective-permute-start.20) | collective-permute-done | bytes 262176 | tf_op jit(solution)/shard_map/ppermute | solution.py:443
  64.8 2.9 %out_parts.1 = (bf16[512,512]{1,0:T(8,128)(2,1)S(1)}, bf16[512,512]{1,0:T(8,128)(2,1)S(1)}, bf16[512,512]{1,0:T(8,128)(2,1)S(1)}, bf16[512,512]{1,0:T(8,128)(2,1)S(1)}) custom-call(s32[3]{0:T(128)S(1)} %pad_add_fusion.refs_0_, bf16[1024,1024]{1,0:T(8,128)(2,1)S(1)} %get-tuple-element.85.refs_2_.refs_1_.hid, ...), custom_call_target="tpu_custom_call" | custom-call | flops 2147483648 | bytes 1048576 | tf_op jit(solution)/shard_map/out_parts/pallas_call | solution.py:465
  68.3 2.4 %collective-permute-start.21 = (bf16[512,512]{1,0:T(8,128)(2,1)S(1)}, bf16[512,512]{1,0:T(8,128)(2,1)S(1)}, u32[]{:S(2)}, u32[]{:S(2)}) collective-permute-start(bf16[512,512]{1,0:T(8,128)(2,1)S(1)} %get-tuple-element.90.refs_11_), channel_id=1, source_target_pairs={{0,8},{8,0},{16,24},{24,16},{1,9},{9,1},{17,25},{25,17},{2,10},{10... | collective-permute-start | bytes 1572872 | tf_op jit(solution)/shard_map/ppermute | solution.py:443
  70.6 8.2 %backward.1 = (bf16[1024,1024]{1,0:T(8,128)(2,1)S(1)}, bf16[1024,1024]{1,0:T(8,128)(2,1)S(1)}, bf16[1024,1024]{1,0:T(8,128)(2,1)S(1)}, bf16[256,512]{1,0:T(8,128...) custom-call(s32[3]{0:T(128)S(1)} %pad_add_fusion.refs_0_, ...), custom_call_target="tpu_custom_call" | custom-call | flops 6442450944 | bytes 1048576 | tf_op jit(solution)/shard_map/backward/pallas_call | solution.py:465
  79.0 2.0 %collective-permute-start.25 = (bf16[256,512]{1,0:T(8,128)(2,1)S(1)}, bf16[256,512]{1,0:T(8,128)(2,1)S(1)}, u32[]{:S(2)}, u32[]{:S(2)}) collective-permute-start(bf16[256,512]{1,0:T(8,128)(2,1)S(1)} %get-tuple-element.99), channel_id=1, source_target_pairs={{0,8},{8,0},{16,24},{24,16},{1,9},{9,1},{17,25},{25,17},{2,10},{10... | collective-permute-start | bytes 786440 | tf_op jit(solution)/shard_map/ppermute | solution.py:443
  81.1 2.0 %collective-permute-start.28 = (bf16[256,512]{1,0:T(8,128)(2,1)S(1)}, bf16[256,512]{1,0:T(8,128)(2,1)S(1)}, u32[]{:S(2)}, u32[]{:S(2)}) collective-permute-start(bf16[256,512]{1,0:T(8,128)(2,1)S(1)} %get-tuple-element.105), channel_id=1, source_target_pairs={{0,16},{8,24},{16,0},{24,8},{1,17},{9,25},{17,1},{25,9},{2,18},{10... | collective-permute-start | bytes 786440 | tf_op jit(solution)/shard_map/ppermute | solution.py:443
  83.7 4.8 %collective-permute-done.27.refs_1_ = bf16[256,512]{1,0:T(8,128)(2,1)S(1)} collective-permute-done((bf16[256,512]{1,0:T(8,128)(2,1)S(1)}, bf16[256,512]{1,0:T(8,128)(2,1)S(1)}, u32[]{:S(2)}, u32[]{:S(2)}) %collective-permute-start.27) | collective-permute-done | bytes 262176 | tf_op jit(solution)/shard_map/ppermute | solution.py:443
  88.6 2.5 %collective-permute-start.24 = (bf16[512,256]{1,0:T(8,128)(2,1)S(1)}, bf16[512,256]{1,0:T(8,128)(2,1)S(1)}, u32[]{:S(2)}, u32[]{:S(2)}) collective-permute-start(bf16[512,256]{1,0:T(8,128)(2,1)S(1)} %get-tuple-element.95), channel_id=1, source_target_pairs={{0,8},{8,0},{16,24},{24,16},{1,9},{9,1},{17,25},{25,17},{2,10},{10... | collective-permute-start | bytes 786440 | tf_op jit(solution)/shard_map/ppermute | solution.py:443
  91.0 8.5 %weight_grads.1 = (f32[1024,1024]{1,0:T(8,128)}, f32[1024,1024]{1,0:T(8,128)}, f32[1024,1024]{1,0:T(8,128)}, f32[8,128]{1,0:T(8,128)S(1)}) custom-call(bf16[1024,1024]{1,0:T(8,128)(2,1)S(1)} %get-tuple-element.106.xcat, bf16[1024,1024]{1,0:T(8,128)(2,1)S(1)} %get-tuple-element.107.gcat, bf16[1024,1024]{1,0:T(8,128)(2,1)S(1)} %get-tuple-element.108.dgate, ...), custom_call_target="tpu_custom_call" | custom-call | flops 6442450944 | bytes 12582912 | tf_op jit(solution)/shard_map/weight_grads/pallas_call | solution.py:600
  99.9 2.0 %collective-permute-start.32 = (bf16[256,256]{1,0:T(8,128)(2,1)S(1)}, bf16[256,256]{1,0:T(8,128)(2,1)S(1)}, u32[]{:S(2)}, u32[]{:S(2)}) collective-permute-start(bf16[256,256]{1,0:T(8,128)(2,1)S(1)} %get-tuple-element.117), channel_id=1, source_target_pairs={{0,16},{8,24},{16,0},{24,8},{1,17},{9,25},{17,1},{25,9},{2,18},{10... | collective-permute-start | bytes 393224 | tf_op jit(solution)/shard_map/ppermute | solution.py:443
  101.9 2.0 %collective-permute-start.33 = (bf16[256,256]{1,0:T(8,128)(2,1)S(1)}, bf16[256,256]{1,0:T(8,128)(2,1)S(1)}, u32[]{:S(2)}, u32[]{:S(2)}) collective-permute-start(bf16[256,256]{1,0:T(8,128)(2,1)S(1)} %get-tuple-element.118), channel_id=1, source_target_pairs={{0,8},{8,0},{16,24},{24,16},{1,9},{9,1},{17,25},{25,17},{2,10},{10... | collective-permute-start | bytes 393224 | tf_op jit(solution)/shard_map/ppermute | solution.py:443
  104.9 3.6 %collective-permute-start.31 = (bf16[256,256]{1,0:T(8,128)(2,1)S(1)}, bf16[256,256]{1,0:T(8,128)(2,1)S(1)}, u32[]{:S(2)}, u32[]{:S(2)}) collective-permute-start(bf16[256,256]{1,0:T(8,128)(2,1)S(1)} %get-tuple-element.116), channel_id=1, source_target_pairs={{0,6},{1,7},{2,4},{3,5},{4,2},{5,3},{6,0},{7,1},{8,14},{9,15},{10,... | collective-permute-start | bytes 393224 | tf_op jit(solution)/shard_map/ppermute | solution.py:443
  109.1 4.2 %collective-permute-done.30.refs_2_ = bf16[256,256]{1,0:T(8,128)(2,1)S(1)} collective-permute-done((bf16[256,256]{1,0:T(8,128)(2,1)S(1)}, bf16[256,256]{1,0:T(8,128)(2,1)S(1)}, u32[]{:S(2)}, u32[]{:S(2)}) %collective-permute-start.30) | collective-permute-done | bytes 131104 | tf_op jit(solution)/shard_map/ppermute | solution.py:443
  114.8 1.5 %collective-permute-done.36 = f32[256,384]{0,1:T(8,128)S(1)} collective-permute-done((f32[256,384]{0,1:T(8,128)S(1)}, f32[256,384]{0,1:T(8,128)S(1)}, u32[]{:S(2)}, u32[]{:S(2)}) %collective-permute-start.36) | collective-permute-done | bytes 393248 | tf_op jit(solution)/shard_map/ppermute | solution.py:443
  116.5 2.8 %collective-permute-start.38 = (bf16[256,256]{1,0:T(8,128)(2,1)S(1)}, bf16[256,256]{1,0:T(8,128)(2,1)S(1)}, u32[]{:S(2)}, u32[]{:S(2)}) collective-permute-start(bf16[256,256]{1,0:T(8,128)(2,1)S(1)} %get-tuple-element.121.refs_3_), channel_id=1, source_target_pairs={{0,4},{1,5},{2,6},{3,7},{4,0},{5,1},{6,2},{7,3},{8,12},{9,13},{10,... | collective-permute-start | bytes 393224 | tf_op jit(solution)/shard_map/ppermute | solution.py:443
  119.3 1.6 %collective-permute-start.39 = (bf16[256,256]{1,0:T(8,128)(2,1)S(1)}, bf16[256,256]{1,0:T(8,128)(2,1)S(1)}, u32[]{:S(2)}, u32[]{:S(2)}) collective-permute-start(bf16[256,256]{1,0:T(8,128)(2,1)S(1)} %get-tuple-element.126), channel_id=1, source_target_pairs={{0,6},{1,7},{2,4},{3,5},{4,2},{5,3},{6,0},{7,1},{8,14},{9,15},{10,... | collective-permute-start | bytes 393224 | tf_op jit(solution)/shard_map/ppermute | solution.py:443
  121.0 3.6 %collective-permute-done.41 = f32[2,256]{1,0:T(2,128)S(1)} collective-permute-done((f32[2,256]{1,0:T(2,128)S(1)}, f32[2,256]{1,0:T(2,128)S(1)}, u32[]{:S(2)}, u32[]{:S(2)}) %collective-permute-start.41) | collective-permute-done | bytes 2080 | tf_op jit(solution)/shard_map/ppermute | solution.py:443
  124.6 3.5 %collective-permute-done.39.refs_3_ = bf16[256,256]{1,0:T(8,128)(2,1)S(1)} collective-permute-done((bf16[256,256]{1,0:T(8,128)(2,1)S(1)}, bf16[256,256]{1,0:T(8,128)(2,1)S(1)}, u32[]{:S(2)}, u32[]{:S(2)}) %collective-permute-start.39) | collective-permute-done | bytes 131104 | tf_op jit(solution)/shard_map/ppermute | solution.py:443
  (101 shorter events, 30.7 us)
Async XLA Ops:
  7.0 9.1 %collective-permute-start.3 = (bf16[272,256]{1,0:T(8,128)(2,1)S(1)}, bf16[272,256]{1,0:T(8,128)(2,1)S(1)}, u32[]{:S(2)}, u32[]{:S(2)}) collective-permute-start(bf16[272,256]{1,0:T(8,128)(2,1)S(1)} %get-tuple-element.70), channel_id=1, source_target_pairs={{0,2},{1,3},{2,0},{3,1},{4,6},{5,7},{6,4},{7,5},{8,10},{9,11},{10,... | collective-permute-start | bytes 417800 | tf_op jit(solution)/shard_map/ppermute | solution.py:443
  9.9 13.4 %collective-permute-start.6 = (bf16[272,256]{1,0:T(8,128)(2,1)S(1)}, bf16[272,256]{1,0:T(8,128)(2,1)S(1)}, u32[]{:S(2)}, u32[]{:S(2)}) collective-permute-start(bf16[272,256]{1,0:T(8,128)(2,1)S(1)} %get-tuple-element.71), channel_id=1, source_target_pairs={{0,4},{1,5},{2,6},{3,7},{4,0},{5,1},{6,2},{7,3},{8,12},{9,13},{10,... | collective-permute-start | bytes 417800 | tf_op jit(solution)/shard_map/ppermute | solution.py:443
  12.5 10.8 %collective-permute-start.7 = (bf16[272,256]{1,0:T(8,128)(2,1)S(1)}, bf16[272,256]{1,0:T(8,128)(2,1)S(1)}, u32[]{:S(2)}, u32[]{:S(2)}) collective-permute-start(bf16[272,256]{1,0:T(8,128)(2,1)S(1)} %get-tuple-element.72), channel_id=1, source_target_pairs={{0,6},{1,7},{2,4},{3,5},{4,2},{5,3},{6,0},{7,1},{8,14},{9,15},{10,... | collective-permute-start | bytes 417800 | tf_op jit(solution)/shard_map/ppermute | solution.py:443
  16.1 12.9 %collective-permute-start.5 = (bf16[512,256]{1,0:T(8,128)(2,1)S(1)}, bf16[512,256]{1,0:T(8,128)(2,1)S(1)}, u32[]{:S(2)}, u32[]{:S(2)}) collective-permute-start(bf16[512,256]{1,0:T(8,128)(2,1)S(1)} %join_near.1.refs_1_), channel_id=1, source_target_pairs={{0,16},{8,24},{16,0},{24,8},{1,17},{9,25},{17,1},{25,9},{2,18},{10... | collective-permute-start | bytes 786440 | tf_op jit(solution)/shard_map/ppermute | solution.py:443
  17.9 12.1 %collective-permute-start.4 = (bf16[512,256]{1,0:T(8,128)(2,1)S(1)}, bf16[512,256]{1,0:T(8,128)(2,1)S(1)}, u32[]{:S(2)}, u32[]{:S(2)}) collective-permute-start(bf16[512,256]{1,0:T(8,128)(2,1)S(1)} %join_near.1.refs_1_), channel_id=1, source_target_pairs={{0,8},{8,0},{16,24},{24,16},{1,9},{9,1},{17,25},{25,17},{2,10},{10... | collective-permute-start | bytes 786440 | tf_op jit(solution)/shard_map/ppermute | solution.py:443
  23.4 17.7 %collective-permute-start.11 = (bf16[512,256]{1,0:T(8,128)(2,1)S(1)}, bf16[512,256]{1,0:T(8,128)(2,1)S(1)}, u32[]{:S(2)}, u32[]{:S(2)}) collective-permute-start(bf16[512,256]{1,0:T(8,128)(2,1)S(1)} %join_far.1.refs_3_.refs_6_), channel_id=1, source_target_pairs={{0,16},{8,24},{16,0},{24,8},{1,17},{9,25},{17,1},{25,9},{2,18},{10... | collective-permute-start | bytes 786440 | tf_op jit(solution)/shard_map/ppermute | solution.py:443
  25.0 16.1 %collective-permute-start.10 = (bf16[512,256]{1,0:T(8,128)(2,1)S(1)}, bf16[512,256]{1,0:T(8,128)(2,1)S(1)}, u32[]{:S(2)}, u32[]{:S(2)}) collective-permute-start(bf16[512,256]{1,0:T(8,128)(2,1)S(1)} %join_far.1.refs_3_.refs_6_), channel_id=1, source_target_pairs={{0,8},{8,0},{16,24},{24,16},{1,9},{9,1},{17,25},{25,17},{2,10},{10... | collective-permute-start | bytes 786440 | tf_op jit(solution)/shard_map/ppermute | solution.py:443
  26.5 6.8 %collective-permute-start.12 = (bf16[256,256]{1,0:T(8,128)(2,1)S(1)}, bf16[256,256]{1,0:T(8,128)(2,1)S(1)}, u32[]{:S(2)}, u32[]{:S(2)}) collective-permute-start(bf16[256,256]{1,0:T(8,128)(2,1)S(1)} %get-tuple-element.77), channel_id=1, source_target_pairs={{0,2},{1,3},{2,0},{3,1},{4,6},{5,7},{6,4},{7,5},{8,10},{9,11},{10,... | collective-permute-start | bytes 393224 | tf_op jit(solution)/shard_map/ppermute | solution.py:443
  29.0 11.6 %collective-permute-start.13 = (bf16[256,256]{1,0:T(8,128)(2,1)S(1)}, bf16[256,256]{1,0:T(8,128)(2,1)S(1)}, u32[]{:S(2)}, u32[]{:S(2)}) collective-permute-start(bf16[256,256]{1,0:T(8,128)(2,1)S(1)} %get-tuple-element.78), channel_id=1, source_target_pairs={{0,4},{1,5},{2,6},{3,7},{4,0},{5,1},{6,2},{7,3},{8,12},{9,13},{10,... | collective-permute-start | bytes 393224 | tf_op jit(solution)/shard_map/ppermute | solution.py:443
  30.0 11.1 %collective-permute-start.14 = (bf16[256,256]{1,0:T(8,128)(2,1)S(1)}, bf16[256,256]{1,0:T(8,128)(2,1)S(1)}, u32[]{:S(2)}, u32[]{:S(2)}) collective-permute-start(bf16[256,256]{1,0:T(8,128)(2,1)S(1)} %get-tuple-element.79), channel_id=1, source_target_pairs={{0,6},{1,7},{2,4},{3,5},{4,2},{5,3},{6,0},{7,1},{8,14},{9,15},{10,... | collective-permute-start | bytes 393224 | tf_op jit(solution)/shard_map/ppermute | solution.py:443
  33.2 11.7 %collective-permute-start.8 = (bf16[256,256]{1,0:T(8,128)(2,1)S(1)}, bf16[256,256]{1,0:T(8,128)(2,1)S(1)}, u32[]{:S(2)}, u32[]{:S(2)}) collective-permute-start(bf16[256,256]{1,0:T(8,128)(2,1)S(1)} %get-tuple-element.75), channel_id=1, source_target_pairs={{0,16},{8,24},{16,0},{24,8},{1,17},{9,25},{17,1},{25,9},{2,18},{10... | collective-permute-start | bytes 393224 | tf_op jit(solution)/shard_map/ppermute | solution.py:443
  40.5 6.4 %collective-permute-start.9 = (bf16[256,256]{1,0:T(8,128)(2,1)S(1)}, bf16[256,256]{1,0:T(8,128)(2,1)S(1)}, u32[]{:S(2)}, u32[]{:S(2)}) collective-permute-start(bf16[256,256]{1,0:T(8,128)(2,1)S(1)} %get-tuple-element.76), channel_id=1, source_target_pairs={{0,8},{8,0},{16,24},{24,16},{1,9},{9,1},{17,25},{25,17},{2,10},{10... | collective-permute-start | bytes 393224 | tf_op jit(solution)/shard_map/ppermute | solution.py:443
  41.7 7.7 %collective-permute-start.16 = (bf16[256,256]{1,0:T(8,128)(2,1)S(1)}, bf16[256,256]{1,0:T(8,128)(2,1)S(1)}, u32[]{:S(2)}, u32[]{:S(2)}) collective-permute-start(bf16[256,256]{1,0:T(8,128)(2,1)S(1)} %get-tuple-element.81), channel_id=1, source_target_pairs={{0,8},{8,0},{16,24},{24,16},{1,9},{9,1},{17,25},{25,17},{2,10},{10... | collective-permute-start | bytes 393224 | tf_op jit(solution)/shard_map/ppermute | solution.py:443
  43.4 11.8 %collective-permute-start.18 = (bf16[1024,256]{1,0:T(8,128)(2,1)S(1)}, bf16[1024,256]{1,0:T(8,128)(2,1)S(1)}, u32[]{:S(2)}, u32[]{:S(2)}) collective-permute-start(bf16[1024,256]{1,0:T(8,128)(2,1)S(1)} %join_grads.1.refs_13_.refs_1_), channel_id=1, source_target_pairs={{0,16},{8,24},{16,0},{24,8},{1,17},{9,25},{17,1},{25,9},{2,18},{10... | collective-permute-start | bytes 1572872 | tf_op jit(solution)/shard_map/ppermute | solution.py:443
  45.0 11.7 %collective-permute-start.17 = (bf16[1024,256]{1,0:T(8,128)(2,1)S(1)}, bf16[1024,256]{1,0:T(8,128)(2,1)S(1)}, u32[]{:S(2)}, u32[]{:S(2)}) collective-permute-start(bf16[1024,256]{1,0:T(8,128)(2,1)S(1)} %join_grads.1.refs_13_.refs_1_), channel_id=1, source_target_pairs={{0,8},{8,0},{16,24},{24,16},{1,9},{9,1},{17,25},{25,17},{2,10},{10... | collective-permute-start | bytes 1572872 | tf_op jit(solution)/shard_map/ppermute | solution.py:443
  56.7 6.4 %collective-permute-start.19 = (bf16[512,256]{1,0:T(8,128)(2,1)S(1)}, bf16[512,256]{1,0:T(8,128)(2,1)S(1)}, u32[]{:S(2)}, u32[]{:S(2)}) collective-permute-start(bf16[512,256]{1,0:T(8,128)(2,1)S(1)} %get-tuple-element.87), channel_id=1, source_target_pairs={{0,16},{8,24},{16,0},{24,8},{1,17},{9,25},{17,1},{25,9},{2,18},{10... | collective-permute-start | bytes 786440 | tf_op jit(solution)/shard_map/ppermute | solution.py:443
  58.1 6.7 %collective-permute-start.20 = (bf16[512,256]{1,0:T(8,128)(2,1)S(1)}, bf16[512,256]{1,0:T(8,128)(2,1)S(1)}, u32[]{:S(2)}, u32[]{:S(2)}) collective-permute-start(bf16[512,256]{1,0:T(8,128)(2,1)S(1)} %get-tuple-element.88), channel_id=1, source_target_pairs={{0,8},{8,0},{16,24},{24,16},{1,9},{9,1},{17,25},{25,17},{2,10},{10... | collective-permute-start | bytes 786440 | tf_op jit(solution)/shard_map/ppermute | solution.py:443
  67.7 13.4 %collective-permute-start.22 = (bf16[512,512]{1,0:T(8,128)(2,1)S(1)}, bf16[512,512]{1,0:T(8,128)(2,1)S(1)}, u32[]{:S(2)}, u32[]{:S(2)}) collective-permute-start(bf16[512,512]{1,0:T(8,128)(2,1)S(1)} %get-tuple-element.92), channel_id=1, source_target_pairs={{0,16},{8,24},{16,0},{24,8},{1,17},{9,25},{17,1},{25,9},{2,18},{10... | collective-permute-start | bytes 1572872 | tf_op jit(solution)/shard_map/ppermute | solution.py:443
  68.3 14.8 %collective-permute-start.21 = (bf16[512,512]{1,0:T(8,128)(2,1)S(1)}, bf16[512,512]{1,0:T(8,128)(2,1)S(1)}, u32[]{:S(2)}, u32[]{:S(2)}) collective-permute-start(bf16[512,512]{1,0:T(8,128)(2,1)S(1)} %get-tuple-element.90.refs_11_), channel_id=1, source_target_pairs={{0,8},{8,0},{16,24},{24,16},{1,9},{9,1},{17,25},{25,17},{2,10},{10... | collective-permute-start | bytes 1572872 | tf_op jit(solution)/shard_map/ppermute | solution.py:443
  78.9 9.6 %collective-permute-start.27 = (bf16[256,512]{1,0:T(8,128)(2,1)S(1)}, bf16[256,512]{1,0:T(8,128)(2,1)S(1)}, u32[]{:S(2)}, u32[]{:S(2)}) collective-permute-start(bf16[256,512]{1,0:T(8,128)(2,1)S(1)} %get-tuple-element.103), channel_id=1, source_target_pairs={{0,8},{8,0},{16,24},{24,16},{1,9},{9,1},{17,25},{25,17},{2,10},{10... | collective-permute-start | bytes 786440 | tf_op jit(solution)/shard_map/ppermute | solution.py:443
  79.0 20.7 %collective-permute-start.25 = (bf16[256,512]{1,0:T(8,128)(2,1)S(1)}, bf16[256,512]{1,0:T(8,128)(2,1)S(1)}, u32[]{:S(2)}, u32[]{:S(2)}) collective-permute-start(bf16[256,512]{1,0:T(8,128)(2,1)S(1)} %get-tuple-element.99), channel_id=1, source_target_pairs={{0,8},{8,0},{16,24},{24,16},{1,9},{9,1},{17,25},{25,17},{2,10},{10... | collective-permute-start | bytes 786440 | tf_op jit(solution)/shard_map/ppermute | solution.py:443
  81.0 18.8 %collective-permute-start.26 = (bf16[256,512]{1,0:T(8,128)(2,1)S(1)}, bf16[256,512]{1,0:T(8,128)(2,1)S(1)}, u32[]{:S(2)}, u32[]{:S(2)}) collective-permute-start(bf16[256,512]{1,0:T(8,128)(2,1)S(1)} %get-tuple-element.101), channel_id=1, source_target_pairs={{0,16},{8,24},{16,0},{24,8},{1,17},{9,25},{17,1},{25,9},{2,18},{10... | collective-permute-start | bytes 786440 | tf_op jit(solution)/shard_map/ppermute | solution.py:443
  81.1 18.4 %collective-permute-start.28 = (bf16[256,512]{1,0:T(8,128)(2,1)S(1)}, bf16[256,512]{1,0:T(8,128)(2,1)S(1)}, u32[]{:S(2)}, u32[]{:S(2)}) collective-permute-start(bf16[256,512]{1,0:T(8,128)(2,1)S(1)} %get-tuple-element.105), channel_id=1, source_target_pairs={{0,16},{8,24},{16,0},{24,8},{1,17},{9,25},{17,1},{25,9},{2,18},{10... | collective-permute-start | bytes 786440 | tf_op jit(solution)/shard_map/ppermute | solution.py:443
  83.3 18.7 %collective-permute-start.23 = (bf16[512,256]{1,0:T(8,128)(2,1)S(1)}, bf16[512,256]{1,0:T(8,128)(2,1)S(1)}, u32[]{:S(2)}, u32[]{:S(2)}) collective-permute-start(bf16[512,256]{1,0:T(8,128)(2,1)S(1)} %get-tuple-element.94), channel_id=1, source_target_pairs={{0,16},{8,24},{16,0},{24,8},{1,17},{9,25},{17,1},{25,9},{2,18},{10... | collective-permute-start | bytes 786440 | tf_op jit(solution)/shard_map/ppermute | solution.py:443
  88.6 15.4 %collective-permute-start.24 = (bf16[512,256]{1,0:T(8,128)(2,1)S(1)}, bf16[512,256]{1,0:T(8,128)(2,1)S(1)}, u32[]{:S(2)}, u32[]{:S(2)}) collective-permute-start(bf16[512,256]{1,0:T(8,128)(2,1)S(1)} %get-tuple-element.95), channel_id=1, source_target_pairs={{0,8},{8,0},{16,24},{24,16},{1,9},{9,1},{17,25},{25,17},{2,10},{10... | collective-permute-start | bytes 786440 | tf_op jit(solution)/shard_map/ppermute | solution.py:443
  99.9 8.6 %collective-permute-start.32 = (bf16[256,256]{1,0:T(8,128)(2,1)S(1)}, bf16[256,256]{1,0:T(8,128)(2,1)S(1)}, u32[]{:S(2)}, u32[]{:S(2)}) collective-permute-start(bf16[256,256]{1,0:T(8,128)(2,1)S(1)} %get-tuple-element.117), channel_id=1, source_target_pairs={{0,16},{8,24},{16,0},{24,8},{1,17},{9,25},{17,1},{25,9},{2,18},{10... | collective-permute-start | bytes 393224 | tf_op jit(solution)/shard_map/ppermute | solution.py:443
  101.9 6.7 %collective-permute-start.33 = (bf16[256,256]{1,0:T(8,128)(2,1)S(1)}, bf16[256,256]{1,0:T(8,128)(2,1)S(1)}, u32[]{:S(2)}, u32[]{:S(2)}) collective-permute-start(bf16[256,256]{1,0:T(8,128)(2,1)S(1)} %get-tuple-element.118), channel_id=1, source_target_pairs={{0,8},{8,0},{16,24},{24,16},{1,9},{9,1},{17,25},{25,17},{2,10},{10... | collective-permute-start | bytes 393224 | tf_op jit(solution)/shard_map/ppermute | solution.py:443
  104.6 8.7 %collective-permute-start.30 = (bf16[256,256]{1,0:T(8,128)(2,1)S(1)}, bf16[256,256]{1,0:T(8,128)(2,1)S(1)}, u32[]{:S(2)}, u32[]{:S(2)}) collective-permute-start(bf16[256,256]{1,0:T(8,128)(2,1)S(1)} %get-tuple-element.115), channel_id=1, source_target_pairs={{0,4},{1,5},{2,6},{3,7},{4,0},{5,1},{6,2},{7,3},{8,12},{9,13},{10,... | collective-permute-start | bytes 393224 | tf_op jit(solution)/shard_map/ppermute | solution.py:443
  104.9 8.4 %collective-permute-start.31 = (bf16[256,256]{1,0:T(8,128)(2,1)S(1)}, bf16[256,256]{1,0:T(8,128)(2,1)S(1)}, u32[]{:S(2)}, u32[]{:S(2)}) collective-permute-start(bf16[256,256]{1,0:T(8,128)(2,1)S(1)} %get-tuple-element.116), channel_id=1, source_target_pairs={{0,6},{1,7},{2,4},{3,5},{4,2},{5,3},{6,0},{7,1},{8,14},{9,15},{10,... | collective-permute-start | bytes 393224 | tf_op jit(solution)/shard_map/ppermute | solution.py:443
  116.5 13.0 %collective-permute-start.38 = (bf16[256,256]{1,0:T(8,128)(2,1)S(1)}, bf16[256,256]{1,0:T(8,128)(2,1)S(1)}, u32[]{:S(2)}, u32[]{:S(2)}) collective-permute-start(bf16[256,256]{1,0:T(8,128)(2,1)S(1)} %get-tuple-element.121.refs_3_), channel_id=1, source_target_pairs={{0,4},{1,5},{2,6},{3,7},{4,0},{5,1},{6,2},{7,3},{8,12},{9,13},{10,... | collective-permute-start | bytes 393224 | tf_op jit(solution)/shard_map/ppermute | solution.py:443
  119.3 8.7 %collective-permute-start.39 = (bf16[256,256]{1,0:T(8,128)(2,1)S(1)}, bf16[256,256]{1,0:T(8,128)(2,1)S(1)}, u32[]{:S(2)}, u32[]{:S(2)}) collective-permute-start(bf16[256,256]{1,0:T(8,128)(2,1)S(1)} %get-tuple-element.126), channel_id=1, source_target_pairs={{0,6},{1,7},{2,4},{3,5},{4,2},{5,3},{6,0},{7,1},{8,14},{9,15},{10,... | collective-permute-start | bytes 393224 | tf_op jit(solution)/shard_map/ppermute | solution.py:443
  120.9 9.1 %collective-permute-start.37 = (bf16[256,256]{1,0:T(8,128)(2,1)S(1)}, bf16[256,256]{1,0:T(8,128)(2,1)S(1)}, u32[]{:S(2)}, u32[]{:S(2)}) collective-permute-start(bf16[256,256]{1,0:T(8,128)(2,1)S(1)} %get-tuple-element.125), channel_id=1, source_target_pairs={{0,2},{1,3},{2,0},{3,1},{4,6},{5,7},{6,4},{7,5},{8,10},{9,11},{10,... | collective-permute-start | bytes 393224 | tf_op jit(solution)/shard_map/ppermute | solution.py:443
  (17 other events, 82.5 us)

commit v3 on v2

--- a/solution.py
+++ b/solution.py
@@ -119,7 +119,7 @@
 BF16 = jnp.bfloat16
 I32 = jnp.int32
 CHIPS = 4
-VMEM_BYTES = 24 * 1024 * 1024
+VMEM_BYTES = 14 * 1024 * 1024
 
 
 def dot(a, b, dims=((1,), (0,))):
@@ -136,6 +136,10 @@
 
 def smem():
     return pl.BlockSpec(memory_space=pltpu.SMEM)
+
+
+def table_of(routes, probs):
+    return jnp.concatenate([routes[...].astype(F32), probs[...]], axis=0)
 
 
 def place_rows(ids, own, par, per):
@@ -168,9 +172,10 @@
     return high, middle, line - high - middle
 
 
-def send_kernel(per, ids, own_x, own_g, own_m, par_m, par_x, par_g, x0, x1, x2, x3, g0, g1, g2, g3):
-    own, par = own_m[...], par_m[...]
+def send_kernel(per, ids, own_x, own_g, own_r, own_p, par_r, par_p, par_x, par_g, c0, c1, c2, c3):
+    own, par = table_of(own_r, own_p), table_of(par_r, par_p)
     toks = own.shape[1]
+    feats = own_x.shape[1]
     _, _, _, either, rank = place_rows(ids, own, par, per)
     tail = lax.broadcasted_iota(I32, (16, toks), 0)
     lines = [own[0:1, :], own[1:2, :], par[0:1, :], par[1:2, :]]
@@ -180,14 +185,15 @@
     extra = jnp.zeros((16, toks), F32)
     for i, line in enumerate(lines):
         extra = jnp.where(tail == i, line, extra)
-    for q in range(CHIPS):
+    for q, out in enumerate((c0, c1, c2, c3)):
         for src in range(2):
             hot = pick(rank, either, CHIPS * src + q, per).astype(BF16)
             place = slice(src * per, (src + 1) * per)
-            (x0, x1, x2, x3)[q][place, :] = dot(hot, (own_x, par_x)[src][...]).astype(BF16)
-            (g0, g1, g2, g3)[q][place, :] = dot(hot, (own_g, par_g)[src][...]).astype(BF16)
+            out[place, 0:feats] = dot(hot, (own_x, par_x)[src][...]).astype(BF16)
+            out[place, feats : 2 * feats] = dot(hot, (own_g, par_g)[src][...]).astype(BF16)
         if q:
-            (x0, x1, x2, x3)[q][2 * per : 2 * per + 16, :] = extra.astype(BF16)
+            out[2 * per : 2 * per + 16, 0:toks] = extra.astype(BF16)
+            out[2 * per : 2 * per + 16, toks : 2 * toks] = jnp.zeros((16, toks), BF16)
 
 
 def room_of(e, cap, plan, extra_slots):
@@ -197,8 +203,8 @@
     return room
 
 
-def place_kernel(per, extra_slots, ids, cap, plan, own_m, par_m, e1, e2, e3, info, scale):
-    own, par = own_m[...], par_m[...]
+def place_kernel(per, extra_slots, ids, cap, plan, own_r, own_p, par_r, par_p, e1, e2, e3, info, near_scale, far_scale):
+    own, par = table_of(own_r, own_p), table_of(par_r, par_p)
     toks = own.shape[1]
     z, c = ids[0], ids[1]
     row, expert, named, either, rank = place_rows(ids, own, par, per)
@@ -210,7 +216,7 @@
     for s, table in enumerate((own, par)):
         sources.append((0, s, [table[k : k + 1, :] for k in range(4)]))
     for p, ref in ((1, e1), (2, e2), (3, e3)):
-        table = ref[2 * per : 2 * per + 16, :].astype(F32)
+        table = ref[2 * per : 2 * per + 16, 0:toks].astype(F32)
         for s in range(2):
             lines = [table[2 * s + k : 2 * s + k + 1, :] for k in range(2)]
             for k in range(2):
@@ -278,10 +284,11 @@
     for i in range(2 * CHIPS):
         hot = pick(rank, either, i, per)
         value = jnp.sum(hot * weight[i : i + 1, :], axis=1, keepdims=True)
-        scale[i * per : (i + 1) * per, :] = jnp.broadcast_to(value, (per, 128))
-
-
-def load_kernel(a, b, c, x, y, z, sems):
+        at = i % 4 * per
+        (near_scale, far_scale)[i // 4][at : at + per, :] = jnp.broadcast_to(value, (per, 128))
+
+
+def load_kernel(a, b, c, after, x, y, z, sems):
     copies = [
         pltpu.make_async_copy(src, dst, sems.at[i])
         for i, (src, dst) in enumerate(((a, x), (b, y), (c, z)))
@@ -298,17 +305,23 @@
     return dot((slots == slot).astype(F32).astype(BF16), rows)
 
 
-def back_kernel(per, with_dots, y0, y1, y2, y3, info_ref, *refs):
+def back_kernel(per, with_dots, at0, feats, y0, y1, y2, y3, info_ref, *refs):
     if with_dots:
-        own_g, par_g, kept, sent = refs
+        own_g, par_g, kept, sent, kept_dots, sent_dots = refs
     else:
         kept, sent = refs
     info = info_ref[...]
-    feats = y0.shape[1]
     toks = info.shape[0]
+    starts = [at0 if y.shape[1] > feats else 0 for y in (y0, y1, y2, y3)]
     lane = lax.broadcasted_iota(I32, (toks, 128), 1)
     for src, out in enumerate((kept, sent)):
-        rows = jnp.concatenate([y[src * per : (src + 1) * per, :] for y in (y0, y1, y2, y3)], axis=0)
+        rows = jnp.concatenate(
+            [
+                y[src * per : (src + 1) * per, at : at + feats]
+                for y, at in zip((y0, y1, y2, y3), starts)
+            ],
+            axis=0,
+        )
         total = jnp.zeros((toks, feats), F32)
         dots = jnp.zeros((toks, 128), F32)
         for k in range(2):
@@ -319,45 +332,41 @@
                 grad = (own_g, par_g)[src][...].astype(F32)
                 inner = jnp.sum(grad * picked, axis=1, keepdims=True) * info[:, 8 + at : 9 + at]
                 dots = jnp.where(lane == k, inner, dots)
-        out[:, 0:feats] = total
+        out[...] = total.astype(out.dtype)
         if with_dots:
-            out[:, feats : feats + 128] = dots
-
-
-def assemble(r, at, shards, cat):
+            (kept_dots, sent_dots)[src][...] = jnp.transpose(dots)[0:8, :]
+
+
+def assemble(r, shards, at, feats, cat, scale):
     own, a, b, c, d = shards
-    rows, feats = own.shape
+    rows = own.shape[0]
     half = rows // 2
-
-    def cols(k):
-        return pl.ds(pl.multiple_of((r ^ k) * feats, feats), feats)
-
-    cat[at : at + rows, cols(0)] = own[...]
-    cat[at : at + rows, cols(1)] = a[...]
-    cat[at : at + rows, cols(2)] = b[...]
-    cat[at : at + half, cols(3)] = c[...]
-    cat[at + half : at + rows, cols(3)] = d[...]
-
-
-def split_out(part, groups):
-    _, (send, *_) = groups[0]
-    feats = send.shape[1] // 2
-    low, high = slice(0, feats), slice(feats, 2 * feats)
+    lanes = slice(at, at + feats)
+    factor = None if scale is None else scale[:, 0:1]
+    for k, start, ref in ((0, 0, own), (1, 0, a), (2, 0, b), (3, 0, c), (3, half, d)):
+        cols = pl.ds(pl.multiple_of((r ^ k) * feats, feats), feats)
+        size = ref.shape[0]
+        piece = ref[:, lanes]
+        if factor is not None:
+            piece = (piece.astype(F32) * factor[start : start + size, :]).astype(BF16)
+        cat[start : start + size, cols] = piece
+
+
+def split_out(part, outs, feats, low, high):
+    send_a, keep_a, send_b, keep_b = outs
+    half = send_a.shape[0]
+    low, high = slice(low, low + feats), slice(high, high + feats)
     for k in (3, 1, 2, 0):
         piece = part(k).astype(BF16)
-        for at, (send_a, keep_a, send_b, keep_b) in groups:
-            half = send_a.shape[0]
-            top = ((keep_a, low), (send_a, low), (keep_a, high), (send_a, high))[k]
-            bottom = ((keep_b, low), (keep_b, high), (send_b, low), (send_b, high))[k]
-            top[0][:, top[1]] = piece[at : at + half, :]
-            bottom[0][:, bottom[1]] = piece[at + half : at + 2 * half, :]
-
-
-def forward_kernel(ids, *refs):
-    near, far, (wg, wu, cat, hid, act, slope) = refs[:5], refs[5:10], refs[10:]
-    r = ids[2]
-    assemble(r, 0, near, cat)
-    assemble(r, near[0].shape[0], far, cat)
+        top = ((keep_a, low), (send_a, low), (keep_a, high), (send_a, high))[k]
+        bottom = ((keep_b, low), (keep_b, high), (send_b, low), (send_b, high))[k]
+        top[0][:, top[1]] = piece[0:half, :]
+        bottom[0][:, bottom[1]] = piece[half : 2 * half, :]
+
+
+def forward(r, shards, wg, wu, wd, cat, hid, act, slope, outs, low, high):
+    feats = shards[0].shape[1] // 2
+    assemble(r, shards, 0, feats, cat, None)
     step = 256
     for j in range(0, hid.shape[1], step):
         cols = slice(j, j + step)
@@ -366,23 +375,18 @@
         sig = jax.nn.sigmoid(gate)
         silu = gate * sig
         hid[:, cols] = (silu * up).astype(BF16)
-        act[:, cols] = silu.astype(BF16)
-        slope[:, cols] = (up * (sig + silu * (1.0 - sig))).astype(BF16)
-
-
-def out_kernel(ids, hid, wd, sa, ka, sb, kb):
-    r = ids[2]
-    feats = sa.shape[1] // 2
+        act[:, cols] = silu.astype(act.dtype)
+        slope[:, cols] = (up * (sig + silu * (1.0 - sig))).astype(slope.dtype)
 
     def part(k):
         return dot(hid[...], wd[:, pl.ds(pl.multiple_of((r ^ k) * feats, feats), feats)])
 
-    split_out(part, [(0, (sa, ka, sb, kb))])
-
-
-def backward_kernel(ids, own, a, b, c, d, wg, wu, wd, act, slope, cat, dgate, dup, *outs):
-    r = ids[2]
-    assemble(r, 0, (own, a, b, c, d), cat)
+    split_out(part, outs, feats, low, high)
+
+
+def backward(r, shards, scale, wg, wu, wd, act, slope, cat, dgate, dup, outs, low, high):
+    feats = shards[0].shape[1] // 2
+    assemble(r, shards, feats, feats, cat, scale)
     step = 256
     for j in range(0, dgate.shape[1], step):
         cols = slice(j, j + step)
@@ -391,34 +395,46 @@
         dup[:, cols] = (dh * act[:, cols].astype(F32)).astype(BF16)
 
     def part(k):
-        feats = own.shape[1]
         line = pl.ds(pl.multiple_of((r ^ k) * feats, feats), feats)
         return dot(dgate[...], wg[line, :], ((1,), (1,))) + dot(dup[...], wu[line, :], ((1,), (1,)))
 
-    split_out(part, [(cat.shape[0] // 2, outs[:4]), (0, outs[4:])])
-
-
-def weights_kernel(xcat, gcat, dgate, dup, hid, ggate, gup, gdown, done):
+    split_out(part, outs, feats, low, high)
+
+
+def near_kernel(ids, *refs):
+    shards, (scale, wg, wu, wd), refs = refs[:5], refs[5:9], refs[9:]
+    (xcat, hid, gcat, dgate, dup), outs, (act, slope) = refs[:5], refs[5:9], refs[9:]
+    r, feats = ids[2], shards[0].shape[1] // 2
+    forward(r, shards, wg, wu, wd, xcat, hid, act, slope, outs, 0, 2 * feats)
+    backward(r, shards, scale, wg, wu, wd, act, slope, gcat, dgate, dup, outs, feats, 3 * feats)
+
+
+def far_forward_kernel(ids, *refs):
+    shards, (wg, wu, wd), (xcat, hid, act, slope), outs = refs[:5], refs[5:8], refs[8:12], refs[12:]
+    feats = shards[0].shape[1] // 2
+    forward(ids[2], shards, wg, wu, wd, xcat, hid, act, slope, outs, 0, feats)
+
+
+def far_backward_kernel(ids, *refs):
+    shards, (scale, wg, wu, wd, act, slope) = refs[:5], refs[5:11]
+    (gcat, dgate, dup), outs = refs[11:14], refs[14:]
+    feats = shards[0].shape[1] // 2
+    backward(ids[2], shards, scale, wg, wu, wd, act, slope, gcat, dgate, dup, outs, 0, feats)
+
+
+def weights_kernel(left_a, left_b, right_a, right_b, after, out, done):
     done[...] = jnp.zeros_like(done)
-    size = ggate.shape[0]
+    size = out.shape[0]
     cols = pl.ds(pl.multiple_of(pl.program_id(0) * size, size), size)
-    x = xcat[:, cols]
-    ggate[...] = dot(x, dgate[...], ((0,), (0,)))
-    gup[...] = dot(x, dup[...], ((0,), (0,)))
-    gdown[...] = dot(hid[:, cols], gcat[...], ((0,), (0,)))
+    out[...] = dot(left_a[:, cols], right_a[...], ((0,), (0,))) + dot(
+        left_b[:, cols], right_b[...], ((0,), (0,))
+    )
 
 
 def join_kernel(a, b, out):
     size = out.shape[0] // 2
     out[0:size, :] = a[0:size, :]
     out[size : 2 * size, :] = b[0:size, :]
-
-
-def join_scaled_kernel(a, b, c, d, scale, out):
-    size = out.shape[0] // CHIPS
-    for q, ref in enumerate((a, b, c, d)):
-        at = slice(q * size, (q + 1) * size)
-        out[at, :] = (ref[...].astype(F32) * scale[at, 0:1]).astype(BF16)
 
 
 def middle_kernel(ka, ra, kb, rb, sa, sb, kept):
@@ -455,9 +471,17 @@
     return [pltpu.with_memory_space_constraint(x, pltpu.VMEM) for x in arrays]
 
 
-def kernel_call(body, name, outs, *args, plan_args=0, loose=0, flops=0, after=()):
+def grad_kernel(per, feats, y0, y1, y2, y3, info, dots, kept, sent, dots_out):
+    back_kernel(per, False, feats, feats, y0, y1, y2, y3, info, kept, sent)
+    dots_out[...] = dots[...]
+
+
+def kernel_call(body, name, outs, *args, plan_args=0, loose=0, flops=1, after=(), scratch=()):
     count = len(args)
-    pinned = list(args[: plan_args + loose]) + pin(*args[plan_args + loose :], *after)
+    pinned = list(args[:plan_args])
+    for x in args[plan_args : plan_args + loose]:
+        pinned.append(pltpu.with_memory_space_constraint(x, pltpu.HBM))
+    pinned += pin(*args[plan_args + loose :], *after)
 
     def run(*refs):
         body(*refs[:count], *refs[count + len(after) :])
@@ -466,6 +490,7 @@
         run,
         in_specs=[smem()] * plan_args + [vmem()] * (count - plan_args + len(after)),
         out_shape=outs,
+        scratch_shapes=scratch,
         compiler_params=params(),
         cost_estimate=pl.CostEstimate(flops=flops, bytes_accessed=1 << 20, transcendentals=0),
         name=name,
@@ -509,7 +534,11 @@
 
 
 def over_chips(chunks):
-    return [chunks[q] if q == 0 else shift(chunks[q], "exp", 2 * q) for q in range(CHIPS)]
+    return over_chips_from(0, chunks)
+
+
+def over_chips_from(first, chunks):
+    return [c if first + n == 0 else shift(c, "exp", 2 * (first + n)) for n, c in enumerate(chunks)]
 
 
 def on_quad(tokens, routes, probs, capacity, plan, grad_out, w_gate, w_up, w_down):
@@ -520,120 +549,135 @@
     rows = 2 * per * CHIPS
     me = lax.axis_index("exp").astype(I32)
     ids = jnp.stack([me // 2, me % 2, lax.axis_index("rep").astype(I32)])
-    own_m = jnp.concatenate(
-        [routes.T.astype(F32), probs.T, jnp.zeros((4, toks), F32)], axis=0
-    )
-    par_m = shift(own_m, "exp", 1)
+    own_m = (routes.T, probs.T)
+    par_m = tuple(shift(x, "exp", 1) for x in own_m)
     par_x = shift(tokens, "exp", 1)
     par_g = shift(grad_out, "exp", 1)
 
     size = 2 * per
-    near = vm((size, feats), BF16)
-    far = vm((size + 16, feats), BF16)
+    both = 2 * feats
+    stay = vm((size, both), BF16)
+    go = vm((size + 16, both), BF16)
     sent = kernel_call(
         functools.partial(send_kernel, per),
         "send",
-        (near, far, far, far) + (near,) * 4,
-        ids, tokens, grad_out, own_m, par_m, par_x, par_g,
+        (stay, go, go, go),
+        ids, tokens, grad_out, *own_m, *par_m, par_x, par_g,
         plan_args=1,
         loose=2,
     )
-    xr = over_chips(sent[:CHIPS])
-    gr = over_chips(sent[CHIPS:])
+    got = over_chips(sent)
+    pair_rows = vm((2 * size, both), BF16)
+    near = gather_first(kernel_call(join_kernel, "join_near", pair_rows, got[0], got[1]))
     loaded = vm((width, ff), BF16)
     wg, wu, wd = pl.pallas_call(
         load_kernel,
-        in_specs=[pl.BlockSpec(memory_space=pltpu.HBM)] * 3,
+        in_specs=[pl.BlockSpec(memory_space=pltpu.HBM)] * 3 + [vmem()],
         out_shape=(loaded, loaded, vm((ff, width), BF16)),
         scratch_shapes=[pltpu.SemaphoreType.DMA((3,))],
         compiler_params=params(),
+        cost_estimate=pl.CostEstimate(flops=2*10**10, bytes_accessed=24 << 20, transcendentals=0),
         name="load_weights",
-    )(*[pltpu.with_memory_space_constraint(w, pltpu.HBM) for w in (wg, wu, wd)])
-    pair_rows = vm((2 * size, feats), BF16)
-    xa = gather_first(kernel_call(join_kernel, "join_near", pair_rows, xr[0], xr[1]))
-    xb = gather_first(kernel_call(join_kernel, "join_far", pair_rows, xr[2], xr[3], after=(wg,)))
-    info, scale = kernel_call(
+    )(*[pltpu.with_memory_space_constraint(w, pltpu.HBM) for w in (wg, wu, wd)], *pin(near[0]))
+    far = gather_first(
+        kernel_call(join_kernel, "join_far", pair_rows, got[2], got[3], after=(wg,))
+    )
+    info, near_scale, far_scale = kernel_call(
         functools.partial(place_kernel, per, 2 * toks),
         "place",
-        (vm((toks, 128), F32), vm((rows, 128), F32)),
-        ids, capacity, plan, own_m, par_m, *xr[1:],
+        (vm((toks, 128), F32), vm((2 * size, 128), F32), vm((2 * size, 128), F32)),
+        ids, capacity, plan, *own_m, *par_m, *got[1:],
         plan_args=3,
     )
-    xa = gather_second(xa, (info, xb[0]))
-    xb = gather_second(xb, gr[1:])
-    gs = gather_first(
-        kernel_call(join_scaled_kernel, "join_grads", vm((rows, feats), BF16), *gr, scale)
-    )
-
-    pair_t = vm((rows // 2, 2 * feats), BF16)
-    inner = vm((rows, ff), BF16)
-    wide = vm((rows, width), BF16)
-    work = 2 * rows * width * ff
-    xcat, hid, act, slope = kernel_call(
-        forward_kernel,
-        "forward",
-        (wide, inner, inner, inner),
-        ids, *xa, *xb, wg, wu,
+    near = gather_second(near, (far[0],))
+
+    inner = vm((2 * size, ff), BF16)
+    wide = vm((2 * size, width), BF16)
+    work = 2 * (2 * size) * width * ff
+    near_x, near_hid, near_g, near_dgate, near_dup, *near_parts = kernel_call(
+        near_kernel,
+        "near",
+        (wide, inner, wide, inner, inner) + (vm((size, 2 * both), BF16),) * 4,
+        ids, *near, near_scale, wg, wu, wd,
         plan_args=1,
-        flops=2 * work,
-        after=gs[:1],
-    )
-    gs = gather_second(gs, (hid,))
-    out_parts = kernel_call(
-        out_kernel, "out_parts", (pair_t,) * 4, ids, hid, wd, plan_args=1, flops=work, after=gs[3:]
-    )
-    out_sums = reduce_second(reduce_first(*out_parts))
-
-    gcat, dgate, dup, *dx_parts = kernel_call(
-        backward_kernel,
-        "backward",
-        (wide, inner, inner) + (vm((size, 2 * feats), BF16),) * 8,
-        ids, *gs, wg, wu, wd, act, slope,
+        flops=6 * work,
+        scratch=[pltpu.VMEM((2 * size, ff), F32)] * 2,
+    )
+    far = gather_second(far, (near_hid,))
+    near_first = reduce_first(*near_parts)
+    part = vm((size, both), BF16)
+    far_x, far_hid, act, slope, *out_parts = kernel_call(
+        far_forward_kernel,
+        "far_forward",
+        (wide, inner, inner, inner) + (part,) * 4,
+        ids, *far, wg, wu, wd,
+        plan_args=1,
+        flops=3 * work,
+    )
+    out_first = reduce_first(*out_parts)
+    far_g, far_dgate, far_dup, *dx_parts = kernel_call(
+        far_backward_kernel,
+        "far_backward",
+        (wide, inner, inner) + (part,) * 4,
+        ids, *far, far_scale, wg, wu, wd, act, slope,
         plan_args=1,
         flops=3 * work,
         after=out_parts[:1],
     )
-    far_first = reduce_first(*dx_parts[:4])
-    near_first = reduce_first(*dx_parts[4:])
-
-    steps = 4
-    grad_gate, grad_up, grad_down, done = pl.pallas_call(
-        weights_kernel,
-        grid=(steps,),
-        in_specs=[vmem()] * 5,
-        out_specs=[pl.BlockSpec((n // steps, m), lambda i: (i, 0)) for n, m in ((width, ff), (width, ff), (ff, width))] + [vmem()],
-        out_shape=(sds((width, ff), F32), sds((width, ff), F32), sds((ff, width), F32), vm((8, 128), F32)),
-        compiler_params=params(),
-        cost_estimate=pl.CostEstimate(flops=3 * work, bytes_accessed=12 << 20, transcendentals=0),
-        name="weight_grads",
-    )(*pin(xcat, gcat, dgate, dup, hid))
-
-    far_sums = reduce_second(far_first, (done, out_sums[0]))
-    near_sums = reduce_second(near_first, (far_sums[0],))
-    yr = over_chips(reduce_last(out_sums, size, (near_sums[0],)))
-    dx_far = reduce_last(far_sums, size, yr[:1])
-    dx_near = reduce_last(near_sums, size, dx_far[:1])
-    dr = over_chips([*dx_near, *dx_far])
-    broad = vm((toks, feats + 128), F32)
-    kept, sent = kernel_call(
-        functools.partial(back_kernel, per, True),
+    dx_first = reduce_first(*dx_parts)
+
+    def weight_grad(name, left, right, n, m, after):
+        steps = 4
+        return pl.pallas_call(
+            weights_kernel,
+            grid=(steps,),
+            in_specs=[vmem()] * 5,
+            out_specs=[pl.BlockSpec((n // steps, m), lambda i: (i, 0)), vmem()],
+            out_shape=(sds((n, m), F32), vm((8, 128), F32)),
+            compiler_params=params(),
+            cost_estimate=pl.CostEstimate(flops=2*10**10, bytes_accessed=1, transcendentals=0),
+            name=name,
+        )(*pin(*left, *right, after))
+
+    near_sums = reduce_second(near_first, (far_dgate,))
+    out_sums = reduce_second(out_first, (near_sums[0],))
+    grad_down, done_d = weight_grad(
+        "grad_down", (near_hid, far_hid), (near_g, far_g), ff, width, out_sums[0]
+    )
+    dx_sums = reduce_second(dx_first, (done_d,))
+    out_rows = reduce_last(out_sums, size, (dx_sums[0],))
+    back_out = over_chips_from(2, out_rows)
+    grad_gate, done_g = weight_grad(
+        "grad_gate", (near_x, far_x), (near_dgate, far_dgate), width, ff, out_rows[0]
+    )
+    dx_rows = reduce_last(dx_sums, size, (done_g,))
+    back_dx = over_chips_from(2, dx_rows)
+    near_rows = reduce_last(near_sums, size, dx_rows[:1])
+    back_near = over_chips_from(0, near_rows)
+    grad_up, done_u = weight_grad(
+        "grad_up", (near_x, far_x), (near_dup, far_dup), width, ff, near_rows[0]
+    )
+
+    whole, narrow, few = vm((toks, feats), F32), vm((toks, feats), BF16), vm((8, toks), F32)
+    kept, sent, kept_dots, sent_dots = kernel_call(
+        functools.partial(back_kernel, per, True, 0, feats),
         "combine_out",
-        (broad, broad),
-        *yr, info, grad_out, par_g,
-        after=dx_near[:1],
-    )
-    both = kept + shift(sent, "exp", 1)
-    mixed = both[:, :feats].astype(BF16)
-    dots = both[:, feats : feats + 2].T
-    dots = dots + shift(dots, "rep", 1)
-    dots = dots + shift(dots, "rep", 2)
-    grad_probs = dots.T
-
-    flat = vm((toks, feats), F32)
-    kept, sent = kernel_call(
-        functools.partial(back_kernel, per, False), "combine_grad", (flat, flat), *dr, info, after=(dots,)
-    )
-    grad_tokens = (kept + shift(sent, "exp", 1)).astype(BF16)
+        (whole, narrow, few, few),
+        *back_near, *back_out, info, grad_out, par_g,
+        after=(done_u,),
+    )
+    mixed = (kept + shift(sent, "exp", 1).astype(F32)).astype(BF16)
+    dots = kept_dots + shift(sent_dots, "exp", 1)
+    kept, sent, dots = kernel_call(
+        functools.partial(grad_kernel, per, feats),
+        "combine_grad",
+        (whole, narrow, few),
+        *back_near, *back_dx, info, dots,
+    )
+    first = dots[0:2]
+    second, third, fourth = (shift(first, "rep", k) for k in (1, 2, 3))
+    grad_probs = ((first + second) + (third + fourth)).T
+    grad_tokens = (kept + shift(sent, "exp", 1).astype(F32)).astype(BF16)
     return (mixed, grad_tokens, grad_probs, grad_gate[None], grad_up[None], grad_down[None])
 
 

time: 133 us -> 127 us (0.955)
  starting transfers between devices: 48 us -> 42.5 us
  Pallas kernels: 33 us -> 37.3 us
  waiting for transfers between devices: 45.6 us -> 42.6 us
  local copies, waits for them, and re-layouts: 3.02 us -> 1.38 us
    ppermute x43 -> x38, starting transfers between devices: 48 us -> 42.5 us  [shift(): return lax.ppermute(x, axis, [(i, i ^ bit) for i in range(n)])]
    pallas_call x1 -> x3, Pallas kernels: 8.47 us -> 12.6 us  [weight_grad(): pl.pallas_call(weights_kernel, grid=(steps,), in_specs=[vmem()] * 5, out_...]
    ppermute x43 -> x38, waiting for transfers between devices: 45.6 us -> 42.6 us  [shift(): return lax.ppermute(x, axis, [(i, i ^ bit) for i in range(n)])]
    pallas_call x19 -> x17, Pallas kernels: 21.6 us -> 21.8 us  [kernel_call(): pl.pallas_call(run, in_specs=[smem()] * plan_args + [vmem()] * (count - p...]
  transfers between devices with their start and end apart: 43 -> 38, of which waited for: 21 -> 20; matrix products, arithmetic and copies ran while one was open for 2% -> 1% of each run, Pallas kernels for 21% -> 28%
where the time goes in v3:
time: 127 us
  waiting for transfers between devices  42.6 us (34%)
  starting transfers between devices  42.5 us (33%)
  Pallas kernels  37.3 us (29%)
  other arithmetic  2.03 us (2%)
  local copies, waits for them, and re-layouts  1.38 us (1%)
    ppermute x38, waiting for transfers between devices, shift(): return lax.ppermute(x, axis, [(i, i ^ bit) for i in range(n)])  42.6 us
    ppermute x38, starting transfers between devices, shift(): return lax.ppermute(x, axis, [(i, i ^ bit) for i in range(n)])  42.5 us
    pallas_call x17, Pallas kernels, kernel_call(): pl.pallas_call(run, in_specs=[smem()] * plan_args + [vmem()] * (count - p...  21.8 us
    pallas_call x3, Pallas kernels, weight_grad(): pl.pallas_call(weights_kernel, grid=(steps,), in_specs=[vmem()] * 5, out_...  12.6 us
    pallas_call x1, Pallas kernels, on_quad(): pl.pallas_call(load_kernel, in_specs=[pl.BlockSpec(memory_space=pltpu.HBM...  2.88 us
  transfers between devices with their start and end apart: 38, of which 20 were waited for; matrix products, arithmetic and copies ran while one was open for 1% of the time, Pallas kernels for 28%

profile of v3, /device:TPU:0, one launch (start us, length us, event | category | flops | bytes accessed | tf_op | source)
XLA Modules:
  0.0 126.6 jit_solution(15783365479334805590)
XLA Ops:
  4.4 1.6 %send.1 = (bf16[256,512]{1,0:T(8,128)(2,1)S(1)}, bf16[272,512]{1,0:T(8,128)(2,1)S(1)}, bf16[272,512]{1,0:T(8,128)(2,1)S(1)}, bf16[272,512]{1,0:T(8,128)(2,1)S(1)}) custom-call(s32[3]{0:T(128)S(1)} %pad_add_fusion.refs_0_, bf16[256,256]{1,0:T(8,128)(2,1)} %refs_1_.2, bf16[256,256]{1,0:T(8,128)(2,1)} %refs_5_.1, s32[2,256]{1,0:T(2,128)S(1)} %bitcast.14, ...), custom_call_target="tpu_custom_call" | custom-call | flops 1 | bytes 1048576 | tf_op jit(solution)/shard_map/send/pallas_call | solution.py:489
  6.0 2.8 %collective-permute-start.4 = (bf16[272,512]{1,0:T(8,128)(2,1)S(1)}, bf16[272,512]{1,0:T(8,128)(2,1)S(1)}, u32[]{:S(2)}, u32[]{:S(2)}) collective-permute-start(bf16[272,512]{1,0:T(8,128)(2,1)S(1)} %get-tuple-element.73), channel_id=1, source_target_pairs={{0,2},{1,3},{2,0},{3,1},{4,6},{5,7},{6,4},{7,5},{8,10},{9,11},{10,... | collective-permute-start | bytes 835592 | tf_op jit(solution)/shard_map/ppermute | solution.py:459
  8.8 2.6 %collective-permute-start.7 = (bf16[272,512]{1,0:T(8,128)(2,1)S(1)}, bf16[272,512]{1,0:T(8,128)(2,1)S(1)}, u32[]{:S(2)}, u32[]{:S(2)}) collective-permute-start(bf16[272,512]{1,0:T(8,128)(2,1)S(1)} %get-tuple-element.74), channel_id=1, source_target_pairs={{0,4},{1,5},{2,6},{3,7},{4,0},{5,1},{6,2},{7,3},{8,12},{9,13},{10,... | collective-permute-start | bytes 835592 | tf_op jit(solution)/shard_map/ppermute | solution.py:459
  11.4 10.0 %collective-permute-done.4.refs_1_.refs_7_ = bf16[272,512]{1,0:T(8,128)(2,1)S(1)} collective-permute-done((bf16[272,512]{1,0:T(8,128)(2,1)S(1)}, bf16[272,512]{1,0:T(8,128)(2,1)S(1)}, u32[]{:S(2)}, u32[]{:S(2)}) %collective-permute-start.4) | collective-permute-done | bytes 278560 | tf_op jit(solution)/shard_map/ppermute | solution.py:459
  21.4 1.7 %collective-permute-start.6 = (bf16[512,512]{1,0:T(8,128)(2,1)S(1)}, bf16[512,512]{1,0:T(8,128)(2,1)S(1)}, u32[]{:S(2)}, u32[]{:S(2)}) collective-permute-start(bf16[512,512]{1,0:T(8,128)(2,1)S(1)} %join_near.1.after.refs_1_), channel_id=1, source_target_pairs={{0,16},{8,24},{16,0},{24,8},{1,17},{9,25},{17,1},{25,9},{2,18},{10... | collective-permute-start | bytes 1572872 | tf_op jit(solution)/shard_map/ppermute | solution.py:459
  23.2 1.5 %collective-permute-start.5 = (bf16[512,512]{1,0:T(8,128)(2,1)S(1)}, bf16[512,512]{1,0:T(8,128)(2,1)S(1)}, u32[]{:S(2)}, u32[]{:S(2)}) collective-permute-start(bf16[512,512]{1,0:T(8,128)(2,1)S(1)} %join_near.1.after.refs_1_), channel_id=1, source_target_pairs={{0,8},{8,0},{16,24},{24,16},{1,9},{9,1},{17,25},{25,17},{2,10},{10... | collective-permute-start | bytes 1572872 | tf_op jit(solution)/shard_map/ppermute | solution.py:459
  24.7 2.9 %load_weights.1 = (bf16[1024,1024]{1,0:T(8,128)(2,1)S(1)}, bf16[1024,1024]{1,0:T(8,128)(2,1)S(1)}, bf16[1024,1024]{1,0:T(8,128)(2,1)S(1)}) custom-call(bf16[1024,1024]{1,0:T(8,128)(2,1)} %bitcast.19, bf16[1024,1024]{1,0:T(8,128)(2,1)} %bitcast.20, bf16[1024,1024]{1,0:T(8,128)(2,1)} %bitcast.21, bf16[512,512]{1,0:T(8,128)(2,1)S(1)} %join_near.1.after.refs_1_), custom_call_target="tpu_custom_call" | custom-call | flops 20000000000 | bytes 25165824 | tf_op jit(solution)/shard_map/load_weights/pallas_call | solution.py:573
  27.6 3.6 %collective-permute-done.7.refs_0_.refs_8_ = bf16[272,512]{1,0:T(8,128)(2,1)S(1)} collective-permute-done((bf16[272,512]{1,0:T(8,128)(2,1)S(1)}, bf16[272,512]{1,0:T(8,128)(2,1)S(1)}, u32[]{:S(2)}, u32[]{:S(2)}) %collective-permute-start.7) | collective-permute-done | bytes 278560 | tf_op jit(solution)/shard_map/ppermute | solution.py:459
  31.2 4.0 %collective-permute-done.6.refs_1_.refs_3_ = bf16[512,512]{1,0:T(8,128)(2,1)S(1)} collective-permute-done((bf16[512,512]{1,0:T(8,128)(2,1)S(1)}, bf16[512,512]{1,0:T(8,128)(2,1)S(1)}, u32[]{:S(2)}, u32[]{:S(2)}) %collective-permute-start.6) | collective-permute-done | bytes 524320 | tf_op jit(solution)/shard_map/ppermute | solution.py:459
  37.0 1.3 %collective-permute-start.10 = (bf16[256,512]{1,0:T(8,128)(2,1)S(1)}, bf16[256,512]{1,0:T(8,128)(2,1)S(1)}, u32[]{:S(2)}, u32[]{:S(2)}) collective-permute-start(bf16[256,512]{1,0:T(8,128)(2,1)S(1)} %get-tuple-element.78), channel_id=1, source_target_pairs={{0,8},{8,0},{16,24},{24,16},{1,9},{9,1},{17,25},{25,17},{2,10},{10... | collective-permute-start | bytes 786440 | tf_op jit(solution)/shard_map/ppermute | solution.py:459
  38.4 1.5 %collective-permute-start.14 = (bf16[512,512]{1,0:T(8,128)(2,1)S(1)}, bf16[512,512]{1,0:T(8,128)(2,1)S(1)}, u32[]{:S(2)}, u32[]{:S(2)}) collective-permute-start(bf16[512,512]{1,0:T(8,128)(2,1)S(1)} %join_far.1.refs_2_.refs_1_), channel_id=1, source_target_pairs={{0,16},{8,24},{16,0},{24,8},{1,17},{9,25},{17,1},{25,9},{2,18},{10... | collective-permute-start | bytes 1572872 | tf_op jit(solution)/shard_map/ppermute | solution.py:459
  41.5 4.2 %collective-permute-done.9.refs_4_ = bf16[256,512]{1,0:T(8,128)(2,1)S(1)} collective-permute-done((bf16[256,512]{1,0:T(8,128)(2,1)S(1)}, bf16[256,512]{1,0:T(8,128)(2,1)S(1)}, u32[]{:S(2)}, u32[]{:S(2)}) %collective-permute-start.9) | collective-permute-done | bytes 262176 | tf_op jit(solution)/shard_map/ppermute | solution.py:459
  46.3 7.7 %near.1 = (bf16[512,1024]{1,0:T(8,128)(2,1)S(1)}, bf16[512,1024]{1,0:T(8,128)(2,1)S(1)}, bf16[512,1024]{1,0:T(8,128)(2,1)S(1)}, bf16[512,1024]{1,0:T(8,128)(2,1)...) custom-call(s32[3]{0:T(128)S(1)} %pad_add_fusion.refs_0_, ...), custom_call_target="tpu_custom_call" | custom-call | flops 6442450944 | bytes 1048576 | tf_op jit(solution)/shard_map/near/pallas_call | solution.py:489
  54.9 1.1 collective-permute-start.15
  56.0 1.5 %collective-permute-start.16 = (bf16[256,512]{1,0:T(8,128)(2,1)S(1)}, bf16[256,512]{1,0:T(8,128)(2,1)S(1)}, u32[]{:S(2)}, u32[]{:S(2)}) collective-permute-start(bf16[256,512]{1,0:T(8,128)(2,1)S(1)} %get-tuple-element.88), channel_id=1, source_target_pairs={{0,8},{8,0},{16,24},{24,16},{1,9},{9,1},{17,25},{25,17},{2,10},{10... | collective-permute-start | bytes 786440 | tf_op jit(solution)/shard_map/ppermute | solution.py:459
  59.0 5.2 %collective-permute-done.15.refs_4_ = bf16[256,512]{1,0:T(8,128)(2,1)S(1)} collective-permute-done((bf16[256,512]{1,0:T(8,128)(2,1)S(1)}, bf16[256,512]{1,0:T(8,128)(2,1)S(1)}, u32[]{:S(2)}, u32[]{:S(2)}) %collective-permute-start.15) | collective-permute-done | bytes 262176 | tf_op jit(solution)/shard_map/ppermute | solution.py:459
  65.2 4.2 %far_forward.1 = (bf16[512,1024]{1,0:T(8,128)(2,1)S(1)}, bf16[512,1024]{1,0:T(8,128)(2,1)S(1)}, bf16[512,1024]{1,0:T(8,128)(2,1)S(1)}, bf16[512,1024]{1,0:T(8,12...) custom-call(s32[3]{0:T(128)S(1)} %pad_add_fusion.refs_0_, ...), custom_call_target="tpu_custom_call" | custom-call | flops 3221225472 | bytes 1048576 | tf_op jit(solution)/shard_map/far_forward/pallas_call | solution.py:489
  71.6 4.9 %far_backward.1 = (bf16[512,1024]{1,0:T(8,128)(2,1)S(1)}, bf16[512,1024]{1,0:T(8,128)(2,1)S(1)}, bf16[512,1024]{1,0:T(8,128)(2,1)S(1)}, bf16[256,512]{1,0:T(8,12...) custom-call(s32[3]{0:T(128)S(1)} %pad_add_fusion.refs_0_, ...), custom_call_target="tpu_custom_call" | custom-call | flops 3221225472 | bytes 1048576 | tf_op jit(solution)/shard_map/far_backward/pallas_call | solution.py:489
  79.8 1.3 %collective-permute-done.22.refs_3_ = bf16[256,512]{1,0:T(8,128)(2,1)S(1)} collective-permute-done((bf16[256,512]{1,0:T(8,128)(2,1)S(1)}, bf16[256,512]{1,0:T(8,128)(2,1)S(1)}, u32[]{:S(2)}, u32[]{:S(2)}) %collective-permute-start.22) | collective-permute-done | bytes 262176 | tf_op jit(solution)/shard_map/ppermute | solution.py:459
  84.3 4.2 %grad_down.1 = (f32[1024,1024]{1,0:T(8,128)}, f32[8,128]{1,0:T(8,128)S(1)}) custom-call(bf16[512,1024]{1,0:T(8,128)(2,1)S(1)} %get-tuple-element.86.refs_2_.left_a, bf16[512,1024]{1,0:T(8,128)(2,1)S(1)} %get-tuple-element.101.left_b, bf16[512,1024]{1,0:T(8,128)(2,1)S(1)} %get-tuple-element.102.right_a, bf16[512,1024]{1,0:T(8,128)(2,1)S(1)} %get-tuple-element.103.right_b, ...), custom_call_target="tpu_custom_call" | custom-call | flops 20000000000 | bytes 1 | tf_op jit(solution)/shard_map/grad_down/pallas_call | solution.py:631
  90.7 2.2 %collective-permute-done.25.refs_1_ = bf16[256,256]{1,0:T(8,128)(2,1)S(1)} collective-permute-done((bf16[256,256]{1,0:T(8,128)(2,1)S(1)}, bf16[256,256]{1,0:T(8,128)(2,1)S(1)}, u32[]{:S(2)}, u32[]{:S(2)}) %collective-permute-start.25) | collective-permute-done | bytes 131104 | tf_op jit(solution)/shard_map/ppermute | solution.py:459
  93.8 4.3 %collective-permute-start.28 = (bf16[256,256]{1,0:T(8,128)(2,1)S(1)}, bf16[256,256]{1,0:T(8,128)(2,1)S(1)}, u32[]{:S(2)}, u32[]{:S(2)}) collective-permute-start(bf16[256,256]{1,0:T(8,128)(2,1)S(1)} %get-tuple-element.117.after), channel_id=1, source_target_pairs={{0,4},{1,5},{2,6},{3,7},{4,0},{5,1},{6,2},{7,3},{8,12},{9,13},{10,... | collective-permute-start | bytes 393224 | tf_op jit(solution)/shard_map/ppermute | solution.py:459
  98.1 4.2 %grad_gate.1 = (f32[1024,1024]{1,0:T(8,128)}, f32[8,128]{1,0:T(8,128)S(1)}) custom-call(bf16[512,1024]{1,0:T(8,128)(2,1)S(1)} %get-tuple-element.112.left_a, bf16[512,1024]{1,0:T(8,128)(2,1)S(1)} %get-tuple-element.113.left_b, bf16[512,1024]{1,0:T(8,128)(2,1)S(1)} %get-tuple-element.114.right_a, bf16[512,1024]{1,0:T(8,128)(2,1)S(1)} %get-tuple-element.93.refs_4_.right_b, ...), custom_call_target="tpu_custom_call" | custom-call | flops 20000000000 | bytes 1 | tf_op jit(solution)/shard_map/grad_gate/pallas_call | solution.py:631
  102.3 1.4 %collective-permute-start.29 = (bf16[256,256]{1,0:T(8,128)(2,1)S(1)}, bf16[256,256]{1,0:T(8,128)(2,1)S(1)}, u32[]{:S(2)}, u32[]{:S(2)}) collective-permute-start(bf16[256,256]{1,0:T(8,128)(2,1)S(1)} %get-tuple-element.122), channel_id=1, source_target_pairs={{0,6},{1,7},{2,4},{3,5},{4,2},{5,3},{6,0},{7,1},{8,14},{9,15},{10,... | collective-permute-start | bytes 393224 | tf_op jit(solution)/shard_map/ppermute | solution.py:459
  103.8 2.5 %collective-permute-start.32 = (bf16[256,256]{1,0:T(8,128)(2,1)S(1)}, bf16[256,256]{1,0:T(8,128)(2,1)S(1)}, u32[]{:S(2)}, u32[]{:S(2)}) collective-permute-start(bf16[256,256]{1,0:T(8,128)(2,1)S(1)} %get-tuple-element.129), channel_id=1, source_target_pairs={{0,6},{1,7},{2,4},{3,5},{4,2},{5,3},{6,0},{7,1},{8,14},{9,15},{10,... | collective-permute-start | bytes 393224 | tf_op jit(solution)/shard_map/ppermute | solution.py:459
  106.4 2.0 %collective-permute-start.27 = (bf16[256,512]{1,0:T(8,128)(2,1)S(1)}, bf16[256,512]{1,0:T(8,128)(2,1)S(1)}, u32[]{:S(2)}, u32[]{:S(2)}) collective-permute-start(bf16[256,512]{1,0:T(8,128)(2,1)S(1)} %get-tuple-element.121), channel_id=1, source_target_pairs={{0,2},{1,3},{2,0},{3,1},{4,6},{5,7},{6,4},{7,5},{8,10},{9,11},{10,... | collective-permute-start | bytes 786440 | tf_op jit(solution)/shard_map/ppermute | solution.py:459
  108.4 4.2 %grad_up.1 = (f32[1024,1024]{1,0:T(8,128)}, f32[8,128]{1,0:T(8,128)S(1)}) custom-call(bf16[512,1024]{1,0:T(8,128)(2,1)S(1)} %get-tuple-element.112.left_a, bf16[512,1024]{1,0:T(8,128)(2,1)S(1)} %get-tuple-element.113.left_b, bf16[512,1024]{1,0:T(8,128)(2,1)S(1)} %get-tuple-element.124.right_a, bf16[512,1024]{1,0:T(8,128)(2,1)S(1)} %get-tuple-element.125.right_b, ...), custom_call_target="tpu_custom_call" | custom-call | flops 20000000000 | bytes 1 | tf_op jit(solution)/shard_map/grad_up/pallas_call | solution.py:631
  112.6 3.0 %collective-permute-done.27.refs_1_ = bf16[256,512]{1,0:T(8,128)(2,1)S(1)} collective-permute-done((bf16[256,512]{1,0:T(8,128)(2,1)S(1)}, bf16[256,512]{1,0:T(8,128)(2,1)S(1)}, u32[]{:S(2)}, u32[]{:S(2)}) %collective-permute-start.27) | collective-permute-done | bytes 262176 | tf_op jit(solution)/shard_map/ppermute | solution.py:459
  115.6 1.1 combine_out.1
  116.8 1.2 collective-permute-done.33
  119.7 1.3 %collective-permute-start.37 = (f32[2,256]{1,0:T(2,128)S(1)}, f32[2,256]{1,0:T(2,128)S(1)}, u32[]{:S(2)}, u32[]{:S(2)}) collective-permute-start(f32[2,256]{1,0:T(2,128)S(1)} %slice.3), channel_id=1, source_target_pairs={{0,24},{8,16},{16,8},{24,0},{1,25},{9,17},{17,9},{25,1},{2,26},{10... | collective-permute-start | bytes 6152 | tf_op jit(solution)/shard_map/ppermute | solution.py:459
  121.1 1.5 %collective-permute-start.35 = (f32[2,256]{1,0:T(2,128)S(1)}, f32[2,256]{1,0:T(2,128)S(1)}, u32[]{:S(2)}, u32[]{:S(2)}) collective-permute-start(f32[2,256]{1,0:T(2,128)S(1)} %slice.3), channel_id=1, source_target_pairs={{0,8},{8,0},{16,24},{24,16},{1,9},{9,1},{17,25},{25,17},{2,10},{10... | collective-permute-start | bytes 6152 | tf_op jit(solution)/shard_map/ppermute | solution.py:459
  (81 shorter events, 29.1 us)
Async XLA Ops:
  6.0 15.4 %collective-permute-start.4 = (bf16[272,512]{1,0:T(8,128)(2,1)S(1)}, bf16[272,512]{1,0:T(8,128)(2,1)S(1)}, u32[]{:S(2)}, u32[]{:S(2)}) collective-permute-start(bf16[272,512]{1,0:T(8,128)(2,1)S(1)} %get-tuple-element.73), channel_id=1, source_target_pairs={{0,2},{1,3},{2,0},{3,1},{4,6},{5,7},{6,4},{7,5},{8,10},{9,11},{10,... | collective-permute-start | bytes 835592 | tf_op jit(solution)/shard_map/ppermute | solution.py:459
  8.8 22.4 %collective-permute-start.7 = (bf16[272,512]{1,0:T(8,128)(2,1)S(1)}, bf16[272,512]{1,0:T(8,128)(2,1)S(1)}, u32[]{:S(2)}, u32[]{:S(2)}) collective-permute-start(bf16[272,512]{1,0:T(8,128)(2,1)S(1)} %get-tuple-element.74), channel_id=1, source_target_pairs={{0,4},{1,5},{2,6},{3,7},{4,0},{5,1},{6,2},{7,3},{8,12},{9,13},{10,... | collective-permute-start | bytes 835592 | tf_op jit(solution)/shard_map/ppermute | solution.py:459
  11.4 19.8 %collective-permute-start.8 = (bf16[272,512]{1,0:T(8,128)(2,1)S(1)}, bf16[272,512]{1,0:T(8,128)(2,1)S(1)}, u32[]{:S(2)}, u32[]{:S(2)}) collective-permute-start(bf16[272,512]{1,0:T(8,128)(2,1)S(1)} %get-tuple-element.75), channel_id=1, source_target_pairs={{0,6},{1,7},{2,4},{3,5},{4,2},{5,3},{6,0},{7,1},{8,14},{9,15},{10,... | collective-permute-start | bytes 835592 | tf_op jit(solution)/shard_map/ppermute | solution.py:459
  21.4 13.7 %collective-permute-start.6 = (bf16[512,512]{1,0:T(8,128)(2,1)S(1)}, bf16[512,512]{1,0:T(8,128)(2,1)S(1)}, u32[]{:S(2)}, u32[]{:S(2)}) collective-permute-start(bf16[512,512]{1,0:T(8,128)(2,1)S(1)} %join_near.1.after.refs_1_), channel_id=1, source_target_pairs={{0,16},{8,24},{16,0},{24,8},{1,17},{9,25},{17,1},{25,9},{2,18},{10... | collective-permute-start | bytes 1572872 | tf_op jit(solution)/shard_map/ppermute | solution.py:459
  23.2 13.1 %collective-permute-start.5 = (bf16[512,512]{1,0:T(8,128)(2,1)S(1)}, bf16[512,512]{1,0:T(8,128)(2,1)S(1)}, u32[]{:S(2)}, u32[]{:S(2)}) collective-permute-start(bf16[512,512]{1,0:T(8,128)(2,1)S(1)} %join_near.1.after.refs_1_), channel_id=1, source_target_pairs={{0,8},{8,0},{16,24},{24,16},{1,9},{9,1},{17,25},{25,17},{2,10},{10... | collective-permute-start | bytes 1572872 | tf_op jit(solution)/shard_map/ppermute | solution.py:459
  36.3 9.3 %collective-permute-start.9 = (bf16[256,512]{1,0:T(8,128)(2,1)S(1)}, bf16[256,512]{1,0:T(8,128)(2,1)S(1)}, u32[]{:S(2)}, u32[]{:S(2)}) collective-permute-start(bf16[256,512]{1,0:T(8,128)(2,1)S(1)} %get-tuple-element.77), channel_id=1, source_target_pairs={{0,16},{8,24},{16,0},{24,8},{1,17},{9,25},{17,1},{25,9},{2,18},{10... | collective-permute-start | bytes 786440 | tf_op jit(solution)/shard_map/ppermute | solution.py:459
  37.0 9.2 %collective-permute-start.10 = (bf16[256,512]{1,0:T(8,128)(2,1)S(1)}, bf16[256,512]{1,0:T(8,128)(2,1)S(1)}, u32[]{:S(2)}, u32[]{:S(2)}) collective-permute-start(bf16[256,512]{1,0:T(8,128)(2,1)S(1)} %get-tuple-element.78), channel_id=1, source_target_pairs={{0,8},{8,0},{16,24},{24,16},{1,9},{9,1},{17,25},{25,17},{2,10},{10... | collective-permute-start | bytes 786440 | tf_op jit(solution)/shard_map/ppermute | solution.py:459
  38.4 15.8 %collective-permute-start.14 = (bf16[512,512]{1,0:T(8,128)(2,1)S(1)}, bf16[512,512]{1,0:T(8,128)(2,1)S(1)}, u32[]{:S(2)}, u32[]{:S(2)}) collective-permute-start(bf16[512,512]{1,0:T(8,128)(2,1)S(1)} %join_far.1.refs_2_.refs_1_), channel_id=1, source_target_pairs={{0,16},{8,24},{16,0},{24,8},{1,17},{9,25},{17,1},{25,9},{2,18},{10... | collective-permute-start | bytes 1572872 | tf_op jit(solution)/shard_map/ppermute | solution.py:459
  39.9 15.0 %collective-permute-start.13 = (bf16[512,512]{1,0:T(8,128)(2,1)S(1)}, bf16[512,512]{1,0:T(8,128)(2,1)S(1)}, u32[]{:S(2)}, u32[]{:S(2)}) collective-permute-start(bf16[512,512]{1,0:T(8,128)(2,1)S(1)} %join_far.1.refs_2_.refs_1_), channel_id=1, source_target_pairs={{0,8},{8,0},{16,24},{24,16},{1,9},{9,1},{17,25},{25,17},{2,10},{10... | collective-permute-start | bytes 1572872 | tf_op jit(solution)/shard_map/ppermute | solution.py:459
  54.9 9.3 %collective-permute-start.15 = (bf16[256,512]{1,0:T(8,128)(2,1)S(1)}, bf16[256,512]{1,0:T(8,128)(2,1)S(1)}, u32[]{:S(2)}, u32[]{:S(2)}) collective-permute-start(bf16[256,512]{1,0:T(8,128)(2,1)S(1)} %get-tuple-element.87), channel_id=1, source_target_pairs={{0,16},{8,24},{16,0},{24,8},{1,17},{9,25},{17,1},{25,9},{2,18},{10... | collective-permute-start | bytes 786440 | tf_op jit(solution)/shard_map/ppermute | solution.py:459
  56.0 9.2 %collective-permute-start.16 = (bf16[256,512]{1,0:T(8,128)(2,1)S(1)}, bf16[256,512]{1,0:T(8,128)(2,1)S(1)}, u32[]{:S(2)}, u32[]{:S(2)}) collective-permute-start(bf16[256,512]{1,0:T(8,128)(2,1)S(1)} %get-tuple-element.88), channel_id=1, source_target_pairs={{0,8},{8,0},{16,24},{24,16},{1,9},{9,1},{17,25},{25,17},{2,10},{10... | collective-permute-start | bytes 786440 | tf_op jit(solution)/shard_map/ppermute | solution.py:459
  57.5 20.0 %collective-permute-start.11 = (bf16[256,1024]{1,0:T(8,128)(2,1)S(1)}, bf16[256,1024]{1,0:T(8,128)(2,1)S(1)}, u32[]{:S(2)}, u32[]{:S(2)}) collective-permute-start(bf16[256,1024]{1,0:T(8,128)(2,1)S(1)} %get-tuple-element.83), channel_id=1, source_target_pairs={{0,8},{8,0},{16,24},{24,16},{1,9},{9,1},{17,25},{25,17},{2,10},{10... | collective-permute-start | bytes 1572872 | tf_op jit(solution)/shard_map/ppermute | solution.py:459
  58.0 20.5 %collective-permute-start.12 = (bf16[256,1024]{1,0:T(8,128)(2,1)S(1)}, bf16[256,1024]{1,0:T(8,128)(2,1)S(1)}, u32[]{:S(2)}, u32[]{:S(2)}) collective-permute-start(bf16[256,1024]{1,0:T(8,128)(2,1)S(1)} %get-tuple-element.85), channel_id=1, source_target_pairs={{0,16},{8,24},{16,0},{24,8},{1,17},{9,25},{17,1},{25,9},{2,18},{10... | collective-permute-start | bytes 1572872 | tf_op jit(solution)/shard_map/ppermute | solution.py:459
  69.4 11.6 %collective-permute-start.22 = (bf16[256,512]{1,0:T(8,128)(2,1)S(1)}, bf16[256,512]{1,0:T(8,128)(2,1)S(1)}, u32[]{:S(2)}, u32[]{:S(2)}) collective-permute-start(bf16[256,512]{1,0:T(8,128)(2,1)S(1)} %get-tuple-element.106), channel_id=1, source_target_pairs={{0,16},{8,24},{16,0},{24,8},{1,17},{9,25},{17,1},{25,9},{2,18},{10... | collective-permute-start | bytes 786440 | tf_op jit(solution)/shard_map/ppermute | solution.py:459
  70.5 11.6 %collective-permute-start.21 = (bf16[256,512]{1,0:T(8,128)(2,1)S(1)}, bf16[256,512]{1,0:T(8,128)(2,1)S(1)}, u32[]{:S(2)}, u32[]{:S(2)}) collective-permute-start(bf16[256,512]{1,0:T(8,128)(2,1)S(1)} %get-tuple-element.92.refs_12_), channel_id=1, source_target_pairs={{0,8},{8,0},{16,24},{24,16},{1,9},{9,1},{17,25},{25,17},{2,10},{10... | collective-permute-start | bytes 786440 | tf_op jit(solution)/shard_map/ppermute | solution.py:459
  76.5 12.1 %collective-permute-start.19 = (bf16[256,512]{1,0:T(8,128)(2,1)S(1)}, bf16[256,512]{1,0:T(8,128)(2,1)S(1)}, u32[]{:S(2)}, u32[]{:S(2)}) collective-permute-start(bf16[256,512]{1,0:T(8,128)(2,1)S(1)} %get-tuple-element.98), channel_id=1, source_target_pairs={{0,8},{8,0},{16,24},{24,16},{1,9},{9,1},{17,25},{25,17},{2,10},{10... | collective-permute-start | bytes 786440 | tf_op jit(solution)/shard_map/ppermute | solution.py:459
  77.5 12.0 %collective-permute-start.20 = (bf16[256,512]{1,0:T(8,128)(2,1)S(1)}, bf16[256,512]{1,0:T(8,128)(2,1)S(1)}, u32[]{:S(2)}, u32[]{:S(2)}) collective-permute-start(bf16[256,512]{1,0:T(8,128)(2,1)S(1)} %get-tuple-element.100), channel_id=1, source_target_pairs={{0,16},{8,24},{16,0},{24,8},{1,17},{9,25},{17,1},{25,9},{2,18},{10... | collective-permute-start | bytes 786440 | tf_op jit(solution)/shard_map/ppermute | solution.py:459
  78.7 27.6 %collective-permute-start.17 = (bf16[256,512]{1,0:T(8,128)(2,1)S(1)}, bf16[256,512]{1,0:T(8,128)(2,1)S(1)}, u32[]{:S(2)}, u32[]{:S(2)}) collective-permute-start(bf16[256,512]{1,0:T(8,128)(2,1)S(1)} %get-tuple-element.95), channel_id=1, source_target_pairs={{0,16},{8,24},{16,0},{24,8},{1,17},{9,25},{17,1},{25,9},{2,18},{10... | collective-permute-start | bytes 786440 | tf_op jit(solution)/shard_map/ppermute | solution.py:459
  82.2 10.7 %collective-permute-start.25 = (bf16[256,256]{1,0:T(8,128)(2,1)S(1)}, bf16[256,256]{1,0:T(8,128)(2,1)S(1)}, u32[]{:S(2)}, u32[]{:S(2)}) collective-permute-start(bf16[256,256]{1,0:T(8,128)(2,1)S(1)} %get-tuple-element.115), channel_id=1, source_target_pairs={{0,16},{8,24},{16,0},{24,8},{1,17},{9,25},{17,1},{25,9},{2,18},{10... | collective-permute-start | bytes 393224 | tf_op jit(solution)/shard_map/ppermute | solution.py:459
  83.3 10.5 %collective-permute-start.26 = (bf16[256,256]{1,0:T(8,128)(2,1)S(1)}, bf16[256,256]{1,0:T(8,128)(2,1)S(1)}, u32[]{:S(2)}, u32[]{:S(2)}) collective-permute-start(bf16[256,256]{1,0:T(8,128)(2,1)S(1)} %get-tuple-element.116), channel_id=1, source_target_pairs={{0,8},{8,0},{16,24},{24,16},{1,9},{9,1},{17,25},{25,17},{2,10},{10... | collective-permute-start | bytes 393224 | tf_op jit(solution)/shard_map/ppermute | solution.py:459
  88.5 17.8 %collective-permute-start.18 = (bf16[256,512]{1,0:T(8,128)(2,1)S(1)}, bf16[256,512]{1,0:T(8,128)(2,1)S(1)}, u32[]{:S(2)}, u32[]{:S(2)}) collective-permute-start(bf16[256,512]{1,0:T(8,128)(2,1)S(1)} %get-tuple-element.96), channel_id=1, source_target_pairs={{0,8},{8,0},{16,24},{24,16},{1,9},{9,1},{17,25},{25,17},{2,10},{10... | collective-permute-start | bytes 786440 | tf_op jit(solution)/shard_map/ppermute | solution.py:459
  89.6 12.7 %collective-permute-start.23 = (bf16[256,256]{1,0:T(8,128)(2,1)S(1)}, bf16[256,256]{1,0:T(8,128)(2,1)S(1)}, u32[]{:S(2)}, u32[]{:S(2)}) collective-permute-start(bf16[256,256]{1,0:T(8,128)(2,1)S(1)} %get-tuple-element.110), channel_id=1, source_target_pairs={{0,16},{8,24},{16,0},{24,8},{1,17},{9,25},{17,1},{25,9},{2,18},{10... | collective-permute-start | bytes 393224 | tf_op jit(solution)/shard_map/ppermute | solution.py:459
  92.9 10.8 %collective-permute-start.24 = (bf16[256,256]{1,0:T(8,128)(2,1)S(1)}, bf16[256,256]{1,0:T(8,128)(2,1)S(1)}, u32[]{:S(2)}, u32[]{:S(2)}) collective-permute-start(bf16[256,256]{1,0:T(8,128)(2,1)S(1)} %get-tuple-element.111), channel_id=1, source_target_pairs={{0,8},{8,0},{16,24},{24,16},{1,9},{9,1},{17,25},{25,17},{2,10},{10... | collective-permute-start | bytes 393224 | tf_op jit(solution)/shard_map/ppermute | solution.py:459
  93.8 18.8 %collective-permute-start.28 = (bf16[256,256]{1,0:T(8,128)(2,1)S(1)}, bf16[256,256]{1,0:T(8,128)(2,1)S(1)}, u32[]{:S(2)}, u32[]{:S(2)}) collective-permute-start(bf16[256,256]{1,0:T(8,128)(2,1)S(1)} %get-tuple-element.117.after), channel_id=1, source_target_pairs={{0,4},{1,5},{2,6},{3,7},{4,0},{5,1},{6,2},{7,3},{8,12},{9,13},{10,... | collective-permute-start | bytes 393224 | tf_op jit(solution)/shard_map/ppermute | solution.py:459
  102.3 10.2 %collective-permute-start.29 = (bf16[256,256]{1,0:T(8,128)(2,1)S(1)}, bf16[256,256]{1,0:T(8,128)(2,1)S(1)}, u32[]{:S(2)}, u32[]{:S(2)}) collective-permute-start(bf16[256,256]{1,0:T(8,128)(2,1)S(1)} %get-tuple-element.122), channel_id=1, source_target_pairs={{0,6},{1,7},{2,4},{3,5},{4,2},{5,3},{6,0},{7,1},{8,14},{9,15},{10,... | collective-permute-start | bytes 393224 | tf_op jit(solution)/shard_map/ppermute | solution.py:459
  103.8 14.2 %collective-permute-start.32 = (bf16[256,256]{1,0:T(8,128)(2,1)S(1)}, bf16[256,256]{1,0:T(8,128)(2,1)S(1)}, u32[]{:S(2)}, u32[]{:S(2)}) collective-permute-start(bf16[256,256]{1,0:T(8,128)(2,1)S(1)} %get-tuple-element.129), channel_id=1, source_target_pairs={{0,6},{1,7},{2,4},{3,5},{4,2},{5,3},{6,0},{7,1},{8,14},{9,15},{10,... | collective-permute-start | bytes 393224 | tf_op jit(solution)/shard_map/ppermute | solution.py:459
  106.3 12.2 %collective-permute-start.31 = (bf16[256,256]{1,0:T(8,128)(2,1)S(1)}, bf16[256,256]{1,0:T(8,128)(2,1)S(1)}, u32[]{:S(2)}, u32[]{:S(2)}) collective-permute-start(bf16[256,256]{1,0:T(8,128)(2,1)S(1)} %get-tuple-element.119.refs_3_), channel_id=1, source_target_pairs={{0,4},{1,5},{2,6},{3,7},{4,0},{5,1},{6,2},{7,3},{8,12},{9,13},{10,... | collective-permute-start | bytes 393224 | tf_op jit(solution)/shard_map/ppermute | solution.py:459
  106.4 9.2 %collective-permute-start.27 = (bf16[256,512]{1,0:T(8,128)(2,1)S(1)}, bf16[256,512]{1,0:T(8,128)(2,1)S(1)}, u32[]{:S(2)}, u32[]{:S(2)}) collective-permute-start(bf16[256,512]{1,0:T(8,128)(2,1)S(1)} %get-tuple-element.121), channel_id=1, source_target_pairs={{0,2},{1,3},{2,0},{3,1},{4,6},{5,7},{6,4},{7,5},{8,10},{9,11},{10,... | collective-permute-start | bytes 786440 | tf_op jit(solution)/shard_map/ppermute | solution.py:459
  119.0 4.1 %collective-permute-start.36 = (f32[2,256]{1,0:T(2,128)S(1)}, f32[2,256]{1,0:T(2,128)S(1)}, u32[]{:S(2)}, u32[]{:S(2)}) collective-permute-start(f32[2,256]{1,0:T(2,128)S(1)} %slice.3), channel_id=1, source_target_pairs={{0,16},{8,24},{16,0},{24,8},{1,17},{9,25},{17,1},{25,9},{2,18},{10... | collective-permute-start | bytes 6152 | tf_op jit(solution)/shard_map/ppermute | solution.py:459
  119.7 4.5 %collective-permute-start.37 = (f32[2,256]{1,0:T(2,128)S(1)}, f32[2,256]{1,0:T(2,128)S(1)}, u32[]{:S(2)}, u32[]{:S(2)}) collective-permute-start(f32[2,256]{1,0:T(2,128)S(1)} %slice.3), channel_id=1, source_target_pairs={{0,24},{8,16},{16,8},{24,0},{1,25},{9,17},{17,9},{25,1},{2,26},{10... | collective-permute-start | bytes 6152 | tf_op jit(solution)/shard_map/ppermute | solution.py:459
  121.1 3.6 %collective-permute-start.35 = (f32[2,256]{1,0:T(2,128)S(1)}, f32[2,256]{1,0:T(2,128)S(1)}, u32[]{:S(2)}, u32[]{:S(2)}) collective-permute-start(f32[2,256]{1,0:T(2,128)S(1)} %slice.3), channel_id=1, source_target_pairs={{0,8},{8,0},{16,24},{24,16},{1,9},{9,1},{17,25},{25,17},{2,10},{10... | collective-permute-start | bytes 6152 | tf_op jit(solution)/shard_map/ppermute | solution.py:459
  122.6 3.3 %collective-permute-start.34 = (bf16[256,256]{1,0:T(8,128)(2,1)S(1)}, bf16[256,256]{1,0:T(8,128)(2,1)S(1)}, u32[]{:S(2)}, u32[]{:S(2)}) collective-permute-start(bf16[256,256]{1,0:T(8,128)(2,1)S(1)} %get-tuple-element.133), channel_id=1, source_target_pairs={{0,1},{1,0},{2,3},{3,2},{4,5},{5,4},{6,7},{7,6},{8,9},{9,8},{10,11... | collective-permute-start | bytes 393224 | tf_op jit(solution)/shard_map/ppermute | solution.py:459
  (11 other events, 38.1 us)

commit v4 on v3

--- a/solution.py
+++ b/solution.py
@@ -471,8 +471,9 @@
     return [pltpu.with_memory_space_constraint(x, pltpu.VMEM) for x in arrays]
 
 
-def grad_kernel(per, feats, y0, y1, y2, y3, info, dots, kept, sent, dots_out):
+def grad_kernel(per, feats, y0, y1, y2, y3, info, dots, here, got, kept, sent, dots_out, mixed):
     back_kernel(per, False, feats, feats, y0, y1, y2, y3, info, kept, sent)
+    mixed[...] = (here[...] + got[...].astype(F32)).astype(BF16)
     dots_out[...] = dots[...]
 
 
@@ -622,7 +623,7 @@
         ids, *far, far_scale, wg, wu, wd, act, slope,
         plan_args=1,
         flops=3 * work,
-        after=out_parts[:1],
+        after=(out_parts[0], near_first[1], near_first[3]),
     )
     dx_first = reduce_first(*dx_parts)
 
@@ -639,8 +640,8 @@
             name=name,
         )(*pin(*left, *right, after))
 
-    near_sums = reduce_second(near_first, (far_dgate,))
-    out_sums = reduce_second(out_first, (near_sums[0],))
+    out_sums = reduce_second(out_first, (far_dgate,))
+    near_sums = reduce_second(near_first, (out_sums[0],))
     grad_down, done_d = weight_grad(
         "grad_down", (near_hid, far_hid), (near_g, far_g), ff, width, out_sums[0]
     )
@@ -666,13 +667,12 @@
         *back_near, *back_out, info, grad_out, par_g,
         after=(done_u,),
     )
-    mixed = (kept + shift(sent, "exp", 1).astype(F32)).astype(BF16)
     dots = kept_dots + shift(sent_dots, "exp", 1)
-    kept, sent, dots = kernel_call(
+    kept, sent, dots, mixed = kernel_call(
         functools.partial(grad_kernel, per, feats),
         "combine_grad",
-        (whole, narrow, few),
-        *back_near, *back_dx, info, dots,
+        (whole, narrow, few, sds((toks, feats), BF16)),
+        *back_near, *back_dx, info, dots, kept, shift(sent, "exp", 1),
     )
     first = dots[0:2]
     second, third, fourth = (shift(first, "rep", k) for k in (1, 2, 3))

time: 127 us -> 124 us (0.976)
  waiting for transfers between devices: 42.6 us -> 40.8 us
    ppermute x38, waiting for transfers between devices: 42.6 us -> 40.8 us  [shift(): return lax.ppermute(x, axis, [(i, i ^ bit) for i in range(n)])]
  transfers between devices with their start and end apart: 38 -> 38, of which waited for: 20 -> 18; matrix products, arithmetic and copies ran while one was open for 1% -> 1% of each run, Pallas kernels for 28% -> 28%
where the time goes in v4:
time: 124 us
  starting transfers between devices  41.9 us (34%)
  waiting for transfers between devices  40.8 us (33%)
  Pallas kernels  38.1 us (31%)
  local copies, waits for them, and re-layouts  1.37 us (1%)
  other arithmetic  1.34 us (1%)
    ppermute x38, starting transfers between devices, shift(): return lax.ppermute(x, axis, [(i, i ^ bit) for i in range(n)])  41.9 us
    ppermute x38, waiting for transfers between devices, shift(): return lax.ppermute(x, axis, [(i, i ^ bit) for i in range(n)])  40.8 us
    pallas_call x17, Pallas kernels, kernel_call(): pl.pallas_call(run, in_specs=[smem()] * plan_args + [vmem()] * (count - p...  22.6 us
    pallas_call x3, Pallas kernels, weight_grad(): pl.pallas_call(weights_kernel, grid=(steps,), in_specs=[vmem()] * 5, out_...  12.6 us
    pallas_call x1, Pallas kernels, on_quad(): pl.pallas_call(load_kernel, in_specs=[pl.BlockSpec(memory_space=pltpu.HBM...  2.88 us
  transfers between devices with their start and end apart: 38, of which 18 were waited for; matrix products, arithmetic and copies ran while one was open for 1% of the time, Pallas kernels for 28%

profile of v4, /device:TPU:0, one launch (start us, length us, event | category | flops | bytes accessed | tf_op | source)
XLA Modules:
  0.0 124.3 jit_solution(4439362373509510650)
XLA Ops:
  4.4 1.6 %send.1 = (bf16[256,512]{1,0:T(8,128)(2,1)S(1)}, bf16[272,512]{1,0:T(8,128)(2,1)S(1)}, bf16[272,512]{1,0:T(8,128)(2,1)S(1)}, bf16[272,512]{1,0:T(8,128)(2,1)S(1)}) custom-call(s32[3]{0:T(128)S(1)} %pad_add_fusion.refs_0_, bf16[256,256]{1,0:T(8,128)(2,1)} %refs_1_.2, bf16[256,256]{1,0:T(8,128)(2,1)} %refs_5_.1, s32[2,256]{1,0:T(2,128)S(1)} %bitcast.14, ...), custom_call_target="tpu_custom_call" | custom-call | flops 1 | bytes 1048576 | tf_op jit(solution)/shard_map/send/pallas_call | solution.py:490
  6.0 2.8 %collective-permute-start.4 = (bf16[272,512]{1,0:T(8,128)(2,1)S(1)}, bf16[272,512]{1,0:T(8,128)(2,1)S(1)}, u32[]{:S(2)}, u32[]{:S(2)}) collective-permute-start(bf16[272,512]{1,0:T(8,128)(2,1)S(1)} %get-tuple-element.74), channel_id=1, source_target_pairs={{0,2},{1,3},{2,0},{3,1},{4,6},{5,7},{6,4},{7,5},{8,10},{9,11},{10,... | collective-permute-start | bytes 835592 | tf_op jit(solution)/shard_map/ppermute | solution.py:459
  8.8 2.6 %collective-permute-start.7 = (bf16[272,512]{1,0:T(8,128)(2,1)S(1)}, bf16[272,512]{1,0:T(8,128)(2,1)S(1)}, u32[]{:S(2)}, u32[]{:S(2)}) collective-permute-start(bf16[272,512]{1,0:T(8,128)(2,1)S(1)} %get-tuple-element.75), channel_id=1, source_target_pairs={{0,4},{1,5},{2,6},{3,7},{4,0},{5,1},{6,2},{7,3},{8,12},{9,13},{10,... | collective-permute-start | bytes 835592 | tf_op jit(solution)/shard_map/ppermute | solution.py:459
  11.4 10.0 %collective-permute-done.4.refs_1_.refs_7_ = bf16[272,512]{1,0:T(8,128)(2,1)S(1)} collective-permute-done((bf16[272,512]{1,0:T(8,128)(2,1)S(1)}, bf16[272,512]{1,0:T(8,128)(2,1)S(1)}, u32[]{:S(2)}, u32[]{:S(2)}) %collective-permute-start.4) | collective-permute-done | bytes 278560 | tf_op jit(solution)/shard_map/ppermute | solution.py:459
  21.4 1.7 %collective-permute-start.6 = (bf16[512,512]{1,0:T(8,128)(2,1)S(1)}, bf16[512,512]{1,0:T(8,128)(2,1)S(1)}, u32[]{:S(2)}, u32[]{:S(2)}) collective-permute-start(bf16[512,512]{1,0:T(8,128)(2,1)S(1)} %join_near.1.after.refs_1_), channel_id=1, source_target_pairs={{0,16},{8,24},{16,0},{24,8},{1,17},{9,25},{17,1},{25,9},{2,18},{10... | collective-permute-start | bytes 1572872 | tf_op jit(solution)/shard_map/ppermute | solution.py:459
  23.2 1.5 %collective-permute-start.5 = (bf16[512,512]{1,0:T(8,128)(2,1)S(1)}, bf16[512,512]{1,0:T(8,128)(2,1)S(1)}, u32[]{:S(2)}, u32[]{:S(2)}) collective-permute-start(bf16[512,512]{1,0:T(8,128)(2,1)S(1)} %join_near.1.after.refs_1_), channel_id=1, source_target_pairs={{0,8},{8,0},{16,24},{24,16},{1,9},{9,1},{17,25},{25,17},{2,10},{10... | collective-permute-start | bytes 1572872 | tf_op jit(solution)/shard_map/ppermute | solution.py:459
  24.7 2.9 %load_weights.1 = (bf16[1024,1024]{1,0:T(8,128)(2,1)S(1)}, bf16[1024,1024]{1,0:T(8,128)(2,1)S(1)}, bf16[1024,1024]{1,0:T(8,128)(2,1)S(1)}) custom-call(bf16[1024,1024]{1,0:T(8,128)(2,1)} %bitcast.19, bf16[1024,1024]{1,0:T(8,128)(2,1)} %bitcast.20, bf16[1024,1024]{1,0:T(8,128)(2,1)} %bitcast.21, bf16[512,512]{1,0:T(8,128)(2,1)S(1)} %join_near.1.after.refs_1_), custom_call_target="tpu_custom_call" | custom-call | flops 20000000000 | bytes 25165824 | tf_op jit(solution)/shard_map/load_weights/pallas_call | solution.py:574
  27.6 3.6 %collective-permute-done.7.refs_0_.refs_8_ = bf16[272,512]{1,0:T(8,128)(2,1)S(1)} collective-permute-done((bf16[272,512]{1,0:T(8,128)(2,1)S(1)}, bf16[272,512]{1,0:T(8,128)(2,1)S(1)}, u32[]{:S(2)}, u32[]{:S(2)}) %collective-permute-start.7) | collective-permute-done | bytes 278560 | tf_op jit(solution)/shard_map/ppermute | solution.py:459
  31.2 4.0 %collective-permute-done.6.refs_1_.refs_3_ = bf16[512,512]{1,0:T(8,128)(2,1)S(1)} collective-permute-done((bf16[512,512]{1,0:T(8,128)(2,1)S(1)}, bf16[512,512]{1,0:T(8,128)(2,1)S(1)}, u32[]{:S(2)}, u32[]{:S(2)}) %collective-permute-start.6) | collective-permute-done | bytes 524320 | tf_op jit(solution)/shard_map/ppermute | solution.py:459
  38.4 1.5 %collective-permute-start.14 = (bf16[512,512]{1,0:T(8,128)(2,1)S(1)}, bf16[512,512]{1,0:T(8,128)(2,1)S(1)}, u32[]{:S(2)}, u32[]{:S(2)}) collective-permute-start(bf16[512,512]{1,0:T(8,128)(2,1)S(1)} %join_far.1.refs_2_.refs_1_), channel_id=1, source_target_pairs={{0,16},{8,24},{16,0},{24,8},{1,17},{9,25},{17,1},{25,9},{2,18},{10... | collective-permute-start | bytes 1572872 | tf_op jit(solution)/shard_map/ppermute | solution.py:459
  41.5 4.2 %collective-permute-done.9.refs_4_ = bf16[256,512]{1,0:T(8,128)(2,1)S(1)} collective-permute-done((bf16[256,512]{1,0:T(8,128)(2,1)S(1)}, bf16[256,512]{1,0:T(8,128)(2,1)S(1)}, u32[]{:S(2)}, u32[]{:S(2)}) %collective-permute-start.9) | collective-permute-done | bytes 262176 | tf_op jit(solution)/shard_map/ppermute | solution.py:459
  46.3 7.7 %near.1 = (bf16[512,1024]{1,0:T(8,128)(2,1)S(1)}, bf16[512,1024]{1,0:T(8,128)(2,1)S(1)}, bf16[512,1024]{1,0:T(8,128)(2,1)S(1)}, bf16[512,1024]{1,0:T(8,128)(2,1)...) custom-call(s32[3]{0:T(128)S(1)} %pad_add_fusion.refs_0_, ...), custom_call_target="tpu_custom_call" | custom-call | flops 6442450944 | bytes 1048576 | tf_op jit(solution)/shard_map/near/pallas_call | solution.py:490
  56.0 1.5 %collective-permute-start.16 = (bf16[256,512]{1,0:T(8,128)(2,1)S(1)}, bf16[256,512]{1,0:T(8,128)(2,1)S(1)}, u32[]{:S(2)}, u32[]{:S(2)}) collective-permute-start(bf16[256,512]{1,0:T(8,128)(2,1)S(1)} %get-tuple-element.89), channel_id=1, source_target_pairs={{0,8},{8,0},{16,24},{24,16},{1,9},{9,1},{17,25},{25,17},{2,10},{10... | collective-permute-start | bytes 786440 | tf_op jit(solution)/shard_map/ppermute | solution.py:459
  59.0 5.2 %collective-permute-done.15.refs_4_ = bf16[256,512]{1,0:T(8,128)(2,1)S(1)} collective-permute-done((bf16[256,512]{1,0:T(8,128)(2,1)S(1)}, bf16[256,512]{1,0:T(8,128)(2,1)S(1)}, u32[]{:S(2)}, u32[]{:S(2)}) %collective-permute-start.15) | collective-permute-done | bytes 262176 | tf_op jit(solution)/shard_map/ppermute | solution.py:459
  65.2 4.2 %far_forward.1 = (bf16[512,1024]{1,0:T(8,128)(2,1)S(1)}, bf16[512,1024]{1,0:T(8,128)(2,1)S(1)}, bf16[512,1024]{1,0:T(8,128)(2,1)S(1)}, bf16[512,1024]{1,0:T(8,12...) custom-call(s32[3]{0:T(128)S(1)} %pad_add_fusion.refs_0_, ...), custom_call_target="tpu_custom_call" | custom-call | flops 3221225472 | bytes 1048576 | tf_op jit(solution)/shard_map/far_forward/pallas_call | solution.py:490
  71.6 3.5 %collective-permute-done.11.refs_13_.refs_1_ = bf16[256,1024]{1,0:T(8,128)(2,1)S(1)} collective-permute-done((bf16[256,1024]{1,0:T(8,128)(2,1)S(1)}, bf16[256,1024]{1,0:T(8,128)(2,1)S(1)}, u32[]{:S(2)}, u32[]{:S(2)}) %collective-permute-start.11) | collective-permute-done | bytes 524320 | tf_op jit(solution)/shard_map/ppermute | solution.py:459
  75.1 4.9 %far_backward.1 = (bf16[512,1024]{1,0:T(8,128)(2,1)S(1)}, bf16[512,1024]{1,0:T(8,128)(2,1)S(1)}, bf16[512,1024]{1,0:T(8,128)(2,1)S(1)}, bf16[256,512]{1,0:T(8,12...) custom-call(s32[3]{0:T(128)S(1)} %pad_add_fusion.refs_0_, ...), custom_call_target="tpu_custom_call" | custom-call | flops 3221225472 | bytes 1048576 | tf_op jit(solution)/shard_map/far_backward/pallas_call | solution.py:490
  80.0 1.6 %collective-permute-start.21 = (bf16[256,512]{1,0:T(8,128)(2,1)S(1)}, bf16[256,512]{1,0:T(8,128)(2,1)S(1)}, u32[]{:S(2)}, u32[]{:S(2)}) collective-permute-start(bf16[256,512]{1,0:T(8,128)(2,1)S(1)} %get-tuple-element.103), channel_id=1, source_target_pairs={{0,8},{8,0},{16,24},{24,16},{1,9},{9,1},{17,25},{25,17},{2,10},{10... | collective-permute-start | bytes 786440 | tf_op jit(solution)/shard_map/ppermute | solution.py:459
  82.3 1.5 %collective-permute-start.25 = (bf16[256,256]{1,0:T(8,128)(2,1)S(1)}, bf16[256,256]{1,0:T(8,128)(2,1)S(1)}, u32[]{:S(2)}, u32[]{:S(2)}) collective-permute-start(bf16[256,256]{1,0:T(8,128)(2,1)S(1)} %get-tuple-element.116), channel_id=1, source_target_pairs={{0,16},{8,24},{16,0},{24,8},{1,17},{9,25},{17,1},{25,9},{2,18},{10... | collective-permute-start | bytes 393224 | tf_op jit(solution)/shard_map/ppermute | solution.py:459
  84.6 1.4 %collective-permute-start.19 = (bf16[256,512]{1,0:T(8,128)(2,1)S(1)}, bf16[256,512]{1,0:T(8,128)(2,1)S(1)}, u32[]{:S(2)}, u32[]{:S(2)}) collective-permute-start(bf16[256,512]{1,0:T(8,128)(2,1)S(1)} %get-tuple-element.100), channel_id=1, source_target_pairs={{0,16},{8,24},{16,0},{24,8},{1,17},{9,25},{17,1},{25,9},{2,18},{10... | collective-permute-start | bytes 786440 | tf_op jit(solution)/shard_map/ppermute | solution.py:459
  86.0 4.2 %grad_down.1 = (f32[1024,1024]{1,0:T(8,128)}, f32[8,128]{1,0:T(8,128)S(1)}) custom-call(bf16[512,1024]{1,0:T(8,128)(2,1)S(1)} %get-tuple-element.87.refs_2_.left_a, bf16[512,1024]{1,0:T(8,128)(2,1)S(1)} %get-tuple-element.106.left_b, bf16[512,1024]{1,0:T(8,128)(2,1)S(1)} %get-tuple-element.107.right_a, bf16[512,1024]{1,0:T(8,128)(2,1)S(1)} %get-tuple-element.108.right_b, ...), custom_call_target="tpu_custom_call" | custom-call | flops 20000000000 | bytes 1 | tf_op jit(solution)/shard_map/grad_down/pallas_call | solution.py:632
  91.1 1.5 %collective-permute-start.23 = (bf16[256,256]{1,0:T(8,128)(2,1)S(1)}, bf16[256,256]{1,0:T(8,128)(2,1)S(1)}, u32[]{:S(2)}, u32[]{:S(2)}) collective-permute-start(bf16[256,256]{1,0:T(8,128)(2,1)S(1)} %get-tuple-element.111), channel_id=1, source_target_pairs={{0,16},{8,24},{16,0},{24,8},{1,17},{9,25},{17,1},{25,9},{2,18},{10... | collective-permute-start | bytes 393224 | tf_op jit(solution)/shard_map/ppermute | solution.py:459
  93.2 3.5 %collective-permute-start.30 = (bf16[256,256]{1,0:T(8,128)(2,1)S(1)}, bf16[256,256]{1,0:T(8,128)(2,1)S(1)}, u32[]{:S(2)}, u32[]{:S(2)}) collective-permute-start(bf16[256,256]{1,0:T(8,128)(2,1)S(1)} %get-tuple-element.118.after), channel_id=1, source_target_pairs={{0,4},{1,5},{2,6},{3,7},{4,0},{5,1},{6,2},{7,3},{8,12},{9,13},{10,... | collective-permute-start | bytes 393224 | tf_op jit(solution)/shard_map/ppermute | solution.py:459
  96.7 4.2 %grad_gate.1 = (f32[1024,1024]{1,0:T(8,128)}, f32[8,128]{1,0:T(8,128)S(1)}) custom-call(bf16[512,1024]{1,0:T(8,128)(2,1)S(1)} %get-tuple-element.113.left_a, bf16[512,1024]{1,0:T(8,128)(2,1)S(1)} %get-tuple-element.114.left_b, bf16[512,1024]{1,0:T(8,128)(2,1)S(1)} %get-tuple-element.115.right_a, bf16[512,1024]{1,0:T(8,128)(2,1)S(1)} %get-tuple-element.97.refs_4_.right_b, ...), custom_call_target="tpu_custom_call" | custom-call | flops 20000000000 | bytes 1 | tf_op jit(solution)/shard_map/grad_gate/pallas_call | solution.py:632
  100.9 1.4 %collective-permute-start.31 = (bf16[256,256]{1,0:T(8,128)(2,1)S(1)}, bf16[256,256]{1,0:T(8,128)(2,1)S(1)}, u32[]{:S(2)}, u32[]{:S(2)}) collective-permute-start(bf16[256,256]{1,0:T(8,128)(2,1)S(1)} %get-tuple-element.125), channel_id=1, source_target_pairs={{0,6},{1,7},{2,4},{3,5},{4,2},{5,3},{6,0},{7,1},{8,14},{9,15},{10,... | collective-permute-start | bytes 393224 | tf_op jit(solution)/shard_map/ppermute | solution.py:459
  102.3 2.5 %collective-permute-start.29 = (bf16[256,256]{1,0:T(8,128)(2,1)S(1)}, bf16[256,256]{1,0:T(8,128)(2,1)S(1)}, u32[]{:S(2)}, u32[]{:S(2)}) collective-permute-start(bf16[256,256]{1,0:T(8,128)(2,1)S(1)} %get-tuple-element.123), channel_id=1, source_target_pairs={{0,6},{1,7},{2,4},{3,5},{4,2},{5,3},{6,0},{7,1},{8,14},{9,15},{10,... | collective-permute-start | bytes 393224 | tf_op jit(solution)/shard_map/ppermute | solution.py:459
  105.0 2.0 %collective-permute-start.27 = (bf16[256,512]{1,0:T(8,128)(2,1)S(1)}, bf16[256,512]{1,0:T(8,128)(2,1)S(1)}, u32[]{:S(2)}, u32[]{:S(2)}) collective-permute-start(bf16[256,512]{1,0:T(8,128)(2,1)S(1)} %get-tuple-element.122), channel_id=1, source_target_pairs={{0,2},{1,3},{2,0},{3,1},{4,6},{5,7},{6,4},{7,5},{8,10},{9,11},{10,... | collective-permute-start | bytes 786440 | tf_op jit(solution)/shard_map/ppermute | solution.py:459
  107.0 4.2 %grad_up.1 = (f32[1024,1024]{1,0:T(8,128)}, f32[8,128]{1,0:T(8,128)S(1)}) custom-call(bf16[512,1024]{1,0:T(8,128)(2,1)S(1)} %get-tuple-element.113.left_a, bf16[512,1024]{1,0:T(8,128)(2,1)S(1)} %get-tuple-element.114.left_b, bf16[512,1024]{1,0:T(8,128)(2,1)S(1)} %get-tuple-element.126.right_a, bf16[512,1024]{1,0:T(8,128)(2,1)S(1)} %get-tuple-element.127.right_b, ...), custom_call_target="tpu_custom_call" | custom-call | flops 20000000000 | bytes 1 | tf_op jit(solution)/shard_map/grad_up/pallas_call | solution.py:632
  111.2 1.6 %collective-permute-done.27.refs_1_ = bf16[256,512]{1,0:T(8,128)(2,1)S(1)} collective-permute-done((bf16[256,512]{1,0:T(8,128)(2,1)S(1)}, bf16[256,512]{1,0:T(8,128)(2,1)S(1)}, u32[]{:S(2)}, u32[]{:S(2)}) %collective-permute-start.27) | collective-permute-done | bytes 262176 | tf_op jit(solution)/shard_map/ppermute | solution.py:459
  116.5 1.4 %collective-permute-start.36 = (f32[2,256]{1,0:T(2,128)S(1)}, f32[2,256]{1,0:T(2,128)S(1)}, u32[]{:S(2)}, u32[]{:S(2)}) collective-permute-start(f32[2,256]{1,0:T(2,128)S(1)} %slice.3), channel_id=1, source_target_pairs={{0,16},{8,24},{16,0},{24,8},{1,17},{9,25},{17,1},{25,9},{2,18},{10... | collective-permute-start | bytes 6152 | tf_op jit(solution)/shard_map/ppermute | solution.py:459
  117.9 1.5 %collective-permute-start.37 = (f32[2,256]{1,0:T(2,128)S(1)}, f32[2,256]{1,0:T(2,128)S(1)}, u32[]{:S(2)}, u32[]{:S(2)}) collective-permute-start(f32[2,256]{1,0:T(2,128)S(1)} %slice.3), channel_id=1, source_target_pairs={{0,24},{8,16},{16,8},{24,0},{1,25},{9,17},{17,9},{25,1},{2,26},{10... | collective-permute-start | bytes 6152 | tf_op jit(solution)/shard_map/ppermute | solution.py:459
  120.1 2.3 %collective-permute-done.37 = f32[2,256]{1,0:T(2,128)S(1)} collective-permute-done((f32[2,256]{1,0:T(2,128)S(1)}, f32[2,256]{1,0:T(2,128)S(1)}, u32[]{:S(2)}, u32[]{:S(2)}) %collective-permute-start.37) | collective-permute-done | bytes 2080 | tf_op jit(solution)/shard_map/ppermute | solution.py:459
  (80 shorter events, 25.5 us)
Async XLA Ops:
  6.0 15.4 %collective-permute-start.4 = (bf16[272,512]{1,0:T(8,128)(2,1)S(1)}, bf16[272,512]{1,0:T(8,128)(2,1)S(1)}, u32[]{:S(2)}, u32[]{:S(2)}) collective-permute-start(bf16[272,512]{1,0:T(8,128)(2,1)S(1)} %get-tuple-element.74), channel_id=1, source_target_pairs={{0,2},{1,3},{2,0},{3,1},{4,6},{5,7},{6,4},{7,5},{8,10},{9,11},{10,... | collective-permute-start | bytes 835592 | tf_op jit(solution)/shard_map/ppermute | solution.py:459
  8.8 22.4 %collective-permute-start.7 = (bf16[272,512]{1,0:T(8,128)(2,1)S(1)}, bf16[272,512]{1,0:T(8,128)(2,1)S(1)}, u32[]{:S(2)}, u32[]{:S(2)}) collective-permute-start(bf16[272,512]{1,0:T(8,128)(2,1)S(1)} %get-tuple-element.75), channel_id=1, source_target_pairs={{0,4},{1,5},{2,6},{3,7},{4,0},{5,1},{6,2},{7,3},{8,12},{9,13},{10,... | collective-permute-start | bytes 835592 | tf_op jit(solution)/shard_map/ppermute | solution.py:459
  11.4 19.8 %collective-permute-start.8 = (bf16[272,512]{1,0:T(8,128)(2,1)S(1)}, bf16[272,512]{1,0:T(8,128)(2,1)S(1)}, u32[]{:S(2)}, u32[]{:S(2)}) collective-permute-start(bf16[272,512]{1,0:T(8,128)(2,1)S(1)} %get-tuple-element.76), channel_id=1, source_target_pairs={{0,6},{1,7},{2,4},{3,5},{4,2},{5,3},{6,0},{7,1},{8,14},{9,15},{10,... | collective-permute-start | bytes 835592 | tf_op jit(solution)/shard_map/ppermute | solution.py:459
  21.4 13.7 %collective-permute-start.6 = (bf16[512,512]{1,0:T(8,128)(2,1)S(1)}, bf16[512,512]{1,0:T(8,128)(2,1)S(1)}, u32[]{:S(2)}, u32[]{:S(2)}) collective-permute-start(bf16[512,512]{1,0:T(8,128)(2,1)S(1)} %join_near.1.after.refs_1_), channel_id=1, source_target_pairs={{0,16},{8,24},{16,0},{24,8},{1,17},{9,25},{17,1},{25,9},{2,18},{10... | collective-permute-start | bytes 1572872 | tf_op jit(solution)/shard_map/ppermute | solution.py:459
  23.2 13.1 %collective-permute-start.5 = (bf16[512,512]{1,0:T(8,128)(2,1)S(1)}, bf16[512,512]{1,0:T(8,128)(2,1)S(1)}, u32[]{:S(2)}, u32[]{:S(2)}) collective-permute-start(bf16[512,512]{1,0:T(8,128)(2,1)S(1)} %join_near.1.after.refs_1_), channel_id=1, source_target_pairs={{0,8},{8,0},{16,24},{24,16},{1,9},{9,1},{17,25},{25,17},{2,10},{10... | collective-permute-start | bytes 1572872 | tf_op jit(solution)/shard_map/ppermute | solution.py:459
  36.3 9.3 %collective-permute-start.9 = (bf16[256,512]{1,0:T(8,128)(2,1)S(1)}, bf16[256,512]{1,0:T(8,128)(2,1)S(1)}, u32[]{:S(2)}, u32[]{:S(2)}) collective-permute-start(bf16[256,512]{1,0:T(8,128)(2,1)S(1)} %get-tuple-element.78), channel_id=1, source_target_pairs={{0,16},{8,24},{16,0},{24,8},{1,17},{9,25},{17,1},{25,9},{2,18},{10... | collective-permute-start | bytes 786440 | tf_op jit(solution)/shard_map/ppermute | solution.py:459
  37.0 9.2 %collective-permute-start.10 = (bf16[256,512]{1,0:T(8,128)(2,1)S(1)}, bf16[256,512]{1,0:T(8,128)(2,1)S(1)}, u32[]{:S(2)}, u32[]{:S(2)}) collective-permute-start(bf16[256,512]{1,0:T(8,128)(2,1)S(1)} %get-tuple-element.79), channel_id=1, source_target_pairs={{0,8},{8,0},{16,24},{24,16},{1,9},{9,1},{17,25},{25,17},{2,10},{10... | collective-permute-start | bytes 786440 | tf_op jit(solution)/shard_map/ppermute | solution.py:459
  38.4 15.8 %collective-permute-start.14 = (bf16[512,512]{1,0:T(8,128)(2,1)S(1)}, bf16[512,512]{1,0:T(8,128)(2,1)S(1)}, u32[]{:S(2)}, u32[]{:S(2)}) collective-permute-start(bf16[512,512]{1,0:T(8,128)(2,1)S(1)} %join_far.1.refs_2_.refs_1_), channel_id=1, source_target_pairs={{0,16},{8,24},{16,0},{24,8},{1,17},{9,25},{17,1},{25,9},{2,18},{10... | collective-permute-start | bytes 1572872 | tf_op jit(solution)/shard_map/ppermute | solution.py:459
  39.9 15.0 %collective-permute-start.13 = (bf16[512,512]{1,0:T(8,128)(2,1)S(1)}, bf16[512,512]{1,0:T(8,128)(2,1)S(1)}, u32[]{:S(2)}, u32[]{:S(2)}) collective-permute-start(bf16[512,512]{1,0:T(8,128)(2,1)S(1)} %join_far.1.refs_2_.refs_1_), channel_id=1, source_target_pairs={{0,8},{8,0},{16,24},{24,16},{1,9},{9,1},{17,25},{25,17},{2,10},{10... | collective-permute-start | bytes 1572872 | tf_op jit(solution)/shard_map/ppermute | solution.py:459
  54.9 9.3 %collective-permute-start.15 = (bf16[256,512]{1,0:T(8,128)(2,1)S(1)}, bf16[256,512]{1,0:T(8,128)(2,1)S(1)}, u32[]{:S(2)}, u32[]{:S(2)}) collective-permute-start(bf16[256,512]{1,0:T(8,128)(2,1)S(1)} %get-tuple-element.88), channel_id=1, source_target_pairs={{0,16},{8,24},{16,0},{24,8},{1,17},{9,25},{17,1},{25,9},{2,18},{10... | collective-permute-start | bytes 786440 | tf_op jit(solution)/shard_map/ppermute | solution.py:459
  56.0 9.2 %collective-permute-start.16 = (bf16[256,512]{1,0:T(8,128)(2,1)S(1)}, bf16[256,512]{1,0:T(8,128)(2,1)S(1)}, u32[]{:S(2)}, u32[]{:S(2)}) collective-permute-start(bf16[256,512]{1,0:T(8,128)(2,1)S(1)} %get-tuple-element.89), channel_id=1, source_target_pairs={{0,8},{8,0},{16,24},{24,16},{1,9},{9,1},{17,25},{25,17},{2,10},{10... | collective-permute-start | bytes 786440 | tf_op jit(solution)/shard_map/ppermute | solution.py:459
  57.5 17.6 %collective-permute-start.11 = (bf16[256,1024]{1,0:T(8,128)(2,1)S(1)}, bf16[256,1024]{1,0:T(8,128)(2,1)S(1)}, u32[]{:S(2)}, u32[]{:S(2)}) collective-permute-start(bf16[256,1024]{1,0:T(8,128)(2,1)S(1)} %get-tuple-element.84), channel_id=1, source_target_pairs={{0,8},{8,0},{16,24},{24,16},{1,9},{9,1},{17,25},{25,17},{2,10},{10... | collective-permute-start | bytes 1572872 | tf_op jit(solution)/shard_map/ppermute | solution.py:459
  58.0 17.1 %collective-permute-start.12 = (bf16[256,1024]{1,0:T(8,128)(2,1)S(1)}, bf16[256,1024]{1,0:T(8,128)(2,1)S(1)}, u32[]{:S(2)}, u32[]{:S(2)}) collective-permute-start(bf16[256,1024]{1,0:T(8,128)(2,1)S(1)} %get-tuple-element.86), channel_id=1, source_target_pairs={{0,16},{8,24},{16,0},{24,8},{1,17},{9,25},{17,1},{25,9},{2,18},{10... | collective-permute-start | bytes 1572872 | tf_op jit(solution)/shard_map/ppermute | solution.py:459
  69.4 12.8 %collective-permute-start.18 = (bf16[256,512]{1,0:T(8,128)(2,1)S(1)}, bf16[256,512]{1,0:T(8,128)(2,1)S(1)}, u32[]{:S(2)}, u32[]{:S(2)}) collective-permute-start(bf16[256,512]{1,0:T(8,128)(2,1)S(1)} %get-tuple-element.93), channel_id=1, source_target_pairs={{0,16},{8,24},{16,0},{24,8},{1,17},{9,25},{17,1},{25,9},{2,18},{10... | collective-permute-start | bytes 786440 | tf_op jit(solution)/shard_map/ppermute | solution.py:459
  70.5 11.7 %collective-permute-start.17 = (bf16[256,512]{1,0:T(8,128)(2,1)S(1)}, bf16[256,512]{1,0:T(8,128)(2,1)S(1)}, u32[]{:S(2)}, u32[]{:S(2)}) collective-permute-start(bf16[256,512]{1,0:T(8,128)(2,1)S(1)} %get-tuple-element.91.refs_12_), channel_id=1, source_target_pairs={{0,8},{8,0},{16,24},{24,16},{1,9},{9,1},{17,25},{25,17},{2,10},{10... | collective-permute-start | bytes 786440 | tf_op jit(solution)/shard_map/ppermute | solution.py:459
  80.0 10.1 %collective-permute-start.21 = (bf16[256,512]{1,0:T(8,128)(2,1)S(1)}, bf16[256,512]{1,0:T(8,128)(2,1)S(1)}, u32[]{:S(2)}, u32[]{:S(2)}) collective-permute-start(bf16[256,512]{1,0:T(8,128)(2,1)S(1)} %get-tuple-element.103), channel_id=1, source_target_pairs={{0,8},{8,0},{16,24},{24,16},{1,9},{9,1},{17,25},{25,17},{2,10},{10... | collective-permute-start | bytes 786440 | tf_op jit(solution)/shard_map/ppermute | solution.py:459
  81.6 9.4 %collective-permute-start.22 = (bf16[256,512]{1,0:T(8,128)(2,1)S(1)}, bf16[256,512]{1,0:T(8,128)(2,1)S(1)}, u32[]{:S(2)}, u32[]{:S(2)}) collective-permute-start(bf16[256,512]{1,0:T(8,128)(2,1)S(1)} %get-tuple-element.105), channel_id=1, source_target_pairs={{0,16},{8,24},{16,0},{24,8},{1,17},{9,25},{17,1},{25,9},{2,18},{10... | collective-permute-start | bytes 786440 | tf_op jit(solution)/shard_map/ppermute | solution.py:459
  82.3 10.2 %collective-permute-start.25 = (bf16[256,256]{1,0:T(8,128)(2,1)S(1)}, bf16[256,256]{1,0:T(8,128)(2,1)S(1)}, u32[]{:S(2)}, u32[]{:S(2)}) collective-permute-start(bf16[256,256]{1,0:T(8,128)(2,1)S(1)} %get-tuple-element.116), channel_id=1, source_target_pairs={{0,16},{8,24},{16,0},{24,8},{1,17},{9,25},{17,1},{25,9},{2,18},{10... | collective-permute-start | bytes 393224 | tf_op jit(solution)/shard_map/ppermute | solution.py:459
  83.8 9.3 %collective-permute-start.26 = (bf16[256,256]{1,0:T(8,128)(2,1)S(1)}, bf16[256,256]{1,0:T(8,128)(2,1)S(1)}, u32[]{:S(2)}, u32[]{:S(2)}) collective-permute-start(bf16[256,256]{1,0:T(8,128)(2,1)S(1)} %get-tuple-element.117), channel_id=1, source_target_pairs={{0,8},{8,0},{16,24},{24,16},{1,9},{9,1},{17,25},{25,17},{2,10},{10... | collective-permute-start | bytes 393224 | tf_op jit(solution)/shard_map/ppermute | solution.py:459
  84.6 20.2 %collective-permute-start.19 = (bf16[256,512]{1,0:T(8,128)(2,1)S(1)}, bf16[256,512]{1,0:T(8,128)(2,1)S(1)}, u32[]{:S(2)}, u32[]{:S(2)}) collective-permute-start(bf16[256,512]{1,0:T(8,128)(2,1)S(1)} %get-tuple-element.100), channel_id=1, source_target_pairs={{0,16},{8,24},{16,0},{24,8},{1,17},{9,25},{17,1},{25,9},{2,18},{10... | collective-permute-start | bytes 786440 | tf_op jit(solution)/shard_map/ppermute | solution.py:459
  90.2 14.7 %collective-permute-start.20 = (bf16[256,512]{1,0:T(8,128)(2,1)S(1)}, bf16[256,512]{1,0:T(8,128)(2,1)S(1)}, u32[]{:S(2)}, u32[]{:S(2)}) collective-permute-start(bf16[256,512]{1,0:T(8,128)(2,1)S(1)} %get-tuple-element.101), channel_id=1, source_target_pairs={{0,8},{8,0},{16,24},{24,16},{1,9},{9,1},{17,25},{25,17},{2,10},{10... | collective-permute-start | bytes 786440 | tf_op jit(solution)/shard_map/ppermute | solution.py:459
  91.1 9.8 %collective-permute-start.23 = (bf16[256,256]{1,0:T(8,128)(2,1)S(1)}, bf16[256,256]{1,0:T(8,128)(2,1)S(1)}, u32[]{:S(2)}, u32[]{:S(2)}) collective-permute-start(bf16[256,256]{1,0:T(8,128)(2,1)S(1)} %get-tuple-element.111), channel_id=1, source_target_pairs={{0,16},{8,24},{16,0},{24,8},{1,17},{9,25},{17,1},{25,9},{2,18},{10... | collective-permute-start | bytes 393224 | tf_op jit(solution)/shard_map/ppermute | solution.py:459
  92.5 9.7 %collective-permute-start.24 = (bf16[256,256]{1,0:T(8,128)(2,1)S(1)}, bf16[256,256]{1,0:T(8,128)(2,1)S(1)}, u32[]{:S(2)}, u32[]{:S(2)}) collective-permute-start(bf16[256,256]{1,0:T(8,128)(2,1)S(1)} %get-tuple-element.112), channel_id=1, source_target_pairs={{0,8},{8,0},{16,24},{24,16},{1,9},{9,1},{17,25},{25,17},{2,10},{10... | collective-permute-start | bytes 393224 | tf_op jit(solution)/shard_map/ppermute | solution.py:459
  93.2 18.0 %collective-permute-start.30 = (bf16[256,256]{1,0:T(8,128)(2,1)S(1)}, bf16[256,256]{1,0:T(8,128)(2,1)S(1)}, u32[]{:S(2)}, u32[]{:S(2)}) collective-permute-start(bf16[256,256]{1,0:T(8,128)(2,1)S(1)} %get-tuple-element.118.after), channel_id=1, source_target_pairs={{0,4},{1,5},{2,6},{3,7},{4,0},{5,1},{6,2},{7,3},{8,12},{9,13},{10,... | collective-permute-start | bytes 393224 | tf_op jit(solution)/shard_map/ppermute | solution.py:459
  100.9 10.3 %collective-permute-start.31 = (bf16[256,256]{1,0:T(8,128)(2,1)S(1)}, bf16[256,256]{1,0:T(8,128)(2,1)S(1)}, u32[]{:S(2)}, u32[]{:S(2)}) collective-permute-start(bf16[256,256]{1,0:T(8,128)(2,1)S(1)} %get-tuple-element.125), channel_id=1, source_target_pairs={{0,6},{1,7},{2,4},{3,5},{4,2},{5,3},{6,0},{7,1},{8,14},{9,15},{10,... | collective-permute-start | bytes 393224 | tf_op jit(solution)/shard_map/ppermute | solution.py:459
  102.3 13.0 %collective-permute-start.29 = (bf16[256,256]{1,0:T(8,128)(2,1)S(1)}, bf16[256,256]{1,0:T(8,128)(2,1)S(1)}, u32[]{:S(2)}, u32[]{:S(2)}) collective-permute-start(bf16[256,256]{1,0:T(8,128)(2,1)S(1)} %get-tuple-element.123), channel_id=1, source_target_pairs={{0,6},{1,7},{2,4},{3,5},{4,2},{5,3},{6,0},{7,1},{8,14},{9,15},{10,... | collective-permute-start | bytes 393224 | tf_op jit(solution)/shard_map/ppermute | solution.py:459
  104.8 10.4 %collective-permute-start.28 = (bf16[256,256]{1,0:T(8,128)(2,1)S(1)}, bf16[256,256]{1,0:T(8,128)(2,1)S(1)}, u32[]{:S(2)}, u32[]{:S(2)}) collective-permute-start(bf16[256,256]{1,0:T(8,128)(2,1)S(1)} %get-tuple-element.120.refs_3_), channel_id=1, source_target_pairs={{0,4},{1,5},{2,6},{3,7},{4,0},{5,1},{6,2},{7,3},{8,12},{9,13},{10,... | collective-permute-start | bytes 393224 | tf_op jit(solution)/shard_map/ppermute | solution.py:459
  105.0 7.7 %collective-permute-start.27 = (bf16[256,512]{1,0:T(8,128)(2,1)S(1)}, bf16[256,512]{1,0:T(8,128)(2,1)S(1)}, u32[]{:S(2)}, u32[]{:S(2)}) collective-permute-start(bf16[256,512]{1,0:T(8,128)(2,1)S(1)} %get-tuple-element.122), channel_id=1, source_target_pairs={{0,2},{1,3},{2,0},{3,1},{4,6},{5,7},{6,4},{7,5},{8,10},{9,11},{10,... | collective-permute-start | bytes 786440 | tf_op jit(solution)/shard_map/ppermute | solution.py:459
  116.5 3.6 %collective-permute-start.36 = (f32[2,256]{1,0:T(2,128)S(1)}, f32[2,256]{1,0:T(2,128)S(1)}, u32[]{:S(2)}, u32[]{:S(2)}) collective-permute-start(f32[2,256]{1,0:T(2,128)S(1)} %slice.3), channel_id=1, source_target_pairs={{0,16},{8,24},{16,0},{24,8},{1,17},{9,25},{17,1},{25,9},{2,18},{10... | collective-permute-start | bytes 6152 | tf_op jit(solution)/shard_map/ppermute | solution.py:459
  117.9 4.5 %collective-permute-start.37 = (f32[2,256]{1,0:T(2,128)S(1)}, f32[2,256]{1,0:T(2,128)S(1)}, u32[]{:S(2)}, u32[]{:S(2)}) collective-permute-start(f32[2,256]{1,0:T(2,128)S(1)} %slice.3), channel_id=1, source_target_pairs={{0,24},{8,16},{16,8},{24,0},{1,25},{9,17},{17,9},{25,1},{2,26},{10... | collective-permute-start | bytes 6152 | tf_op jit(solution)/shard_map/ppermute | solution.py:459
  119.4 3.6 %collective-permute-start.35 = (f32[2,256]{1,0:T(2,128)S(1)}, f32[2,256]{1,0:T(2,128)S(1)}, u32[]{:S(2)}, u32[]{:S(2)}) collective-permute-start(f32[2,256]{1,0:T(2,128)S(1)} %slice.3), channel_id=1, source_target_pairs={{0,8},{8,0},{16,24},{24,16},{1,9},{9,1},{17,25},{25,17},{2,10},{10... | collective-permute-start | bytes 6152 | tf_op jit(solution)/shard_map/ppermute | solution.py:459
  120.0 3.6 %collective-permute-start.34 = (bf16[256,256]{1,0:T(8,128)(2,1)S(1)}, bf16[256,256]{1,0:T(8,128)(2,1)S(1)}, u32[]{:S(2)}, u32[]{:S(2)}) collective-permute-start(bf16[256,256]{1,0:T(8,128)(2,1)S(1)} %get-tuple-element.135), channel_id=1, source_target_pairs={{0,1},{1,0},{2,3},{3,2},{4,5},{5,4},{6,7},{7,6},{8,9},{9,8},{10,11... | collective-permute-start | bytes 393224 | tf_op jit(solution)/shard_map/ppermute | solution.py:459
  (11 other events, 35.5 us)

commit v5 on v4

--- a/solution.py
+++ b/solution.py
@@ -648,15 +648,15 @@
     dx_sums = reduce_second(dx_first, (done_d,))
     out_rows = reduce_last(out_sums, size, (dx_sums[0],))
     back_out = over_chips_from(2, out_rows)
-    grad_gate, done_g = weight_grad(
-        "grad_gate", (near_x, far_x), (near_dgate, far_dgate), width, ff, out_rows[0]
-    )
-    dx_rows = reduce_last(dx_sums, size, (done_g,))
+    dx_rows = reduce_last(dx_sums, size, out_rows[:1])
     back_dx = over_chips_from(2, dx_rows)
     near_rows = reduce_last(near_sums, size, dx_rows[:1])
     back_near = over_chips_from(0, near_rows)
+    grad_gate, done_g = weight_grad(
+        "grad_gate", (near_x, far_x), (near_dgate, far_dgate), width, ff, near_rows[0]
+    )
     grad_up, done_u = weight_grad(
-        "grad_up", (near_x, far_x), (near_dup, far_dup), width, ff, near_rows[0]
+        "grad_up", (near_x, far_x), (near_dup, far_dup), width, ff, done_g
     )
 
     whole, narrow, few = vm((toks, feats), F32), vm((toks, feats), BF16), vm((8, toks), F32)

time: 124 us -> 124 us (level)
  no operation moved by 1% of the time
where the time goes in v5:
time: 124 us
  starting transfers between devices  42.3 us (34%)
  waiting for transfers between devices  40.2 us (32%)
  Pallas kernels  38.1 us (31%)
  local copies, waits for them, and re-layouts  1.37 us (1%)
  other arithmetic  1.35 us (1%)
    ppermute x38, starting transfers between devices, shift(): return lax.ppermute(x, axis, [(i, i ^ bit) for i in range(n)])  42.3 us
    ppermute x38, waiting for transfers between devices, shift(): return lax.ppermute(x, axis, [(i, i ^ bit) for i in range(n)])  40.2 us
    pallas_call x17, Pallas kernels, kernel_call(): pl.pallas_call(run, in_specs=[smem()] * plan_args + [vmem()] * (count - p...  22.6 us
    pallas_call x3, Pallas kernels, weight_grad(): pl.pallas_call(weights_kernel, grid=(steps,), in_specs=[vmem()] * 5, out_...  12.6 us
    pallas_call x1, Pallas kernels, on_quad(): pl.pallas_call(load_kernel, in_specs=[pl.BlockSpec(memory_space=pltpu.HBM...  2.88 us
  transfers between devices with their start and end apart: 38, of which 18 were waited for; matrix products, arithmetic and copies ran while one was open for 1% of the time, Pallas kernels for 28%

profile of v5, /device:TPU:0, one launch (start us, length us, event | category | flops | bytes accessed | tf_op | source)
XLA Modules:
  0.0 124.1 jit_solution(10051870802761875327)
XLA Ops:
  4.4 1.6 %send.1 = (bf16[256,512]{1,0:T(8,128)(2,1)S(1)}, bf16[272,512]{1,0:T(8,128)(2,1)S(1)}, bf16[272,512]{1,0:T(8,128)(2,1)S(1)}, bf16[272,512]{1,0:T(8,128)(2,1)S(1)}) custom-call(s32[3]{0:T(128)S(1)} %pad_add_fusion.refs_0_, bf16[256,256]{1,0:T(8,128)(2,1)} %refs_1_.2, bf16[256,256]{1,0:T(8,128)(2,1)} %refs_5_.1, s32[2,256]{1,0:T(2,128)S(1)} %bitcast.14, ...), custom_call_target="tpu_custom_call" | custom-call | flops 1 | bytes 1048576 | tf_op jit(solution)/shard_map/send/pallas_call | solution.py:490
  6.0 2.8 %collective-permute-start.4 = (bf16[272,512]{1,0:T(8,128)(2,1)S(1)}, bf16[272,512]{1,0:T(8,128)(2,1)S(1)}, u32[]{:S(2)}, u32[]{:S(2)}) collective-permute-start(bf16[272,512]{1,0:T(8,128)(2,1)S(1)} %get-tuple-element.74), channel_id=1, source_target_pairs={{0,2},{1,3},{2,0},{3,1},{4,6},{5,7},{6,4},{7,5},{8,10},{9,11},{10,... | collective-permute-start | bytes 835592 | tf_op jit(solution)/shard_map/ppermute | solution.py:459
  8.8 2.6 %collective-permute-start.7 = (bf16[272,512]{1,0:T(8,128)(2,1)S(1)}, bf16[272,512]{1,0:T(8,128)(2,1)S(1)}, u32[]{:S(2)}, u32[]{:S(2)}) collective-permute-start(bf16[272,512]{1,0:T(8,128)(2,1)S(1)} %get-tuple-element.75), channel_id=1, source_target_pairs={{0,4},{1,5},{2,6},{3,7},{4,0},{5,1},{6,2},{7,3},{8,12},{9,13},{10,... | collective-permute-start | bytes 835592 | tf_op jit(solution)/shard_map/ppermute | solution.py:459
  11.4 10.0 %collective-permute-done.4.refs_1_.refs_7_ = bf16[272,512]{1,0:T(8,128)(2,1)S(1)} collective-permute-done((bf16[272,512]{1,0:T(8,128)(2,1)S(1)}, bf16[272,512]{1,0:T(8,128)(2,1)S(1)}, u32[]{:S(2)}, u32[]{:S(2)}) %collective-permute-start.4) | collective-permute-done | bytes 278560 | tf_op jit(solution)/shard_map/ppermute | solution.py:459
  21.4 1.7 %collective-permute-start.6 = (bf16[512,512]{1,0:T(8,128)(2,1)S(1)}, bf16[512,512]{1,0:T(8,128)(2,1)S(1)}, u32[]{:S(2)}, u32[]{:S(2)}) collective-permute-start(bf16[512,512]{1,0:T(8,128)(2,1)S(1)} %join_near.1.after.refs_1_), channel_id=1, source_target_pairs={{0,16},{8,24},{16,0},{24,8},{1,17},{9,25},{17,1},{25,9},{2,18},{10... | collective-permute-start | bytes 1572872 | tf_op jit(solution)/shard_map/ppermute | solution.py:459
  23.2 1.5 %collective-permute-start.5 = (bf16[512,512]{1,0:T(8,128)(2,1)S(1)}, bf16[512,512]{1,0:T(8,128)(2,1)S(1)}, u32[]{:S(2)}, u32[]{:S(2)}) collective-permute-start(bf16[512,512]{1,0:T(8,128)(2,1)S(1)} %join_near.1.after.refs_1_), channel_id=1, source_target_pairs={{0,8},{8,0},{16,24},{24,16},{1,9},{9,1},{17,25},{25,17},{2,10},{10... | collective-permute-start | bytes 1572872 | tf_op jit(solution)/shard_map/ppermute | solution.py:459
  24.7 2.9 %load_weights.1 = (bf16[1024,1024]{1,0:T(8,128)(2,1)S(1)}, bf16[1024,1024]{1,0:T(8,128)(2,1)S(1)}, bf16[1024,1024]{1,0:T(8,128)(2,1)S(1)}) custom-call(bf16[1024,1024]{1,0:T(8,128)(2,1)} %bitcast.19, bf16[1024,1024]{1,0:T(8,128)(2,1)} %bitcast.20, bf16[1024,1024]{1,0:T(8,128)(2,1)} %bitcast.21, bf16[512,512]{1,0:T(8,128)(2,1)S(1)} %join_near.1.after.refs_1_), custom_call_target="tpu_custom_call" | custom-call | flops 20000000000 | bytes 25165824 | tf_op jit(solution)/shard_map/load_weights/pallas_call | solution.py:574
  27.6 3.6 %collective-permute-done.7.refs_0_.refs_8_ = bf16[272,512]{1,0:T(8,128)(2,1)S(1)} collective-permute-done((bf16[272,512]{1,0:T(8,128)(2,1)S(1)}, bf16[272,512]{1,0:T(8,128)(2,1)S(1)}, u32[]{:S(2)}, u32[]{:S(2)}) %collective-permute-start.7) | collective-permute-done | bytes 278560 | tf_op jit(solution)/shard_map/ppermute | solution.py:459
  31.2 4.0 %collective-permute-done.6.refs_1_.refs_3_ = bf16[512,512]{1,0:T(8,128)(2,1)S(1)} collective-permute-done((bf16[512,512]{1,0:T(8,128)(2,1)S(1)}, bf16[512,512]{1,0:T(8,128)(2,1)S(1)}, u32[]{:S(2)}, u32[]{:S(2)}) %collective-permute-start.6) | collective-permute-done | bytes 524320 | tf_op jit(solution)/shard_map/ppermute | solution.py:459
  37.0 1.3 %collective-permute-start.10 = (bf16[256,512]{1,0:T(8,128)(2,1)S(1)}, bf16[256,512]{1,0:T(8,128)(2,1)S(1)}, u32[]{:S(2)}, u32[]{:S(2)}) collective-permute-start(bf16[256,512]{1,0:T(8,128)(2,1)S(1)} %get-tuple-element.79), channel_id=1, source_target_pairs={{0,8},{8,0},{16,24},{24,16},{1,9},{9,1},{17,25},{25,17},{2,10},{10... | collective-permute-start | bytes 786440 | tf_op jit(solution)/shard_map/ppermute | solution.py:459
  38.4 1.5 %collective-permute-start.14 = (bf16[512,512]{1,0:T(8,128)(2,1)S(1)}, bf16[512,512]{1,0:T(8,128)(2,1)S(1)}, u32[]{:S(2)}, u32[]{:S(2)}) collective-permute-start(bf16[512,512]{1,0:T(8,128)(2,1)S(1)} %join_far.1.refs_2_.refs_1_), channel_id=1, source_target_pairs={{0,16},{8,24},{16,0},{24,8},{1,17},{9,25},{17,1},{25,9},{2,18},{10... | collective-permute-start | bytes 1572872 | tf_op jit(solution)/shard_map/ppermute | solution.py:459
  41.5 4.2 %collective-permute-done.9.refs_4_ = bf16[256,512]{1,0:T(8,128)(2,1)S(1)} collective-permute-done((bf16[256,512]{1,0:T(8,128)(2,1)S(1)}, bf16[256,512]{1,0:T(8,128)(2,1)S(1)}, u32[]{:S(2)}, u32[]{:S(2)}) %collective-permute-start.9) | collective-permute-done | bytes 262176 | tf_op jit(solution)/shard_map/ppermute | solution.py:459
  46.3 7.8 %near.1 = (bf16[512,1024]{1,0:T(8,128)(2,1)S(1)}, bf16[512,1024]{1,0:T(8,128)(2,1)S(1)}, bf16[512,1024]{1,0:T(8,128)(2,1)S(1)}, bf16[512,1024]{1,0:T(8,128)(2,1)...) custom-call(s32[3]{0:T(128)S(1)} %pad_add_fusion.refs_0_, ...), custom_call_target="tpu_custom_call" | custom-call | flops 6442450944 | bytes 1048576 | tf_op jit(solution)/shard_map/near/pallas_call | solution.py:490
  56.0 1.5 %collective-permute-start.16 = (bf16[256,512]{1,0:T(8,128)(2,1)S(1)}, bf16[256,512]{1,0:T(8,128)(2,1)S(1)}, u32[]{:S(2)}, u32[]{:S(2)}) collective-permute-start(bf16[256,512]{1,0:T(8,128)(2,1)S(1)} %get-tuple-element.89), channel_id=1, source_target_pairs={{0,8},{8,0},{16,24},{24,16},{1,9},{9,1},{17,25},{25,17},{2,10},{10... | collective-permute-start | bytes 786440 | tf_op jit(solution)/shard_map/ppermute | solution.py:459
  59.0 5.2 %collective-permute-done.15.refs_4_ = bf16[256,512]{1,0:T(8,128)(2,1)S(1)} collective-permute-done((bf16[256,512]{1,0:T(8,128)(2,1)S(1)}, bf16[256,512]{1,0:T(8,128)(2,1)S(1)}, u32[]{:S(2)}, u32[]{:S(2)}) %collective-permute-start.15) | collective-permute-done | bytes 262176 | tf_op jit(solution)/shard_map/ppermute | solution.py:459
  65.2 4.2 %far_forward.1 = (bf16[512,1024]{1,0:T(8,128)(2,1)S(1)}, bf16[512,1024]{1,0:T(8,128)(2,1)S(1)}, bf16[512,1024]{1,0:T(8,128)(2,1)S(1)}, bf16[512,1024]{1,0:T(8,12...) custom-call(s32[3]{0:T(128)S(1)} %pad_add_fusion.refs_0_, ...), custom_call_target="tpu_custom_call" | custom-call | flops 3221225472 | bytes 1048576 | tf_op jit(solution)/shard_map/far_forward/pallas_call | solution.py:490
  71.6 3.5 %collective-permute-done.11.refs_13_.refs_1_ = bf16[256,1024]{1,0:T(8,128)(2,1)S(1)} collective-permute-done((bf16[256,1024]{1,0:T(8,128)(2,1)S(1)}, bf16[256,1024]{1,0:T(8,128)(2,1)S(1)}, u32[]{:S(2)}, u32[]{:S(2)}) %collective-permute-start.11) | collective-permute-done | bytes 524320 | tf_op jit(solution)/shard_map/ppermute | solution.py:459
  75.1 4.9 %far_backward.1 = (bf16[512,1024]{1,0:T(8,128)(2,1)S(1)}, bf16[512,1024]{1,0:T(8,128)(2,1)S(1)}, bf16[512,1024]{1,0:T(8,128)(2,1)S(1)}, bf16[256,512]{1,0:T(8,12...) custom-call(s32[3]{0:T(128)S(1)} %pad_add_fusion.refs_0_, ...), custom_call_target="tpu_custom_call" | custom-call | flops 3221225472 | bytes 1048576 | tf_op jit(solution)/shard_map/far_backward/pallas_call | solution.py:490
  80.0 1.6 %collective-permute-start.21 = (bf16[256,512]{1,0:T(8,128)(2,1)S(1)}, bf16[256,512]{1,0:T(8,128)(2,1)S(1)}, u32[]{:S(2)}, u32[]{:S(2)}) collective-permute-start(bf16[256,512]{1,0:T(8,128)(2,1)S(1)} %get-tuple-element.103), channel_id=1, source_target_pairs={{0,8},{8,0},{16,24},{24,16},{1,9},{9,1},{17,25},{25,17},{2,10},{10... | collective-permute-start | bytes 786440 | tf_op jit(solution)/shard_map/ppermute | solution.py:459
  82.3 1.5 %collective-permute-start.25 = (bf16[256,256]{1,0:T(8,128)(2,1)S(1)}, bf16[256,256]{1,0:T(8,128)(2,1)S(1)}, u32[]{:S(2)}, u32[]{:S(2)}) collective-permute-start(bf16[256,256]{1,0:T(8,128)(2,1)S(1)} %get-tuple-element.113), channel_id=1, source_target_pairs={{0,16},{8,24},{16,0},{24,8},{1,17},{9,25},{17,1},{25,9},{2,18},{10... | collective-permute-start | bytes 393224 | tf_op jit(solution)/shard_map/ppermute | solution.py:459
  85.9 4.2 %grad_down.1 = (f32[1024,1024]{1,0:T(8,128)}, f32[8,128]{1,0:T(8,128)S(1)}) custom-call(bf16[512,1024]{1,0:T(8,128)(2,1)S(1)} %get-tuple-element.87.refs_2_.left_a, bf16[512,1024]{1,0:T(8,128)(2,1)S(1)} %get-tuple-element.106.left_b, bf16[512,1024]{1,0:T(8,128)(2,1)S(1)} %get-tuple-element.107.right_a, bf16[512,1024]{1,0:T(8,128)(2,1)S(1)} %get-tuple-element.108.right_b, ...), custom_call_target="tpu_custom_call" | custom-call | flops 20000000000 | bytes 1 | tf_op jit(solution)/shard_map/grad_down/pallas_call | solution.py:632
  91.1 1.5 %collective-permute-start.23 = (bf16[256,256]{1,0:T(8,128)(2,1)S(1)}, bf16[256,256]{1,0:T(8,128)(2,1)S(1)}, u32[]{:S(2)}, u32[]{:S(2)}) collective-permute-start(bf16[256,256]{1,0:T(8,128)(2,1)S(1)} %get-tuple-element.111), channel_id=1, source_target_pairs={{0,16},{8,24},{16,0},{24,8},{1,17},{9,25},{17,1},{25,9},{2,18},{10... | collective-permute-start | bytes 393224 | tf_op jit(solution)/shard_map/ppermute | solution.py:459
  93.1 2.0 %collective-permute-done.26.refs_2_ = bf16[256,256]{1,0:T(8,128)(2,1)S(1)} collective-permute-done((bf16[256,256]{1,0:T(8,128)(2,1)S(1)}, bf16[256,256]{1,0:T(8,128)(2,1)S(1)}, u32[]{:S(2)}, u32[]{:S(2)}) %collective-permute-start.26) | collective-permute-done | bytes 131104 | tf_op jit(solution)/shard_map/ppermute | solution.py:459
  95.2 2.2 %collective-permute-start.31 = (bf16[256,256]{1,0:T(8,128)(2,1)S(1)}, bf16[256,256]{1,0:T(8,128)(2,1)S(1)}, u32[]{:S(2)}, u32[]{:S(2)}) collective-permute-start(bf16[256,256]{1,0:T(8,128)(2,1)S(1)} %get-tuple-element.121), channel_id=1, source_target_pairs={{0,6},{1,7},{2,4},{3,5},{4,2},{5,3},{6,0},{7,1},{8,14},{9,15},{10,... | collective-permute-start | bytes 393224 | tf_op jit(solution)/shard_map/ppermute | solution.py:459
  97.4 3.0 %collective-permute-start.30 = (bf16[256,256]{1,0:T(8,128)(2,1)S(1)}, bf16[256,256]{1,0:T(8,128)(2,1)S(1)}, u32[]{:S(2)}, u32[]{:S(2)}) collective-permute-start(bf16[256,256]{1,0:T(8,128)(2,1)S(1)} %get-tuple-element.115.refs_3_), channel_id=1, source_target_pairs={{0,4},{1,5},{2,6},{3,7},{4,0},{5,1},{6,2},{7,3},{8,12},{9,13},{10,... | collective-permute-start | bytes 393224 | tf_op jit(solution)/shard_map/ppermute | solution.py:459
  100.4 1.4 %collective-permute-start.29 = (bf16[256,256]{1,0:T(8,128)(2,1)S(1)}, bf16[256,256]{1,0:T(8,128)(2,1)S(1)}, u32[]{:S(2)}, u32[]{:S(2)}) collective-permute-start(bf16[256,256]{1,0:T(8,128)(2,1)S(1)} %get-tuple-element.119), channel_id=1, source_target_pairs={{0,6},{1,7},{2,4},{3,5},{4,2},{5,3},{6,0},{7,1},{8,14},{9,15},{10,... | collective-permute-start | bytes 393224 | tf_op jit(solution)/shard_map/ppermute | solution.py:459
  102.0 3.1 %collective-permute-start.27 = (bf16[256,512]{1,0:T(8,128)(2,1)S(1)}, bf16[256,512]{1,0:T(8,128)(2,1)S(1)}, u32[]{:S(2)}, u32[]{:S(2)}) collective-permute-start(bf16[256,512]{1,0:T(8,128)(2,1)S(1)} %get-tuple-element.118), channel_id=1, source_target_pairs={{0,2},{1,3},{2,0},{3,1},{4,6},{5,7},{6,4},{7,5},{8,10},{9,11},{10,... | collective-permute-start | bytes 786440 | tf_op jit(solution)/shard_map/ppermute | solution.py:459
  105.1 4.2 %grad_gate.1 = (f32[1024,1024]{1,0:T(8,128)}, f32[8,128]{1,0:T(8,128)S(1)}) custom-call(bf16[512,1024]{1,0:T(8,128)(2,1)S(1)} %get-tuple-element.122.left_a, bf16[512,1024]{1,0:T(8,128)(2,1)S(1)} %get-tuple-element.123.left_b, bf16[512,1024]{1,0:T(8,128)(2,1)S(1)} %get-tuple-element.126.right_a, bf16[512,1024]{1,0:T(8,128)(2,1)S(1)} %get-tuple-element.97.refs_4_.right_b, ...), custom_call_target="tpu_custom_call" | custom-call | flops 20000000000 | bytes 1 | tf_op jit(solution)/shard_map/grad_gate/pallas_call | solution.py:632
  109.3 4.2 %grad_up.1 = (f32[1024,1024]{1,0:T(8,128)}, f32[8,128]{1,0:T(8,128)S(1)}) custom-call(bf16[512,1024]{1,0:T(8,128)(2,1)S(1)} %get-tuple-element.122.left_a, bf16[512,1024]{1,0:T(8,128)(2,1)S(1)} %get-tuple-element.123.left_b, bf16[512,1024]{1,0:T(8,128)(2,1)S(1)} %get-tuple-element.124.right_a, bf16[512,1024]{1,0:T(8,128)(2,1)S(1)} %get-tuple-element.125.right_b, ...), custom_call_target="tpu_custom_call" | custom-call | flops 20000000000 | bytes 1 | tf_op jit(solution)/shard_map/grad_up/pallas_call | solution.py:632
  117.8 1.4 %collective-permute-start.37 = (f32[2,256]{1,0:T(2,128)S(1)}, f32[2,256]{1,0:T(2,128)S(1)}, u32[]{:S(2)}, u32[]{:S(2)}) collective-permute-start(f32[2,256]{1,0:T(2,128)S(1)} %slice.3), channel_id=1, source_target_pairs={{0,24},{8,16},{16,8},{24,0},{1,25},{9,17},{17,9},{25,1},{2,26},{10... | collective-permute-start | bytes 6152 | tf_op jit(solution)/shard_map/ppermute | solution.py:459
  119.2 1.5 %collective-permute-start.35 = (f32[2,256]{1,0:T(2,128)S(1)}, f32[2,256]{1,0:T(2,128)S(1)}, u32[]{:S(2)}, u32[]{:S(2)}) collective-permute-start(f32[2,256]{1,0:T(2,128)S(1)} %slice.3), channel_id=1, source_target_pairs={{0,8},{8,0},{16,24},{24,16},{1,9},{9,1},{17,25},{25,17},{2,10},{10... | collective-permute-start | bytes 6152 | tf_op jit(solution)/shard_map/ppermute | solution.py:459
  120.8 1.5 %collective-permute-done.37 = f32[2,256]{1,0:T(2,128)S(1)} collective-permute-done((f32[2,256]{1,0:T(2,128)S(1)}, f32[2,256]{1,0:T(2,128)S(1)}, u32[]{:S(2)}, u32[]{:S(2)}) %collective-permute-start.37) | collective-permute-done | bytes 2080 | tf_op jit(solution)/shard_map/ppermute | solution.py:459
  (80 shorter events, 25.3 us)
Async XLA Ops:
  6.0 15.4 %collective-permute-start.4 = (bf16[272,512]{1,0:T(8,128)(2,1)S(1)}, bf16[272,512]{1,0:T(8,128)(2,1)S(1)}, u32[]{:S(2)}, u32[]{:S(2)}) collective-permute-start(bf16[272,512]{1,0:T(8,128)(2,1)S(1)} %get-tuple-element.74), channel_id=1, source_target_pairs={{0,2},{1,3},{2,0},{3,1},{4,6},{5,7},{6,4},{7,5},{8,10},{9,11},{10,... | collective-permute-start | bytes 835592 | tf_op jit(solution)/shard_map/ppermute | solution.py:459
  8.8 22.4 %collective-permute-start.7 = (bf16[272,512]{1,0:T(8,128)(2,1)S(1)}, bf16[272,512]{1,0:T(8,128)(2,1)S(1)}, u32[]{:S(2)}, u32[]{:S(2)}) collective-permute-start(bf16[272,512]{1,0:T(8,128)(2,1)S(1)} %get-tuple-element.75), channel_id=1, source_target_pairs={{0,4},{1,5},{2,6},{3,7},{4,0},{5,1},{6,2},{7,3},{8,12},{9,13},{10,... | collective-permute-start | bytes 835592 | tf_op jit(solution)/shard_map/ppermute | solution.py:459
  11.4 19.8 %collective-permute-start.8 = (bf16[272,512]{1,0:T(8,128)(2,1)S(1)}, bf16[272,512]{1,0:T(8,128)(2,1)S(1)}, u32[]{:S(2)}, u32[]{:S(2)}) collective-permute-start(bf16[272,512]{1,0:T(8,128)(2,1)S(1)} %get-tuple-element.76), channel_id=1, source_target_pairs={{0,6},{1,7},{2,4},{3,5},{4,2},{5,3},{6,0},{7,1},{8,14},{9,15},{10,... | collective-permute-start | bytes 835592 | tf_op jit(solution)/shard_map/ppermute | solution.py:459
  21.4 13.7 %collective-permute-start.6 = (bf16[512,512]{1,0:T(8,128)(2,1)S(1)}, bf16[512,512]{1,0:T(8,128)(2,1)S(1)}, u32[]{:S(2)}, u32[]{:S(2)}) collective-permute-start(bf16[512,512]{1,0:T(8,128)(2,1)S(1)} %join_near.1.after.refs_1_), channel_id=1, source_target_pairs={{0,16},{8,24},{16,0},{24,8},{1,17},{9,25},{17,1},{25,9},{2,18},{10... | collective-permute-start | bytes 1572872 | tf_op jit(solution)/shard_map/ppermute | solution.py:459
  23.2 13.1 %collective-permute-start.5 = (bf16[512,512]{1,0:T(8,128)(2,1)S(1)}, bf16[512,512]{1,0:T(8,128)(2,1)S(1)}, u32[]{:S(2)}, u32[]{:S(2)}) collective-permute-start(bf16[512,512]{1,0:T(8,128)(2,1)S(1)} %join_near.1.after.refs_1_), channel_id=1, source_target_pairs={{0,8},{8,0},{16,24},{24,16},{1,9},{9,1},{17,25},{25,17},{2,10},{10... | collective-permute-start | bytes 1572872 | tf_op jit(solution)/shard_map/ppermute | solution.py:459
  36.3 9.3 %collective-permute-start.9 = (bf16[256,512]{1,0:T(8,128)(2,1)S(1)}, bf16[256,512]{1,0:T(8,128)(2,1)S(1)}, u32[]{:S(2)}, u32[]{:S(2)}) collective-permute-start(bf16[256,512]{1,0:T(8,128)(2,1)S(1)} %get-tuple-element.78), channel_id=1, source_target_pairs={{0,16},{8,24},{16,0},{24,8},{1,17},{9,25},{17,1},{25,9},{2,18},{10... | collective-permute-start | bytes 786440 | tf_op jit(solution)/shard_map/ppermute | solution.py:459
  37.0 9.2 %collective-permute-start.10 = (bf16[256,512]{1,0:T(8,128)(2,1)S(1)}, bf16[256,512]{1,0:T(8,128)(2,1)S(1)}, u32[]{:S(2)}, u32[]{:S(2)}) collective-permute-start(bf16[256,512]{1,0:T(8,128)(2,1)S(1)} %get-tuple-element.79), channel_id=1, source_target_pairs={{0,8},{8,0},{16,24},{24,16},{1,9},{9,1},{17,25},{25,17},{2,10},{10... | collective-permute-start | bytes 786440 | tf_op jit(solution)/shard_map/ppermute | solution.py:459
  38.4 15.8 %collective-permute-start.14 = (bf16[512,512]{1,0:T(8,128)(2,1)S(1)}, bf16[512,512]{1,0:T(8,128)(2,1)S(1)}, u32[]{:S(2)}, u32[]{:S(2)}) collective-permute-start(bf16[512,512]{1,0:T(8,128)(2,1)S(1)} %join_far.1.refs_2_.refs_1_), channel_id=1, source_target_pairs={{0,16},{8,24},{16,0},{24,8},{1,17},{9,25},{17,1},{25,9},{2,18},{10... | collective-permute-start | bytes 1572872 | tf_op jit(solution)/shard_map/ppermute | solution.py:459
  39.9 15.0 %collective-permute-start.13 = (bf16[512,512]{1,0:T(8,128)(2,1)S(1)}, bf16[512,512]{1,0:T(8,128)(2,1)S(1)}, u32[]{:S(2)}, u32[]{:S(2)}) collective-permute-start(bf16[512,512]{1,0:T(8,128)(2,1)S(1)} %join_far.1.refs_2_.refs_1_), channel_id=1, source_target_pairs={{0,8},{8,0},{16,24},{24,16},{1,9},{9,1},{17,25},{25,17},{2,10},{10... | collective-permute-start | bytes 1572872 | tf_op jit(solution)/shard_map/ppermute | solution.py:459
  54.9 9.3 %collective-permute-start.15 = (bf16[256,512]{1,0:T(8,128)(2,1)S(1)}, bf16[256,512]{1,0:T(8,128)(2,1)S(1)}, u32[]{:S(2)}, u32[]{:S(2)}) collective-permute-start(bf16[256,512]{1,0:T(8,128)(2,1)S(1)} %get-tuple-element.88), channel_id=1, source_target_pairs={{0,16},{8,24},{16,0},{24,8},{1,17},{9,25},{17,1},{25,9},{2,18},{10... | collective-permute-start | bytes 786440 | tf_op jit(solution)/shard_map/ppermute | solution.py:459
  56.0 9.2 %collective-permute-start.16 = (bf16[256,512]{1,0:T(8,128)(2,1)S(1)}, bf16[256,512]{1,0:T(8,128)(2,1)S(1)}, u32[]{:S(2)}, u32[]{:S(2)}) collective-permute-start(bf16[256,512]{1,0:T(8,128)(2,1)S(1)} %get-tuple-element.89), channel_id=1, source_target_pairs={{0,8},{8,0},{16,24},{24,16},{1,9},{9,1},{17,25},{25,17},{2,10},{10... | collective-permute-start | bytes 786440 | tf_op jit(solution)/shard_map/ppermute | solution.py:459
  57.5 17.6 %collective-permute-start.11 = (bf16[256,1024]{1,0:T(8,128)(2,1)S(1)}, bf16[256,1024]{1,0:T(8,128)(2,1)S(1)}, u32[]{:S(2)}, u32[]{:S(2)}) collective-permute-start(bf16[256,1024]{1,0:T(8,128)(2,1)S(1)} %get-tuple-element.84), channel_id=1, source_target_pairs={{0,8},{8,0},{16,24},{24,16},{1,9},{9,1},{17,25},{25,17},{2,10},{10... | collective-permute-start | bytes 1572872 | tf_op jit(solution)/shard_map/ppermute | solution.py:459
  58.0 17.1 %collective-permute-start.12 = (bf16[256,1024]{1,0:T(8,128)(2,1)S(1)}, bf16[256,1024]{1,0:T(8,128)(2,1)S(1)}, u32[]{:S(2)}, u32[]{:S(2)}) collective-permute-start(bf16[256,1024]{1,0:T(8,128)(2,1)S(1)} %get-tuple-element.86), channel_id=1, source_target_pairs={{0,16},{8,24},{16,0},{24,8},{1,17},{9,25},{17,1},{25,9},{2,18},{10... | collective-permute-start | bytes 1572872 | tf_op jit(solution)/shard_map/ppermute | solution.py:459
  69.5 12.7 %collective-permute-start.18 = (bf16[256,512]{1,0:T(8,128)(2,1)S(1)}, bf16[256,512]{1,0:T(8,128)(2,1)S(1)}, u32[]{:S(2)}, u32[]{:S(2)}) collective-permute-start(bf16[256,512]{1,0:T(8,128)(2,1)S(1)} %get-tuple-element.93), channel_id=1, source_target_pairs={{0,16},{8,24},{16,0},{24,8},{1,17},{9,25},{17,1},{25,9},{2,18},{10... | collective-permute-start | bytes 786440 | tf_op jit(solution)/shard_map/ppermute | solution.py:459
  70.5 11.7 %collective-permute-start.17 = (bf16[256,512]{1,0:T(8,128)(2,1)S(1)}, bf16[256,512]{1,0:T(8,128)(2,1)S(1)}, u32[]{:S(2)}, u32[]{:S(2)}) collective-permute-start(bf16[256,512]{1,0:T(8,128)(2,1)S(1)} %get-tuple-element.91.refs_12_), channel_id=1, source_target_pairs={{0,8},{8,0},{16,24},{24,16},{1,9},{9,1},{17,25},{25,17},{2,10},{10... | collective-permute-start | bytes 786440 | tf_op jit(solution)/shard_map/ppermute | solution.py:459
  80.0 10.1 %collective-permute-start.21 = (bf16[256,512]{1,0:T(8,128)(2,1)S(1)}, bf16[256,512]{1,0:T(8,128)(2,1)S(1)}, u32[]{:S(2)}, u32[]{:S(2)}) collective-permute-start(bf16[256,512]{1,0:T(8,128)(2,1)S(1)} %get-tuple-element.103), channel_id=1, source_target_pairs={{0,8},{8,0},{16,24},{24,16},{1,9},{9,1},{17,25},{25,17},{2,10},{10... | collective-permute-start | bytes 786440 | tf_op jit(solution)/shard_map/ppermute | solution.py:459
  81.6 9.4 %collective-permute-start.22 = (bf16[256,512]{1,0:T(8,128)(2,1)S(1)}, bf16[256,512]{1,0:T(8,128)(2,1)S(1)}, u32[]{:S(2)}, u32[]{:S(2)}) collective-permute-start(bf16[256,512]{1,0:T(8,128)(2,1)S(1)} %get-tuple-element.105), channel_id=1, source_target_pairs={{0,16},{8,24},{16,0},{24,8},{1,17},{9,25},{17,1},{25,9},{2,18},{10... | collective-permute-start | bytes 786440 | tf_op jit(solution)/shard_map/ppermute | solution.py:459
  82.3 10.2 %collective-permute-start.25 = (bf16[256,256]{1,0:T(8,128)(2,1)S(1)}, bf16[256,256]{1,0:T(8,128)(2,1)S(1)}, u32[]{:S(2)}, u32[]{:S(2)}) collective-permute-start(bf16[256,256]{1,0:T(8,128)(2,1)S(1)} %get-tuple-element.113), channel_id=1, source_target_pairs={{0,16},{8,24},{16,0},{24,8},{1,17},{9,25},{17,1},{25,9},{2,18},{10... | collective-permute-start | bytes 393224 | tf_op jit(solution)/shard_map/ppermute | solution.py:459
  84.0 17.8 %collective-permute-start.19 = (bf16[256,512]{1,0:T(8,128)(2,1)S(1)}, bf16[256,512]{1,0:T(8,128)(2,1)S(1)}, u32[]{:S(2)}, u32[]{:S(2)}) collective-permute-start(bf16[256,512]{1,0:T(8,128)(2,1)S(1)} %get-tuple-element.100), channel_id=1, source_target_pairs={{0,16},{8,24},{16,0},{24,8},{1,17},{9,25},{17,1},{25,9},{2,18},{10... | collective-permute-start | bytes 786440 | tf_op jit(solution)/shard_map/ppermute | solution.py:459
  84.7 17.1 %collective-permute-start.20 = (bf16[256,512]{1,0:T(8,128)(2,1)S(1)}, bf16[256,512]{1,0:T(8,128)(2,1)S(1)}, u32[]{:S(2)}, u32[]{:S(2)}) collective-permute-start(bf16[256,512]{1,0:T(8,128)(2,1)S(1)} %get-tuple-element.101), channel_id=1, source_target_pairs={{0,8},{8,0},{16,24},{24,16},{1,9},{9,1},{17,25},{25,17},{2,10},{10... | collective-permute-start | bytes 786440 | tf_op jit(solution)/shard_map/ppermute | solution.py:459
  90.1 5.0 %collective-permute-start.26 = (bf16[256,256]{1,0:T(8,128)(2,1)S(1)}, bf16[256,256]{1,0:T(8,128)(2,1)S(1)}, u32[]{:S(2)}, u32[]{:S(2)}) collective-permute-start(bf16[256,256]{1,0:T(8,128)(2,1)S(1)} %get-tuple-element.114), channel_id=1, source_target_pairs={{0,8},{8,0},{16,24},{24,16},{1,9},{9,1},{17,25},{25,17},{2,10},{10... | collective-permute-start | bytes 393224 | tf_op jit(solution)/shard_map/ppermute | solution.py:459
  91.1 6.3 %collective-permute-start.23 = (bf16[256,256]{1,0:T(8,128)(2,1)S(1)}, bf16[256,256]{1,0:T(8,128)(2,1)S(1)}, u32[]{:S(2)}, u32[]{:S(2)}) collective-permute-start(bf16[256,256]{1,0:T(8,128)(2,1)S(1)} %get-tuple-element.111), channel_id=1, source_target_pairs={{0,16},{8,24},{16,0},{24,8},{1,17},{9,25},{17,1},{25,9},{2,18},{10... | collective-permute-start | bytes 393224 | tf_op jit(solution)/shard_map/ppermute | solution.py:459
  92.5 7.8 %collective-permute-start.24 = (bf16[256,256]{1,0:T(8,128)(2,1)S(1)}, bf16[256,256]{1,0:T(8,128)(2,1)S(1)}, u32[]{:S(2)}, u32[]{:S(2)}) collective-permute-start(bf16[256,256]{1,0:T(8,128)(2,1)S(1)} %get-tuple-element.112), channel_id=1, source_target_pairs={{0,8},{8,0},{16,24},{24,16},{1,9},{9,1},{17,25},{25,17},{2,10},{10... | collective-permute-start | bytes 393224 | tf_op jit(solution)/shard_map/ppermute | solution.py:459
  95.2 18.3 %collective-permute-start.31 = (bf16[256,256]{1,0:T(8,128)(2,1)S(1)}, bf16[256,256]{1,0:T(8,128)(2,1)S(1)}, u32[]{:S(2)}, u32[]{:S(2)}) collective-permute-start(bf16[256,256]{1,0:T(8,128)(2,1)S(1)} %get-tuple-element.121), channel_id=1, source_target_pairs={{0,6},{1,7},{2,4},{3,5},{4,2},{5,3},{6,0},{7,1},{8,14},{9,15},{10,... | collective-permute-start | bytes 393224 | tf_op jit(solution)/shard_map/ppermute | solution.py:459
  97.4 16.1 %collective-permute-start.30 = (bf16[256,256]{1,0:T(8,128)(2,1)S(1)}, bf16[256,256]{1,0:T(8,128)(2,1)S(1)}, u32[]{:S(2)}, u32[]{:S(2)}) collective-permute-start(bf16[256,256]{1,0:T(8,128)(2,1)S(1)} %get-tuple-element.115.refs_3_), channel_id=1, source_target_pairs={{0,4},{1,5},{2,6},{3,7},{4,0},{5,1},{6,2},{7,3},{8,12},{9,13},{10,... | collective-permute-start | bytes 393224 | tf_op jit(solution)/shard_map/ppermute | solution.py:459
  100.4 15.6 %collective-permute-start.29 = (bf16[256,256]{1,0:T(8,128)(2,1)S(1)}, bf16[256,256]{1,0:T(8,128)(2,1)S(1)}, u32[]{:S(2)}, u32[]{:S(2)}) collective-permute-start(bf16[256,256]{1,0:T(8,128)(2,1)S(1)} %get-tuple-element.119), channel_id=1, source_target_pairs={{0,6},{1,7},{2,4},{3,5},{4,2},{5,3},{6,0},{7,1},{8,14},{9,15},{10,... | collective-permute-start | bytes 393224 | tf_op jit(solution)/shard_map/ppermute | solution.py:459
  101.9 14.2 %collective-permute-start.28 = (bf16[256,256]{1,0:T(8,128)(2,1)S(1)}, bf16[256,256]{1,0:T(8,128)(2,1)S(1)}, u32[]{:S(2)}, u32[]{:S(2)}) collective-permute-start(bf16[256,256]{1,0:T(8,128)(2,1)S(1)} %get-tuple-element.116.refs_3_), channel_id=1, source_target_pairs={{0,4},{1,5},{2,6},{3,7},{4,0},{5,1},{6,2},{7,3},{8,12},{9,13},{10,... | collective-permute-start | bytes 393224 | tf_op jit(solution)/shard_map/ppermute | solution.py:459
  102.0 11.5 %collective-permute-start.27 = (bf16[256,512]{1,0:T(8,128)(2,1)S(1)}, bf16[256,512]{1,0:T(8,128)(2,1)S(1)}, u32[]{:S(2)}, u32[]{:S(2)}) collective-permute-start(bf16[256,512]{1,0:T(8,128)(2,1)S(1)} %get-tuple-element.118), channel_id=1, source_target_pairs={{0,2},{1,3},{2,0},{3,1},{4,6},{5,7},{6,4},{7,5},{8,10},{9,11},{10,... | collective-permute-start | bytes 786440 | tf_op jit(solution)/shard_map/ppermute | solution.py:459
  117.2 3.6 %collective-permute-start.36 = (f32[2,256]{1,0:T(2,128)S(1)}, f32[2,256]{1,0:T(2,128)S(1)}, u32[]{:S(2)}, u32[]{:S(2)}) collective-permute-start(f32[2,256]{1,0:T(2,128)S(1)} %slice.3), channel_id=1, source_target_pairs={{0,16},{8,24},{16,0},{24,8},{1,17},{9,25},{17,1},{25,9},{2,18},{10... | collective-permute-start | bytes 6152 | tf_op jit(solution)/shard_map/ppermute | solution.py:459
  117.8 4.5 %collective-permute-start.37 = (f32[2,256]{1,0:T(2,128)S(1)}, f32[2,256]{1,0:T(2,128)S(1)}, u32[]{:S(2)}, u32[]{:S(2)}) collective-permute-start(f32[2,256]{1,0:T(2,128)S(1)} %slice.3), channel_id=1, source_target_pairs={{0,24},{8,16},{16,8},{24,0},{1,25},{9,17},{17,9},{25,1},{2,26},{10... | collective-permute-start | bytes 6152 | tf_op jit(solution)/shard_map/ppermute | solution.py:459
  119.2 3.6 %collective-permute-start.35 = (f32[2,256]{1,0:T(2,128)S(1)}, f32[2,256]{1,0:T(2,128)S(1)}, u32[]{:S(2)}, u32[]{:S(2)}) collective-permute-start(f32[2,256]{1,0:T(2,128)S(1)} %slice.3), channel_id=1, source_target_pairs={{0,8},{8,0},{16,24},{24,16},{1,9},{9,1},{17,25},{25,17},{2,10},{10... | collective-permute-start | bytes 6152 | tf_op jit(solution)/shard_map/ppermute | solution.py:459
  120.7 2.7 %collective-permute-start.34 = (bf16[256,256]{1,0:T(8,128)(2,1)S(1)}, bf16[256,256]{1,0:T(8,128)(2,1)S(1)}, u32[]{:S(2)}, u32[]{:S(2)}) collective-permute-start(bf16[256,256]{1,0:T(8,128)(2,1)S(1)} %get-tuple-element.135), channel_id=1, source_target_pairs={{0,1},{1,0},{2,3},{3,2},{4,5},{5,4},{6,7},{7,6},{8,9},{9,8},{10,11... | collective-permute-start | bytes 393224 | tf_op jit(solution)/shard_map/ppermute | solution.py:459
  (11 other events, 34.0 us)
